TPU v7x, 256 devices: a whole 4x4x8 slice. The times are simulated.
256 devices in a mesh: section: 4 (over y), vocab: 32 (over x, z), dp: 2 (over core).
Axes of the slice: x: 4, y: 4, z: 8, core: 2. Of those that a mesh axis runs over, the one named last changes fastest.
Arguments:
- student_hidden: bfloat16 [2, 256, 3584], P('dp', ('section', 'vocab')), may hold values from -6 to 6
- teacher_hidden: bfloat16 [2, 256, 4608], P('dp', 'section'), may hold values from -6 to 6
- student_gain: float32 [3584], replicated, may hold values from 0.5 to 1.5
- teacher_gain: float32 [4608], replicated, may hold values from 0.5 to 1.5
- student_head: bfloat16 [3584, 131072], P('dp', ('section', 'vocab')), may hold values from -0.3125 to 0.3125
- teacher_head: bfloat16 [4608, 131072], P('dp', ('section', 'vocab')), may hold values from -0.25 to 0.25
- targets: int32 [2, 256], P('dp'), may hold values from 0 to 131071
Outputs:
- row_loss: float32 [2, 256], P('dp', ('section', 'vocab'))
- head_grad: bfloat16 [3584, 131072], P('dp', ('section', 'vocab'))
All inputs are finite; a program needn't handle non-finite values.
Results may differ from a plain program's by a relative error of at most 0.025.
Values may be sent and summed in bfloat16 or wider, within the bound.
No kernel may reach another device: no remote copies, remote signals or barrier semaphores. Data moves between devices by JAX's collectives and lax.ppermute only.
A program may use at most 128 MiB of HBM per device.

v0:
```python
import jax
import jax.numpy as jnp
from jax import lax
from jax.sharding import PartitionSpec as P


def rms_norm(hidden, scales):
    values = hidden.astype(jnp.float32)
    spread = jnp.mean(values * values, axis=-1, keepdims=True)
    return (values * lax.rsqrt(spread + 1e-06) * scales).astype(jnp.bfloat16)


def soft_cap(logits):
    return (30.0 * jnp.tanh(logits / 30.0)).astype(jnp.bfloat16)


def add_columns(hidden, portion):
    return jnp.dot(hidden, portion, preferred_element_type=jnp.float32)


def row_terms(capped_teacher, capped_student, targets_here):
    teach_vals = capped_teacher.astype(jnp.float32)
    stud_vals = capped_student.astype(jnp.float32)
    target_hit = (
        lax.broadcasted_iota(jnp.int32, stud_vals.shape, 1) == targets_here[:, None]
    ).astype(jnp.float32)
    teach_exp = jnp.exp(teach_vals)
    stud_exp = jnp.exp(stud_vals)
    sums = (
        jnp.sum(teach_exp, axis=1),
        jnp.sum(stud_exp, axis=1),
        jnp.sum(teach_exp * (teach_vals - stud_vals), axis=1),
        jnp.sum(target_hit * stud_vals, axis=1),
    )
    return (stud_vals, teach_exp, stud_exp, target_hit, sums)


def finish_loss(sums):
    teach_total, stud_total, cross_sum, target_logit = sums
    return cross_sum / teach_total - jnp.log(teach_total) + 2.0 * jnp.log(stud_total) - target_logit


def logit_gradient(stud_vals, teach_exp, stud_exp, target_hit, sums):
    teach_total, stud_total, cross_sum, target_logit = sums
    scaled = 2.0 * stud_exp / stud_total[:, None] - teach_exp / teach_total[:, None] - target_hit
    return (scaled * (1.0 - stud_vals * stud_vals / 900.0)).astype(jnp.bfloat16)


def contract_rows(left, right):
    return lax.dot_general(
        left, right, (((0,), (0,)), ((), ())), preferred_element_type=jnp.float32
    )


def shards(
    student_hidden, teacher_hidden, student_gain, teacher_gain, student_head, teacher_head, targets
):
    normed_student = lax.all_gather(
        rms_norm(student_hidden[0], student_gain), ("section", "vocab"), axis=0, tiled=True
    )
    normed_teacher = lax.all_gather(
        rms_norm(teacher_hidden[0], teacher_gain), "section", axis=0, tiled=True
    )
    all_rows = normed_student.shape[0]
    student_logits = add_columns(
        normed_student, lax.all_gather(student_head, "dp", axis=0, tiled=True)
    )
    teacher_logits = add_columns(
        normed_teacher, lax.all_gather(teacher_head, "dp", axis=0, tiled=True)
    )
    capped_student = soft_cap(student_logits)
    capped_teacher = soft_cap(teacher_logits)
    group_index = lax.axis_index(("section", "vocab"))
    here_rows = all_rows // lax.axis_size(("section", "vocab"))
    teach_rows, stud_rows = (
        lax.all_to_all(
            capped_teacher, ("section", "vocab"), split_axis=0, concat_axis=1, tiled=True
        ),
        lax.all_to_all(
            capped_student, ("section", "vocab"), split_axis=0, concat_axis=1, tiled=True
        ),
    )
    targets_here = lax.dynamic_slice_in_dim(targets[0], group_index * here_rows, here_rows)
    stud_vals, teach_exp, stud_exp, target_hit, sums = row_terms(
        teach_rows, stud_rows, targets_here
    )
    row_loss = finish_loss(sums)[None, :]
    grad_here = logit_gradient(stud_vals, teach_exp, stud_exp, target_hit, sums)
    row_grad = lax.all_to_all(
        grad_here, ("section", "vocab"), split_axis=1, concat_axis=0, tiled=True
    )
    head_grad = lax.psum_scatter(
        contract_rows(normed_student, row_grad), "dp", scatter_dimension=0, tiled=True
    ).astype(jnp.bfloat16)
    return (row_loss, head_grad)


def solution(mesh):
    placed = (
        P("dp", ("section", "vocab"), None),
        P("dp", "section", None),
        P(),
        P(),
        P("dp", ("section", "vocab")),
        P("dp", ("section", "vocab")),
        P("dp", None),
    )
    return jax.shard_map(
        shards,
        mesh=mesh,
        in_specs=placed,
        out_specs=(P("dp", ("section", "vocab")), P("dp", ("section", "vocab"))),
        check_vma=False,
    )
```

profile of v0, /device:TPU:1, one launch (start us, length us, event | category | flops | bytes accessed | tf_op | source)
XLA Modules:
  0.0 342.2 jit_solution(13983659001921396012)
XLA Ops:
  7.2 0.0 copy-start
  7.2 0.0 copy-start.1
  7.2 0.0 copy-start.2
  7.2 0.0 all-gather.12.cloned.1.call-start
  7.2 0.9 fusion.20
  8.2 1.4 fusion.23
  9.6 0.0 all-gather.12.cloned.1.call-update
  9.6 0.0 all-gather.10.cloned.1.call-start
  9.6 0.7 all-gather.10.cloned.1.call-update
  10.4 0.0 all-gather.6.cloned.1.call-start
  10.4 0.0 copy-done.1
  10.4 0.2 fusion.6
  10.6 0.0 copy-done.2
  10.7 1.0 fusion.8
  11.7 0.0 all-gather.6.cloned.1.call-update
  11.7 0.0 all-gather.8.cloned.1.call-start
  11.7 0.5 all-gather.8.cloned.1.call-update
  12.3 112.3 %all-gather.12.cloned.1.call-done = bf16[128,2,3584]{2,1,0:T(2,128)(2,1)} async-done(((bf16[1,2,3584]{2,1,0:T(2,128)(2,1)}), bf16[128,2,3584]{2,1,0:T(2,128)(2,1)}) %all-gather.12.cloned.1.call-update) | async-done | bytes 1835024 | tf_op jit(solution)/shard_map/all_gather | solution.py:58
  124.6 4.1 %reshape.120 = bf16[256,3584]{1,0:T(8,128)(2,1)S(1)} reshape(bf16[128,2,3584]{2,1,0:T(2,128)(2,1)} %all-gather.12.cloned.1.call-done) | data formatting | bytes 3670016
  128.6 24.1 %all-gather.10.cloned.1.call-done = bf16[3584,1024]{1,0:T(8,128)(2,1)} async-done(((bf16[1792,1024]{1,0:T(8,128)(2,1)}), bf16[3584,1024]{1,0:T(8,128)(2,1)}) %all-gather.10.cloned.1.call-update) | async-done | bytes 7340048 | tf_op jit(solution)/shard_map/all_gather | solution.py:66
  152.7 5.3 %fusion.4 = bf16[256,1024]{1,0:T(8,128)(2,1)S(1)} fusion(bf16[256,3584]{1,0:T(8,128)(2,1)S(1)} %reshape.120, bf16[3584,1024]{1,0:T(8,128)(2,1)} %all-gather.10.cloned.1.call-done), kind=kOutput, calls=%fused_computation.10 | convolution fusion | flops 1879834624 | bytes 9699328 | tf_op jit(solution)/shard_map/dot_general | solution.py:18
  158.0 1.0 all_to_all.34
  159.0 13.6 %all-to-all-start.1 = ((bf16[128,2,1024]{2,1,0:T(2,128)(2,1)}), bf16[128,2,1024]{2,1,0:T(2,128)(2,1)S(1)}, u32[]{:S(2)}, u32[]{:S(2)}) async-start(bf16[128,2,1024]{2,1,0:T(2,128)(2,1)} %all_to_all.34), calls=%async_computation.1 | async-start | bytes 1048576 | tf_op jit(solution)/shard_map/all_to_all | solution.py:79
  172.6 24.3 %all-gather.6.cloned.1.call-done = bf16[256,4608]{1,0:T(8,128)(2,1)} async-done(((bf16[64,4608]{1,0:T(8,128)(2,1)}), bf16[256,4608]{1,0:T(8,128)(2,1)}) %all-gather.6.cloned.1.call-update) | async-done | bytes 2359312 | tf_op jit(solution)/shard_map/all_gather | solution.py:61
  196.9 29.7 %all-gather.8.cloned.1.call-done = bf16[4608,1024]{1,0:T(8,128)(2,1)} async-done(((bf16[2304,1024]{1,0:T(8,128)(2,1)}), bf16[4608,1024]{1,0:T(8,128)(2,1)}) %all-gather.8.cloned.1.call-update) | async-done | bytes 9437200 | tf_op jit(solution)/shard_map/all_gather | solution.py:69
  226.6 7.0 %fusion.5 = bf16[256,1024]{1,0:T(8,128)(2,1)S(1)} fusion(bf16[256,4608]{1,0:T(8,128)(2,1)} %all-gather.6.cloned.1.call-done, bf16[4608,1024]{1,0:T(8,128)(2,1)} %all-gather.8.cloned.1.call-done), kind=kOutput, calls=%fused_computation.11 | convolution fusion | flops 2416705536 | bytes 12320768 | tf_op jit(solution)/shard_map/dot_general | solution.py:18
  233.6 1.0 all_to_all.32
  234.6 0.0 all-to-all-done.1
  234.6 13.6 %all-to-all-start = ((bf16[128,2,1024]{2,1,0:T(2,128)(2,1)}), bf16[128,2,1024]{2,1,0:T(2,128)(2,1)S(1)}, u32[]{:S(2)}, u32[]{:S(2)}) async-start(bf16[128,2,1024]{2,1,0:T(2,128)(2,1)} %all_to_all.32), calls=%async_computation | async-start | bytes 1048576 | tf_op jit(solution)/shard_map/all_to_all | solution.py:76
  248.2 0.2 reduce-scatter.2.cloned.1.call-start
  248.4 0.0 copy-done
  248.4 0.1 dynamic-slice_bitcast_fusion
  248.5 0.1 multiply_add_fusion
  248.6 19.1 %all-to-all-done = bf16[128,2,1024]{2,1,0:T(2,128)(2,1)S(1)} async-done(((bf16[128,2,1024]{2,1,0:T(2,128)(2,1)}), bf16[128,2,1024]{2,1,0:T(2,128)(2,1)S(1)}, u32[]{:S(2)}, u32[]{:S(2)}) %all-to-all-start) | async-done | bytes 524320 | tf_op jit(solution)/shard_map/all_to_all | solution.py:76
  267.7 2.6 fusion.15
  270.3 2.5 fusion.19
  272.8 24.8 %all_to_all.42 = bf16[2,128,1024]{2,0,1:T(2,128)(2,1)S(1)} all-to-all(bf16[2,128,1024]{2,0,1:T(2,128)(2,1)S(1)} %fusion.19), channel_id=1, replica_groups=mesh['section'=4,'vocab'=32,'dp'=2] {'section','vocab'}, dimensions={1} | all-to-all | bytes 1048576 | tf_op jit(solution)/shard_map/all_to_all | solution.py:89
  297.6 0.2 all_to_all.38
  297.8 7.3 %fusion.24 = f32[3584,1024]{1,0:T(8,128)} fusion(bf16[256,3584]{1,0:T(8,128)(2,1)S(1)} %reshape.120, bf16[256,1024]{1,0:T(8,128)(2,1)S(1)} %all_to_all.38), kind=kOutput, calls=%fused_computation.42 | convolution fusion | flops 1879048192 | bytes 17039360 | tf_op jit(solution)/shard_map/dot_general | solution.py:50
  305.1 0.0 reduce-scatter.2.cloned.1.call-update
  305.1 0.5 subtract_bitcast_fusion
  305.6 24.6 %reduce-scatter.2.cloned.1.call-done = f32[1792,1024]{1,0:T(8,128)} async-done(((f32[3584,1024]{1,0:T(8,128)}), f32[1792,1024]{1,0:T(8,128)}) %reduce-scatter.2.cloned.1.call-update) | async-done | bytes 7340048 | tf_op jit(solution)/shard_map/reduce_scatter | solution.py:92
  330.2 5.5 %convert_element_type.68 = bf16[1792,1024]{1,0:T(8,128)(2,1)} convert(f32[1792,1024]{1,0:T(8,128)} %reduce-scatter.2.cloned.1.call-done) | non-fusion elementwise | flops 1835008 | bytes 11010048 | tf_op jit(solution)/shard_map/convert_element_type | solution.py:94
  (2 shorter events, 0.0 us)
Async XLA Ops:
  7.2 241.2 %copy-start = (s32[1,256]{1,0:T(1,128)S(1)}, s32[1,256]{1,0:T(1,128)}, u32[]{:S(2)}) copy-start(s32[1,256]{1,0:T(1,128)} %param.13) | copy-start | bytes 3076
  7.2 3.2 copy-start.1
  7.2 3.5 %copy-start.2 = (f32[4608]{0:T(1024)S(1)}, f32[4608]{0:T(1024)}, u32[]{:S(2)}) copy-start(f32[4608]{0:T(1024)} %param.10) | copy-start | bytes 55300
  7.2 117.4 %all-gather.12.cloned.1.call-start = ((), (), s32[]{:S(2)}) async-start(), calls=%async_computation.8 | async-start | bytes 1849344 | tf_op jit(solution)/shard_map/all_gather | solution.py:58
  9.6 143.1 %all-gather.10.cloned.1.call-start = ((), (), s32[]{:S(2)}) async-start(), calls=%async_computation.6 | async-start | bytes 11010048 | tf_op jit(solution)/shard_map/all_gather | solution.py:66
  10.4 186.5 %all-gather.6.cloned.1.call-start = ((), (), s32[]{:S(2)}) async-start(), calls=%async_computation.4 | async-start | bytes 2949120 | tf_op jit(solution)/shard_map/all_gather | solution.py:61
  11.7 214.9 %all-gather.8.cloned.1.call-start = ((), (), s32[]{:S(2)}) async-start(), calls=%async_computation.5 | async-start | bytes 14155776 | tf_op jit(solution)/shard_map/all_gather | solution.py:69
  159.0 75.6 %all-to-all-start.1 = ((bf16[128,2,1024]{2,1,0:T(2,128)(2,1)}), bf16[128,2,1024]{2,1,0:T(2,128)(2,1)S(1)}, u32[]{:S(2)}, u32[]{:S(2)}) async-start(bf16[128,2,1024]{2,1,0:T(2,128)(2,1)} %all_to_all.34), calls=%async_computation.1 | async-start | bytes 1048576 | tf_op jit(solution)/shard_map/all_to_all | solution.py:79
  234.6 33.1 %all-to-all-start = ((bf16[128,2,1024]{2,1,0:T(2,128)(2,1)}), bf16[128,2,1024]{2,1,0:T(2,128)(2,1)S(1)}, u32[]{:S(2)}, u32[]{:S(2)}) async-start(bf16[128,2,1024]{2,1,0:T(2,128)(2,1)} %all_to_all.32), calls=%async_computation | async-start | bytes 1048576 | tf_op jit(solution)/shard_map/all_to_all | solution.py:76
  248.2 82.0 %reduce-scatter.2.cloned.1.call-start = ((), (), s32[]{:S(2)}) async-start(), calls=%async_computation.7 | async-start | bytes 22020096 | tf_op jit(solution)/shard_map/reduce_scatter | solution.py:92
Sparse Core Ops, SparseCore 0:
  11.7 112.8 all-gather.11
  126.4 26.2 all-gather.9
  155.1 41.7 all-gather.5
  198.6 27.9 all-gather.7
  305.2 24.9 reduce-scatter.1
where the time goes:
time: 343 us; the launch traced here: 342 us
  waiting for transfers between devices  235 us (69%)
  starting transfers between devices  27.5 us (8%)
  blocking collectives  24.8 us (7%)
  matrix products  19.6 us (6%)
  other arithmetic  14.8 us (4%)
  between operations  13.9 us (4%)
  local copies, waits for them, and re-layouts  6.33 us (2%)
    all_gather x1, waiting for transfers between devices, shards(): lax.all_gather(rms_norm(student_hidden[0], student_gain), ('section', 'vo...  112 us
    all_gather x1, waiting for transfers between devices, shards(): lax.all_gather(teacher_head, 'dp', axis=0, tiled=True)  29.7 us
    all_to_all x1, blocking collectives, shards(): lax.all_to_all(grad_here, ('section', 'vocab'), split_axis=1, concat_axis...  24.8 us
    reduce_scatter x1, waiting for transfers between devices, shards(): lax.psum_scatter(contract_rows(normed_student, row_grad), 'dp', scatter_d...  24.6 us
    all_gather x1, waiting for transfers between devices, shards(): lax.all_gather(rms_norm(teacher_hidden[0], teacher_gain), 'section', axis...  24.3 us
    all_gather x1, waiting for transfers between devices, shards(): lax.all_gather(student_head, 'dp', axis=0, tiled=True)  24.1 us
    all_to_all x1, waiting for transfers between devices, shards(): lax.all_to_all(capped_teacher, ('section', 'vocab'), split_axis=0, concat...  19.1 us
    all_to_all x1, starting transfers between devices, shards(): lax.all_to_all(capped_teacher, ('section', 'vocab'), split_axis=0, concat...  13.6 us
  transfers between devices with their start and end apart: 7, of which 6 were waited for; matrix products, arithmetic and copies ran while one was open for 5% of the time, Pallas kernels for 0%

commit v1 on v0

v1 whole, which is shorter than its diff:
```python
import jax
import jax.numpy as jnp
from jax import lax
from jax.sharding import Mesh, PartitionSpec as P

F32 = jnp.float32
BF16 = jnp.bfloat16


def rms_norm(hidden, scales):
    values = hidden.astype(F32)
    spread = jnp.mean(values * values, axis=-1, keepdims=True)
    return (values * lax.rsqrt(spread + 1e-06) * scales).astype(BF16)


def soft_cap(logits):
    return (30.0 * jnp.tanh(logits / 30.0)).astype(BF16)


def up(n, k):
    return [(i, (i + k) % n) for i in range(n)]


def swap_cores(value):
    return lax.ppermute(value, "c", [(0, 1), (1, 0)])


def mine_and_other(first, second, core):
    return jnp.where(core == 0, first, second), jnp.where(core == 0, second, first)


def ring(block, axis, n):
    blocks = [block]
    from_low = from_high = block
    for _ in range(n // 2 - 1):
        from_low = lax.ppermute(from_low, axis, up(n, 1))
        from_high = lax.ppermute(from_high, axis, up(n, -1))
        blocks += [from_low, from_high]
    half = block.shape[0] // 2
    blocks.append(
        jnp.concatenate(
            [
                lax.ppermute(from_low[:half], axis, up(n, 1)),
                lax.ppermute(from_high[half:], axis, up(n, -1)),
            ]
        )
    )
    return blocks


def ring_order(n):
    order = [0]
    for step in range(1, n // 2):
        order += [n - step, step]
    return order + [n // 2]


def by_distance(entries, n):
    order = ring_order(n)
    return [entries[order.index(d)] for d in range(n)]


def turn(array, amount):
    n = array.shape[0]
    return lax.dynamic_slice_in_dim(jnp.concatenate([array, array]), amount % n, n)


def dot(left, right):
    return jnp.dot(left, right, preferred_element_type=F32)


def shards(
    student_hidden, teacher_hidden, student_gain, teacher_gain, student_head, teacher_head, targets
):
    nx, ny, nz = lax.axis_size("x"), lax.axis_size("y"), lax.axis_size("z")
    x, y, z, core = (lax.axis_index(a) for a in ("x", "y", "z", "c"))
    rows = student_hidden.shape[1]
    k_s, vocab = student_head.shape
    k_t = teacher_head.shape[0]
    per_plane = ny * nx * rows

    normed = rms_norm(student_hidden[0], student_gain)
    halves = normed.reshape(rows, 2, k_s).transpose(1, 0, 2)
    sent = jnp.broadcast_to(halves[None], (ny * nx, 2, rows, k_s)).reshape(ny * nx * 2, rows, k_s)
    got = lax.all_to_all(sent, ("y", "x", "c"), 0, 0, tiled=True).reshape(ny * nx, 2, rows, k_s)
    own, other = mine_and_other(got[:, 0], got[:, 1], core)
    plane = jnp.concatenate([own.reshape(per_plane, k_s), other.reshape(per_plane, k_s)])
    planes = by_distance(ring(plane, "z", nz), nz)

    t_norm = rms_norm(teacher_hidden[0], teacher_gain)
    section = t_norm.shape[0]
    t_norm = t_norm.reshape(nx, nz, rows, 2 * k_t).transpose(1, 0, 2, 3)
    t_norm = turn(t_norm, z).reshape(section, 2, k_t)
    t_keep, t_send = mine_and_other(t_norm[:, 0], t_norm[:, 1], core)
    t_block = jnp.concatenate([t_keep, swap_cores(t_send)])
    t_blocks = by_distance(ring(t_block, "y", ny), ny)

    t_all = jnp.stack(t_blocks).reshape(ny, 2, section, k_t)
    t_part = dot(t_all.transpose(1, 0, 2, 3).reshape(2 * ny * section, k_t), teacher_head)
    half_rows = ny * section
    t_logits = t_part[:half_rows] + swap_cores(t_part[half_rows:])
    capped_teacher = soft_cap(t_logits).reshape(ny, nz, nx * rows, vocab)
    capped_teacher = turn(capped_teacher, -y).transpose(1, 0, 2, 3).reshape(half_rows, vocab)

    s_rows = jnp.stack(planes).reshape(nz, 2, per_plane, k_s).transpose(1, 0, 2, 3)
    s_rows = s_rows.reshape(2 * half_rows, k_s)
    s_part = dot(s_rows, student_head)
    s_logits = s_part[:half_rows] + swap_cores(s_part[half_rows:])
    capped_student = soft_cap(s_logits)

    stud_vals = capped_student.astype(F32)
    teach_vals = capped_teacher.astype(F32)
    ordered = targets[0].reshape(ny, nx, nz, rows).transpose(2, 0, 1, 3)
    first = ((y * nx + x) * nz + z) * vocab
    local_targets = turn(ordered, z).reshape(half_rows) - first
    hit = (lax.broadcasted_iota(jnp.int32, stud_vals.shape, 1) == local_targets[:, None]).astype(F32)
    teach_exp = jnp.exp(teach_vals)
    stud_exp = jnp.exp(stud_vals)
    sums = jnp.stack(
        [
            jnp.sum(teach_exp, axis=1),
            jnp.sum(stud_exp, axis=1),
            jnp.sum(teach_exp * (teach_vals - stud_vals), axis=1),
            jnp.sum(hit * stud_vals, axis=1),
        ]
    ).reshape(4, nz, per_plane)
    sums = sums.transpose(1, 0, 2).reshape(nz, 4 * per_plane)
    spread = jnp.broadcast_to(sums[None], (ny * nx,) + sums.shape)
    sums = jnp.sum(lax.all_to_all(spread, ("y", "x"), 0, 0, tiled=True), axis=0)
    sums = turn(sums, -z)
    spread = jnp.broadcast_to(sums[None], (nz,) + sums.shape)
    sums = jnp.sum(lax.all_to_all(spread, "z", 0, 0, tiled=True), axis=0)
    sums = turn(sums, z).reshape(nz, 4, per_plane)
    teach_total, stud_total, cross_sum, target_logit = (
        sums[:, q].reshape(half_rows) for q in range(4)
    )
    here = sums[0].reshape(4, ny * nx, rows)
    tt, st, cs, tl = (lax.dynamic_index_in_dim(here[q], y * nx + x, 0, False) for q in range(4))
    row_loss = (cs / tt - jnp.log(tt) + 2.0 * jnp.log(st) - tl)[None, :]

    scaled = 2.0 * stud_exp / stud_total[:, None] - teach_exp / teach_total[:, None] - hit
    row_grad = (scaled * (1.0 - stud_vals * stud_vals / 900.0)).astype(BF16)
    both = jnp.concatenate([row_grad, swap_cores(row_grad)])
    head_grad = lax.dot_general(
        s_rows, both, (((0,), (0,)), ((), ())), preferred_element_type=F32
    ).astype(BF16)
    return (row_loss, head_grad)


def solution(mesh):
    sizes = mesh.shape
    cube = mesh.devices.reshape(sizes["section"], 4, sizes["vocab"] // 4, sizes["dp"])
    grid = Mesh(cube, ("y", "x", "z", "c"))
    group = ("y", "x", "z")
    placed = (
        P("c", group, None),
        P("c", "y", None),
        P(),
        P(),
        P("c", group),
        P("c", group),
        P("c", None),
    )
    return jax.shard_map(
        shards,
        mesh=grid,
        in_specs=placed,
        out_specs=(P("c", group), P("c", group)),
        check_vma=False,
    )
```

time: 343 us -> 110 us (0.32)
  waiting for transfers between devices: 235 us -> 21.3 us
  between operations: 13.9 us -> 1.13 us
  blocking collectives: 24.8 us -> 12.1 us
  starting transfers between devices: 27.5 us -> 39.2 us
  matrix products: 19.6 us -> 12.3 us
  local copies, waits for them, and re-layouts: 6.33 us -> 12.1 us
    all_gather x4 -> x0, waiting for transfers between devices: 190 us -> none  [the longest x1 112 us: shards(): lax.all_gather(rms_norm(student_hidden[0], student_gain), ('section', 'vo...]
    ppermute x0 -> x16, starting transfers between devices: none -> 26.8 us  [the longest x4 11.7 us: ring(): from_high = lax.ppermute(from_high, axis, up(n, -1))]
    reduce_scatter x1 -> x0, waiting for transfers between devices: 24.6 us -> none  [shards(): lax.psum_scatter(contract_rows(normed_student, row_grad), 'dp', scatter_d...]
    all_to_all x2, starting transfers between devices: 27.1 us -> 12.4 us  [the longest x1 8.59 us: shards(): lax.all_to_all(sent, ('y', 'x', 'c'), 0, 0, tiled=True)]
    all_to_all x1, blocking collectives: 24.8 us -> 12.1 us  [shards(): sums = jnp.sum(lax.all_to_all(spread, 'z', 0, 0, tiled=True), axis=0)]
    ppermute x0 -> x16, waiting for transfers between devices: none -> 11.8 us  [the longest x4 8.89 us: ring(): from_low = lax.ppermute(from_low, axis, up(n, 1))]
    all_to_all x2, waiting for transfers between devices: 19.1 us -> 9.45 us  [the longest x1 6.49 us: shards(): sums = jnp.sum(lax.all_to_all(spread, ('y', 'x'), 0, 0, tiled=True), axis=0)]
    dot_general x3, matrix products: 19.6 us -> 12.3 us  [the longest x2 6.81 us: dot(): return jnp.dot(left, right, preferred_element_type=F32)]
  transfers between devices with their start and end apart: 7 -> 18, of which waited for: 6 -> 7; matrix products, arithmetic and copies ran while one was open for 5% -> 13% of each run, Pallas kernels for 0% -> 0%
where the time goes in v1:
time: 110 us; the launch traced here: 109 us
  starting transfers between devices  39.2 us (36%)
  waiting for transfers between devices  21.3 us (19%)
  matrix products  12.3 us (11%)
  local copies, waits for them, and re-layouts  12.1 us (11%)
  blocking collectives  12.1 us (11%)
  other arithmetic  11.4 us (10%)
  between operations  1.13 us (1%)
    all_to_all x1, blocking collectives, shards(): sums = jnp.sum(lax.all_to_all(spread, 'z', 0, 0, tiled=True), axis=0)  12.1 us
    ppermute x4, starting transfers between devices, ring(): from_high = lax.ppermute(from_high, axis, up(n, -1))  11.7 us
    ppermute x4, waiting for transfers between devices, ring(): from_low = lax.ppermute(from_low, axis, up(n, 1))  8.89 us
    all_to_all x1, starting transfers between devices, shards(): lax.all_to_all(sent, ('y', 'x', 'c'), 0, 0, tiled=True)  8.59 us
    ppermute x4, starting transfers between devices, swap_cores(): return lax.ppermute(value, 'c', [(0, 1), (1, 0)])  7.12 us
    dot_general x2, matrix products, dot(): return jnp.dot(left, right, preferred_element_type=F32)  6.81 us
    all_to_all x1, waiting for transfers between devices, shards(): sums = jnp.sum(lax.all_to_all(spread, ('y', 'x'), 0, 0, tiled=True), axis=0)  6.49 us
    dot_general x1, matrix products, shards(): lax.dot_general(s_rows, both, (((0,), (0,)), ((), ())), preferred_element...  5.45 us
  transfers between devices with their start and end apart: 18, of which 7 were waited for; matrix products, arithmetic and copies ran while one was open for 13% of the time, Pallas kernels for 0%

profile of v1, /device:TPU:1, one launch (start us, length us, event | category | flops | bytes accessed | tf_op | source)
XLA Modules:
  0.0 109.4 jit_solution(16315945733019344161)
XLA Ops:
  0.7 0.9 multiply_reduce_fusion.1
  1.6 0.7 reshape.166
  2.3 0.7 mul.96
  3.0 0.1 fusion.31
  3.2 0.8 broadcast_in_dim.8
  4.0 8.6 %all-to-all-start = ((bf16[32,2,1792]{2,1,0:T(2,128)(2,1)}), bf16[32,2,1792]{2,1,0:T(2,128)(2,1)S(1)}, u32[]{:S(2)}, u32[]{:S(2)}) async-start(bf16[32,2,1792]{2,1,0:T(2,128)(2,1)} %bitcast.14), calls=%async_computation | async-start | bytes 458752 | tf_op jit(solution)/shard_map/all_to_all | solution.py:85
  12.6 1.3 %multiply_reduce_fusion = f32[64]{0:T(128)S(1)} fusion(bf16[1,64,4608]{2,1,0:T(8,128)(2,1)} %param.8), kind=kLoop, calls=%fused_computation.15 | loop fusion | flops 884672 | bytes 590080 | tf_op jit(solution)/shard_map/reduce_sum | solution.py:12
  13.9 0.7 reshape.165
  14.6 0.1 rsqrt.20
  14.7 0.1 copy.73
  14.8 0.3 fusion.27
  15.1 0.4 fusion.28
  15.6 0.5 copy.75
  16.0 0.4 reshape.158
  16.4 1.4 %broadcast_select_fusion.1 = (bf16[64,1,2304]{2,1,0:T(2,128)(2,1)S(1)}, bf16[64,1,2304]{2,1,0:T(2,128)(2,1)S(1)}) fusion(pred[]{:T(512)S(6)} %eq.20, bf16[64,2,2304]{2,1,0:T(2,128)(2,1)S(1)} %reshape.158), kind=kLoop, calls=%fused_computation.17 | loop fusion | flops 294912 | bytes 1179649 | tf_op jit(solution)/shard_map/jit(_where)/select_n | solution.py:29
  17.8 0.3 collective-permute-start
  18.2 3.0 %all-to-all-done = bf16[32,2,1792]{2,1,0:T(2,128)(2,1)S(1)} async-done(((bf16[32,2,1792]{2,1,0:T(2,128)(2,1)}), bf16[32,2,1792]{2,1,0:T(2,128)(2,1)S(1)}, u32[]{:S(2)}, u32[]{:S(2)}) %all-to-all-start) | async-done | bytes 229408 | tf_op jit(solution)/shard_map/all_to_all | solution.py:85
  21.1 0.2 broadcast_select_fusion.2
  21.5 1.7 %collective-permute-start.9 = (bf16[64,1792]{1,0:T(8,128)(2,1)S(1)}, bf16[64,1792]{1,0:T(8,128)(2,1)S(1)}, u32[]{:S(2)}, u32[]{:S(2)}) collective-permute-start(bf16[64,1792]{1,0:T(8,128)(2,1)S(1)} %constant_dynamic-update-slice_fusion), channel_id=1, source_target_pairs={{0,2},{2,4},{4,6},{6,8},{8,10},{10,12},{12,14},{14,0},{1,3},{3,5},... | collective-permute-start | bytes 688136 | tf_op jit(solution)/shard_map/ppermute | solution.py:36
  23.2 4.0 %collective-permute-start.6 = (bf16[64,1792]{1,0:T(8,128)(2,1)S(1)}, bf16[64,1792]{1,0:T(8,128)(2,1)S(1)}, u32[]{:S(2)}, u32[]{:S(2)}) collective-permute-start(bf16[64,1792]{1,0:T(8,128)(2,1)S(1)} %constant_dynamic-update-slice_fusion), channel_id=1, source_target_pairs={{0,14},{2,0},{4,2},{6,4},{8,6},{10,8},{12,10},{14,12},{1,15},{3,1}... | collective-permute-start | bytes 688136 | tf_op jit(solution)/shard_map/ppermute | solution.py:37
  27.3 0.4 collective-permute-start.2
  27.7 2.3 %collective-permute-start.1 = (bf16[128,2304]{1,0:T(8,128)(2,1)S(1)}, bf16[128,2304]{1,0:T(8,128)(2,1)S(1)}, u32[]{:S(2)}, u32[]{:S(2)}) collective-permute-start(bf16[128,2304]{1,0:T(8,128)(2,1)S(1)} %pad_maximum_fusion.1), channel_id=1, source_target_pairs={{0,192},{64,0},{128,64},{192,128},{1,193},{65,1},{129,65},{193,129... | collective-permute-start | bytes 1769480 | tf_op jit(solution)/shard_map/ppermute | solution.py:37
  30.0 3.0 %collective-permute-done.9 = bf16[64,1792]{1,0:T(8,128)(2,1)S(1)} collective-permute-done((bf16[64,1792]{1,0:T(8,128)(2,1)S(1)}, bf16[64,1792]{1,0:T(8,128)(2,1)S(1)}, u32[]{:S(2)}, u32[]{:S(2)}) %collective-permute-start.9) | collective-permute-done | bytes 229408 | tf_op jit(solution)/shard_map/ppermute | solution.py:36
  33.0 2.7 %collective-permute-start.7 = (bf16[64,1792]{1,0:T(8,128)(2,1)S(1)}, bf16[64,1792]{1,0:T(8,128)(2,1)S(1)}, u32[]{:S(2)}, u32[]{:S(2)}) collective-permute-start(bf16[64,1792]{1,0:T(8,128)(2,1)S(1)} %collective-permute-done.6), channel_id=1, source_target_pairs={{0,14},{2,0},{4,2},{6,4},{8,6},{10,8},{12,10},{14,12},{1,15},{3,1}... | collective-permute-start | bytes 688136 | tf_op jit(solution)/shard_map/ppermute | solution.py:37
  35.7 5.0 %collective-permute-done.10 = bf16[64,1792]{1,0:T(8,128)(2,1)S(1)} collective-permute-done((bf16[64,1792]{1,0:T(8,128)(2,1)S(1)}, bf16[64,1792]{1,0:T(8,128)(2,1)S(1)}, u32[]{:S(2)}, u32[]{:S(2)}) %collective-permute-start.10) | collective-permute-done | bytes 229408 | tf_op jit(solution)/shard_map/ppermute | solution.py:36
  40.7 2.7 %collective-permute-start.8 = (bf16[64,1792]{1,0:T(8,128)(2,1)S(1)}, bf16[64,1792]{1,0:T(8,128)(2,1)S(1)}, u32[]{:S(2)}, u32[]{:S(2)}) collective-permute-start(bf16[64,1792]{1,0:T(8,128)(2,1)S(1)} %collective-permute-done.7), channel_id=1, source_target_pairs={{0,14},{2,0},{4,2},{6,4},{8,6},{10,8},{12,10},{14,12},{1,15},{3,1}... | collective-permute-start | bytes 688136 | tf_op jit(solution)/shard_map/ppermute | solution.py:37
  43.4 0.8 collective-permute-start.3
  44.2 2.2 %collective-permute-start.4 = (bf16[64,2304]{1,0:T(8,128)(2,1)S(1)}, bf16[64,2304]{1,0:T(8,128)(2,1)S(1)}, u32[]{:S(2)}, u32[]{:S(2)}) collective-permute-start(bf16[64,2304]{1,0:T(8,128)(2,1)S(1)} %slice.85), channel_id=1, source_target_pairs={{0,192},{64,0},{128,64},{192,128},{1,193},{65,1},{129,65},{193,129... | collective-permute-start | bytes 884744 | tf_op jit(solution)/shard_map/ppermute | solution.py:44
  46.4 1.0 collective-permute-done.11
  47.4 0.1 collective-permute-start.12
  47.5 2.7 %collective-permute-start.13 = (bf16[32,1792]{1,0:T(8,128)(2,1)S(1)}, bf16[32,1792]{1,0:T(8,128)(2,1)S(1)}, u32[]{:S(2)}, u32[]{:S(2)}) collective-permute-start(bf16[32,1792]{1,0:T(8,128)(2,1)S(1)} %slice.91), channel_id=1, source_target_pairs={{0,14},{2,0},{4,2},{6,4},{8,6},{10,8},{12,10},{14,12},{1,15},{3,1}... | collective-permute-start | bytes 344072 | tf_op jit(solution)/shard_map/ppermute | solution.py:44
  50.3 2.4 %collective-permute-done.12 = bf16[32,1792]{1,0:T(8,128)(2,1)S(1)} collective-permute-done((bf16[32,1792]{1,0:T(8,128)(2,1)S(1)}, bf16[32,1792]{1,0:T(8,128)(2,1)S(1)}, u32[]{:S(2)}, u32[]{:S(2)}) %collective-permute-start.12) | collective-permute-done | bytes 114720 | tf_op jit(solution)/shard_map/ppermute | solution.py:43
  52.9 0.3 pad_maximum_fusion
  53.2 4.8 %fusion.41 = f32[512,1024]{1,0:T(8,128)S(1)} fusion(bf16[512,2304]{1,0:T(8,128)(2,1)S(1)} %bitcast.65, bf16[2304,1024]{1,0:T(8,128)(2,1)} %param.12), kind=kOutput, calls=%fused_computation.97 | convolution fusion | flops 2415919104 | bytes 9175040 | tf_op jit(solution)/shard_map/dot_general | solution.py:69
  57.9 1.1 slice.87
  59.0 3.3 %collective-permute-start.5 = (f32[256,1024]{1,0:T(8,128)}, f32[256,1024]{1,0:T(8,128)}, u32[]{:S(2)}, u32[]{:S(2)}) collective-permute-start(f32[256,1024]{1,0:T(8,128)} %slice.87), channel_id=1, source_target_pairs={{0,1},{1,0},{2,3},{3,2},{4,5},{5,4},{6,7},{7,6},{8,9},{9,8},{10,11... | collective-permute-start | bytes 3145736 | tf_op jit(solution)/shard_map/ppermute | solution.py:25
  62.3 2.1 %fusion.42 = f32[512,1024]{1,0:T(8,128)S(1)} fusion(bf16[512,1792]{1,0:T(8,128)(2,1)S(1)} %bitcast.81, bf16[1792,1024]{1,0:T(8,128)(2,1)S(1)} %copy-done.6), kind=kOutput, calls=%fused_computation.98 | convolution fusion | flops 1879048192 | bytes 7602176 | tf_op jit(solution)/shard_map/dot_general | solution.py:69
  64.4 1.3 %copy-done.1 = f32[512,1024]{1,0:T(8,128)} copy-done((f32[512,1024]{1,0:T(8,128)}, f32[512,1024]{1,0:T(8,128)S(1)}, u32[]{:S(2)}) %copy-start.1) | copy-done | bytes 2097176
  65.7 1.1 slice.93
  66.8 0.5 broadcast.114
  67.3 0.7 reduce.31
  68.0 0.1 reshape_squeeze.4
  68.1 0.2 copy.83
  68.3 0.1 fusion.30
  68.4 0.2 copy.85
  68.5 0.1 sub.39
  68.7 1.5 %fusion.21 = bf16[256,1024]{1,0:T(8,128)(2,1)S(1)} fusion(f32[256,1024]{1,0:T(8,128)} %collective-permute-done.5, f32[512,1024]{1,0:T(8,128)S(1)} %fusion.41), kind=kLoop, calls=%fused_computation.37 | loop fusion | flops 1048576 | bytes 2621440 | tf_op jit(solution)/shard_map/convert_element_type | solution.py:17
  70.2 0.4 fusion.8
  70.6 0.1 stack.62
  70.6 0.2 convert_bitcast_fusion
  71.0 1.3 %copy-done.2 = f32[512,1024]{1,0:T(8,128)S(1)} copy-done((f32[512,1024]{1,0:T(8,128)S(1)}, f32[512,1024]{1,0:T(8,128)}, u32[]{:S(2)}) %copy-start.2) | copy-done | bytes 2097176
  72.2 2.4 %fusion.1 = (f32[256]{0:T(256)S(1)}, f32[256]{0:T(256)S(1)}, f32[256]{0:T(256)S(1)}, bf16[256,1024]{1,0:T(8,128)(2,1)S(1)}) fusion(f32[8,4,8,1024]{3,2,1,0:T(8,128)S(1)} %copy.82, s32[256]{0:T(256)S(1)} %sub.39, f32[256,1024]{1,0:T(8,128)} %collective-permute-done.14, f32[512,1024]{1,0:T(8,128)S(1)} %copy-done.2), kind=kLoop, calls=%fused_computation.9 | loop fusion | flops 3144960 | bytes 3674112 | tf_op jit(solution)/shard_map/reduce_sum | solution.py:122
  75.0 0.6 broadcast_in_dim.10
  75.6 3.8 %all-to-all-start.1 = ((f32[16,8,128]{2,1,0:T(8,128)}), f32[16,8,128]{2,1,0:T(8,128)S(1)}, u32[]{:S(2)}, u32[]{:S(2)}) async-start(f32[16,8,128]{2,1,0:T(8,128)} %broadcast_in_dim.10), calls=%async_computation.1 | async-start | bytes 131072 | tf_op jit(solution)/shard_map/all_to_all | solution.py:129
  79.4 6.5 %all-to-all-done.1 = f32[16,8,128]{2,1,0:T(8,128)S(1)} async-done(((f32[16,8,128]{2,1,0:T(8,128)}), f32[16,8,128]{2,1,0:T(8,128)S(1)}, u32[]{:S(2)}, u32[]{:S(2)}) %all-to-all-start.1) | async-done | bytes 65568 | tf_op jit(solution)/shard_map/all_to_all | solution.py:129
  86.0 12.1 %all_to_all.15 = f32[8,8,128]{2,1,0:T(8,128)S(1)} all-to-all(f32[8,8,128]{2,1,0:T(8,128)S(1)} %broadcast_in_dim.11), channel_id=1, replica_groups=mesh['y'=4,'x'=4,'z'=8,'c'=2] {'z'}, dimensions={0} | all-to-all | bytes 65536 | tf_op jit(solution)/shard_map/all_to_all | solution.py:132
  98.4 0.6 fusion.26
  99.0 3.5 %collective-permute-start.15 = (bf16[256,1024]{1,0:T(8,128)(2,1)S(1)}, bf16[256,1024]{1,0:T(8,128)(2,1)S(1)}, u32[]{:S(2)}, u32[]{:S(2)}) collective-permute-start(bf16[256,1024]{1,0:T(8,128)(2,1)S(1)} %fusion.26), channel_id=1, source_target_pairs={{0,1},{1,0},{2,3},{3,2},{4,5},{5,4},{6,7},{7,6},{8,9},{9,8},{10,11... | collective-permute-start | bytes 1572872 | tf_op jit(solution)/shard_map/ppermute | solution.py:25
  102.4 0.1 slice_reduce_fusion.4
  102.7 0.1 squeeze.25
  102.8 0.1 squeeze.23
  102.9 0.5 fusion.38
  103.4 0.6 collective-permute-done.15
  104.0 5.4 %convolution_convert_fusion = bf16[1792,1024]{1,0:T(8,128)(2,1)} fusion(bf16[512,1792]{1,0:T(8,128)(2,1)} %bitcast.82, bf16[256,1024]{1,0:T(8,128)(2,1)S(1)} %collective-permute-done.15, bf16[256,1024]{1,0:T(8,128)(2,1)S(1)} %fusion.26), kind=kOutput, calls=%fused_computation | convolution fusion | flops 1882980352 | bytes 6553600 | tf_op jit(solution)/shard_map/dot_general | solution.py:144
  (69 shorter events, 1.4 us)
Async XLA Ops:
  0.6 13.2 %copy-start = (bf16[1,64,4608]{2,1,0:T(8,128)(2,1)S(1)}, bf16[1,64,4608]{2,1,0:T(8,128)(2,1)}, u32[]{:S(2)}) copy-start(bf16[1,64,4608]{2,1,0:T(8,128)(2,1)} %param.8) | copy-start | bytes 1769476
  0.6 14.2 %copy-start.4 = (f32[4608]{0:T(1024)S(1)}, f32[4608]{0:T(1024)}, u32[]{:S(2)}) copy-start(f32[4608]{0:T(1024)} %param.10) | copy-start | bytes 55300
  4.0 17.2 %all-to-all-start = ((bf16[32,2,1792]{2,1,0:T(2,128)(2,1)}), bf16[32,2,1792]{2,1,0:T(2,128)(2,1)S(1)}, u32[]{:S(2)}, u32[]{:S(2)}) async-start(bf16[32,2,1792]{2,1,0:T(2,128)(2,1)} %bitcast.14), calls=%async_computation | async-start | bytes 458752 | tf_op jit(solution)/shard_map/all_to_all | solution.py:85
  17.8 9.4 %collective-permute-start = (bf16[64,2304]{1,0:T(8,128)(2,1)S(1)}, bf16[64,2304]{1,0:T(8,128)(2,1)S(1)}, u32[]{:S(2)}, u32[]{:S(2)}) collective-permute-start(bf16[64,2304]{1,0:T(8,128)(2,1)S(1)} %bitcast.74), channel_id=1, source_target_pairs={{0,1},{1,0},{2,3},{3,2},{4,5},{5,4},{6,7},{7,6},{8,9},{9,8},{10,11... | collective-permute-start | bytes 884744 | tf_op jit(solution)/shard_map/ppermute | solution.py:25
  21.5 11.5 %collective-permute-start.9 = (bf16[64,1792]{1,0:T(8,128)(2,1)S(1)}, bf16[64,1792]{1,0:T(8,128)(2,1)S(1)}, u32[]{:S(2)}, u32[]{:S(2)}) collective-permute-start(bf16[64,1792]{1,0:T(8,128)(2,1)S(1)} %constant_dynamic-update-slice_fusion), channel_id=1, source_target_pairs={{0,2},{2,4},{4,6},{6,8},{8,10},{10,12},{12,14},{14,0},{1,3},{3,5},... | collective-permute-start | bytes 688136 | tf_op jit(solution)/shard_map/ppermute | solution.py:36
  23.2 9.8 %collective-permute-start.6 = (bf16[64,1792]{1,0:T(8,128)(2,1)S(1)}, bf16[64,1792]{1,0:T(8,128)(2,1)S(1)}, u32[]{:S(2)}, u32[]{:S(2)}) collective-permute-start(bf16[64,1792]{1,0:T(8,128)(2,1)S(1)} %constant_dynamic-update-slice_fusion), channel_id=1, source_target_pairs={{0,14},{2,0},{4,2},{6,4},{8,6},{10,8},{12,10},{14,12},{1,15},{3,1}... | collective-permute-start | bytes 688136 | tf_op jit(solution)/shard_map/ppermute | solution.py:37
  27.3 16.1 %collective-permute-start.2 = (bf16[128,2304]{1,0:T(8,128)(2,1)S(1)}, bf16[128,2304]{1,0:T(8,128)(2,1)S(1)}, u32[]{:S(2)}, u32[]{:S(2)}) collective-permute-start(bf16[128,2304]{1,0:T(8,128)(2,1)S(1)} %pad_maximum_fusion.1), channel_id=1, source_target_pairs={{0,64},{64,128},{128,192},{192,0},{1,65},{65,129},{129,193},{193,1... | collective-permute-start | bytes 1769480 | tf_op jit(solution)/shard_map/ppermute | solution.py:36
  27.7 16.5 %collective-permute-start.1 = (bf16[128,2304]{1,0:T(8,128)(2,1)S(1)}, bf16[128,2304]{1,0:T(8,128)(2,1)S(1)}, u32[]{:S(2)}, u32[]{:S(2)}) collective-permute-start(bf16[128,2304]{1,0:T(8,128)(2,1)S(1)} %pad_maximum_fusion.1), channel_id=1, source_target_pairs={{0,192},{64,0},{128,64},{192,128},{1,193},{65,1},{129,65},{193,129... | collective-permute-start | bytes 1769480 | tf_op jit(solution)/shard_map/ppermute | solution.py:37
  33.0 7.7 %collective-permute-start.10 = (bf16[64,1792]{1,0:T(8,128)(2,1)S(1)}, bf16[64,1792]{1,0:T(8,128)(2,1)S(1)}, u32[]{:S(2)}, u32[]{:S(2)}) collective-permute-start(bf16[64,1792]{1,0:T(8,128)(2,1)S(1)} %collective-permute-done.9), channel_id=1, source_target_pairs={{0,2},{2,4},{4,6},{6,8},{8,10},{10,12},{12,14},{14,0},{1,3},{3,5},... | collective-permute-start | bytes 688136 | tf_op jit(solution)/shard_map/ppermute | solution.py:36
  33.0 7.7 %collective-permute-start.7 = (bf16[64,1792]{1,0:T(8,128)(2,1)S(1)}, bf16[64,1792]{1,0:T(8,128)(2,1)S(1)}, u32[]{:S(2)}, u32[]{:S(2)}) collective-permute-start(bf16[64,1792]{1,0:T(8,128)(2,1)S(1)} %collective-permute-done.6), channel_id=1, source_target_pairs={{0,14},{2,0},{4,2},{6,4},{8,6},{10,8},{12,10},{14,12},{1,15},{3,1}... | collective-permute-start | bytes 688136 | tf_op jit(solution)/shard_map/ppermute | solution.py:37
  40.7 6.7 %collective-permute-start.11 = (bf16[64,1792]{1,0:T(8,128)(2,1)S(1)}, bf16[64,1792]{1,0:T(8,128)(2,1)S(1)}, u32[]{:S(2)}, u32[]{:S(2)}) collective-permute-start(bf16[64,1792]{1,0:T(8,128)(2,1)S(1)} %collective-permute-done.10), channel_id=1, source_target_pairs={{0,2},{2,4},{4,6},{6,8},{8,10},{10,12},{12,14},{14,0},{1,3},{3,5},... | collective-permute-start | bytes 688136 | tf_op jit(solution)/shard_map/ppermute | solution.py:36
  40.7 6.8 %collective-permute-start.8 = (bf16[64,1792]{1,0:T(8,128)(2,1)S(1)}, bf16[64,1792]{1,0:T(8,128)(2,1)S(1)}, u32[]{:S(2)}, u32[]{:S(2)}) collective-permute-start(bf16[64,1792]{1,0:T(8,128)(2,1)S(1)} %collective-permute-done.7), channel_id=1, source_target_pairs={{0,14},{2,0},{4,2},{6,4},{8,6},{10,8},{12,10},{14,12},{1,15},{3,1}... | collective-permute-start | bytes 688136 | tf_op jit(solution)/shard_map/ppermute | solution.py:37
  43.4 9.4 %collective-permute-start.3 = (bf16[64,2304]{1,0:T(8,128)(2,1)S(1)}, bf16[64,2304]{1,0:T(8,128)(2,1)S(1)}, u32[]{:S(2)}, u32[]{:S(2)}) collective-permute-start(bf16[64,2304]{1,0:T(8,128)(2,1)S(1)} %slice.84), channel_id=1, source_target_pairs={{0,64},{64,128},{128,192},{192,0},{1,65},{65,129},{129,193},{193,1... | collective-permute-start | bytes 884744 | tf_op jit(solution)/shard_map/ppermute | solution.py:43
  44.2 8.6 %collective-permute-start.4 = (bf16[64,2304]{1,0:T(8,128)(2,1)S(1)}, bf16[64,2304]{1,0:T(8,128)(2,1)S(1)}, u32[]{:S(2)}, u32[]{:S(2)}) collective-permute-start(bf16[64,2304]{1,0:T(8,128)(2,1)S(1)} %slice.85), channel_id=1, source_target_pairs={{0,192},{64,0},{128,64},{192,128},{1,193},{65,1},{129,65},{193,129... | collective-permute-start | bytes 884744 | tf_op jit(solution)/shard_map/ppermute | solution.py:44
  47.4 5.2 %collective-permute-start.12 = (bf16[32,1792]{1,0:T(8,128)(2,1)S(1)}, bf16[32,1792]{1,0:T(8,128)(2,1)S(1)}, u32[]{:S(2)}, u32[]{:S(2)}) collective-permute-start(bf16[32,1792]{1,0:T(8,128)(2,1)S(1)} %slice.90), channel_id=1, source_target_pairs={{0,2},{2,4},{4,6},{6,8},{8,10},{10,12},{12,14},{14,0},{1,3},{3,5},... | collective-permute-start | bytes 344072 | tf_op jit(solution)/shard_map/ppermute | solution.py:43
  47.5 5.1 %collective-permute-start.13 = (bf16[32,1792]{1,0:T(8,128)(2,1)S(1)}, bf16[32,1792]{1,0:T(8,128)(2,1)S(1)}, u32[]{:S(2)}, u32[]{:S(2)}) collective-permute-start(bf16[32,1792]{1,0:T(8,128)(2,1)S(1)} %slice.91), channel_id=1, source_target_pairs={{0,14},{2,0},{4,2},{6,4},{8,6},{10,8},{12,10},{14,12},{1,15},{3,1}... | collective-permute-start | bytes 344072 | tf_op jit(solution)/shard_map/ppermute | solution.py:44
  52.8 9.6 %copy-start.3 = (bf16[8,2,32,1792]{3,2,0,1:T(8,128)(2,1)}, bf16[8,2,32,1792]{3,2,0,1:T(8,128)(2,1)S(1)}, u32[]{:S(2)}) copy-start(bf16[8,2,32,1792]{3,2,0,1:T(8,128)(2,1)S(1)} %constant_dynamic-update-slice_fusion.2) | copy-start | bytes 5505028
  53.2 9.2 %copy-start.6 = (bf16[1792,1024]{1,0:T(8,128)(2,1)S(1)}, bf16[1792,1024]{1,0:T(8,128)(2,1)}, u32[]{:S(2)}) copy-start(bf16[1792,1024]{1,0:T(8,128)(2,1)} %param.11) | copy-start | bytes 11010052
  59.0 9.7 %collective-permute-start.5 = (f32[256,1024]{1,0:T(8,128)}, f32[256,1024]{1,0:T(8,128)}, u32[]{:S(2)}, u32[]{:S(2)}) collective-permute-start(f32[256,1024]{1,0:T(8,128)} %slice.87), channel_id=1, source_target_pairs={{0,1},{1,0},{2,3},{3,2},{4,5},{5,4},{6,7},{7,6},{8,9},{9,8},{10,11... | collective-permute-start | bytes 3145736 | tf_op jit(solution)/shard_map/ppermute | solution.py:25
  64.4 1.3 %copy-start.1 = (f32[512,1024]{1,0:T(8,128)}, f32[512,1024]{1,0:T(8,128)S(1)}, u32[]{:S(2)}) copy-start(f32[512,1024]{1,0:T(8,128)S(1)} %fusion.42) | copy-start | bytes 6291460
  65.7 1.6 %copy-start.5 = (s32[1,256]{1,0:T(1,128)S(1)}, s32[1,256]{1,0:T(1,128)}, u32[]{:S(2)}) copy-start(s32[1,256]{1,0:T(1,128)} %param.13) | copy-start | bytes 3076
  66.8 4.2 %collective-permute-start.14 = (f32[256,1024]{1,0:T(8,128)}, f32[256,1024]{1,0:T(8,128)}, u32[]{:S(2)}, u32[]{:S(2)}) collective-permute-start(f32[256,1024]{1,0:T(8,128)} %slice.93), channel_id=1, source_target_pairs={{0,1},{1,0},{2,3},{3,2},{4,5},{5,4},{6,7},{7,6},{8,9},{9,8},{10,11... | collective-permute-start | bytes 3145736 | tf_op jit(solution)/shard_map/ppermute | solution.py:25
  70.6 1.6 %copy-start.2 = (f32[512,1024]{1,0:T(8,128)S(1)}, f32[512,1024]{1,0:T(8,128)}, u32[]{:S(2)}) copy-start(f32[512,1024]{1,0:T(8,128)} %copy-done.1) | copy-start | bytes 6291460
  75.6 10.3 %all-to-all-start.1 = ((f32[16,8,128]{2,1,0:T(8,128)}), f32[16,8,128]{2,1,0:T(8,128)S(1)}, u32[]{:S(2)}, u32[]{:S(2)}) async-start(f32[16,8,128]{2,1,0:T(8,128)} %broadcast_in_dim.10), calls=%async_computation.1 | async-start | bytes 131072 | tf_op jit(solution)/shard_map/all_to_all | solution.py:129
  99.0 5.0 %collective-permute-start.15 = (bf16[256,1024]{1,0:T(8,128)(2,1)S(1)}, bf16[256,1024]{1,0:T(8,128)(2,1)S(1)}, u32[]{:S(2)}, u32[]{:S(2)}) collective-permute-start(bf16[256,1024]{1,0:T(8,128)(2,1)S(1)} %fusion.26), channel_id=1, source_target_pairs={{0,1},{1,0},{2,3},{3,2},{4,5},{5,4},{6,7},{7,6},{8,9},{9,8},{10,11... | collective-permute-start | bytes 1572872 | tf_op jit(solution)/shard_map/ppermute | solution.py:25

commit v2 on v1

v2 whole, which is shorter than its diff:
```python
import functools

import jax
import jax.numpy as jnp
from jax import lax
from jax.experimental import pallas as pl
from jax.experimental.pallas import tpu as pltpu
from jax.sharding import Mesh, PartitionSpec as P

F32 = jnp.float32
BF16 = jnp.bfloat16
I32 = jnp.int32
NY, NX, NZ = 4, 4, 8
ROWS = 2
PLANE = NY * NX * ROWS
OWN = NZ * PLANE
EARLY = OWN - PLANE
LANES = 128
VMEM = pl.BlockSpec(memory_space=pltpu.VMEM)


def params():
    return pltpu.CompilerParams(vmem_limit_bytes=50 * 1024 * 1024)


def cost(flops, bytes_accessed, transcendentals=0):
    return pl.CostEstimate(
        flops=flops, bytes_accessed=bytes_accessed, transcendentals=transcendentals
    )


def up(n, k):
    return [(i, (i + k) % n) for i in range(n)]


def swap_cores(value):
    return lax.ppermute(value, "c", [(0, 1), (1, 0)])


def ring(block, axis, n):
    blocks = [block]
    from_low = from_high = block
    for _ in range(n // 2 - 1):
        from_low = lax.ppermute(from_low, axis, up(n, 1))
        from_high = lax.ppermute(from_high, axis, up(n, -1))
        blocks += [from_low, from_high]
    half = block.shape[0] // 2
    blocks.append(lax.ppermute(from_low[:half], axis, up(n, 1)))
    blocks.append(lax.ppermute(from_high[half:], axis, up(n, -1)))
    return blocks


def distance(position):
    return jnp.where(position % 2 == 1, NZ - (position + 1) // 2, position // 2)


def natural_row(row, z):
    position, inner = row // PLANE, row % PLANE
    y, x, i = inner // (NX * ROWS), inner // ROWS % NX, inner % ROWS
    return ((y * NX + x) * NZ + (z + distance(position)) % NZ) * ROWS + i


def iota(shape, axis):
    return lax.broadcasted_iota(I32, shape, axis)


def normalize(hidden, gain):
    values = hidden.astype(F32)
    spread = jnp.mean(values * values, axis=-1, keepdims=True)
    return (values * lax.rsqrt(spread + 1e-06) * gain).astype(BF16)


def student_norm_kernel(hidden_ref, gain_ref, out_ref):
    normed = normalize(hidden_ref[...], gain_ref[...])
    half = normed.shape[1] // 2
    for peer in range(NY * NX):
        out_ref[2 * peer] = normed[:, :half]
        out_ref[2 * peer + 1] = normed[:, half:]


def student_norm(hidden, gain):
    rows, width = hidden.shape
    return pl.pallas_call(
        student_norm_kernel,
        out_shape=jax.ShapeDtypeStruct((NY * NX * 2, rows, width // 2), BF16),
        in_specs=[VMEM, VMEM],
        out_specs=VMEM,
        compiler_params=params(),
    )(hidden, gain[None])


def teacher_norm_kernel(hidden_ref, gain_ref, keep_ref, send_ref):
    z, core = lax.axis_index("z"), lax.axis_index("c")
    normed = normalize(hidden_ref[...], gain_ref[...])
    n = normed.shape[0]
    row = iota((n, n), 0)
    position, x, i = row // (NX * ROWS), row // ROWS % NX, row % ROWS
    source = (x * NZ + (z + distance(position)) % NZ) * ROWS + i
    moved = jnp.where(iota((n, n), 1) == source, 1.0, 0.0).astype(BF16)
    normed = jnp.dot(moved, normed, preferred_element_type=F32).astype(BF16)
    half = normed.shape[1] // 2

    @pl.when(core == 0)
    def _():
        keep_ref[...] = normed[:, :half]
        send_ref[...] = normed[:, half:]

    @pl.when(core != 0)
    def _():
        keep_ref[...] = normed[:, half:]
        send_ref[...] = normed[:, :half]


def teacher_norm(hidden, gain):
    rows, width = hidden.shape
    part = jax.ShapeDtypeStruct((rows, width // 2), BF16)
    return pl.pallas_call(
        teacher_norm_kernel,
        out_shape=(part, part),
        in_specs=[VMEM, VMEM],
        out_specs=(VMEM, VMEM),
        compiler_params=params(),
    )(hidden, gain[None])


def teacher_logits_kernel(b0, b1, b2, b3, b4, w_ref, own_ref, other_ref, rows_ref):
    section = b0.shape[0] // 2

    @pl.when(pl.program_id(0) == 0)
    def _():
        y = lax.axis_index("y")
        row = iota((OWN, OWN), 0)
        position, inner = row // PLANE, row % PLANE
        apart = (inner // (NX * ROWS) - y) % NY
        place = jnp.where(
            apart == 0, 0, jnp.where(apart == NY - 1, 1, jnp.where(apart == 1, 2, 3))
        )
        source = place * section + position * (NX * ROWS) + inner % (NX * ROWS)
        moved = jnp.where(iota((OWN, OWN), 1) == source, 1.0, 0.0).astype(BF16)
        for side, last in ((0, b3), (1, b4)):
            part = pl.ds(side * section, section)
            whole = jnp.concatenate([b0[part], b1[part], b2[part], last[...]])
            rows_ref[pl.ds(side * OWN, OWN)] = jnp.dot(
                moved, whole, preferred_element_type=F32
            ).astype(BF16)

    result = jnp.dot(rows_ref[...], w_ref[...], preferred_element_type=F32)
    own_ref[...] = result[:OWN]
    other_ref[...] = result[OWN:]


def teacher_logits(blocks, head):
    k, vocab = head.shape
    tile = 256
    part = jax.ShapeDtypeStruct((OWN, vocab), F32)
    whole = [pl.BlockSpec(b.shape, lambda j: (0, 0)) for b in blocks]
    column = pl.BlockSpec((OWN, tile), lambda j: (0, j))
    return pl.pallas_call(
        teacher_logits_kernel,
        grid=(vocab // tile,),
        out_shape=(part, part),
        in_specs=whole + [pl.BlockSpec((k, tile), lambda j: (0, j))],
        out_specs=(column, column),
        scratch_shapes=[pltpu.VMEM((2 * OWN, k), BF16)],
        compiler_params=params(),
        cost_estimate=cost(4 * OWN * k * vocab, 2 * k * vocab + 8 * OWN * vocab),
    )(*blocks, head)


def student_logits_kernel(*refs):
    *blocks, w_ref, own_ref, other_ref, rows_ref = refs
    n = own_ref.shape[0]

    @pl.when(pl.program_id(0) == 0)
    def _():
        for q, block in enumerate(blocks):
            if len(blocks) == 2:
                rows_ref[pl.ds(q * PLANE, PLANE)] = block[...]
            else:
                rows_ref[pl.ds(q * PLANE, PLANE)] = block[:PLANE]
                rows_ref[pl.ds(n + q * PLANE, PLANE)] = block[PLANE:]

    result = jnp.dot(rows_ref[...], w_ref[...], preferred_element_type=F32)
    own_ref[...] = result[:n]
    other_ref[...] = result[n:]


def student_logits(blocks, head):
    k, vocab = head.shape
    tile = 256
    n = sum(b.shape[0] for b in blocks) // 2
    part = jax.ShapeDtypeStruct((n, vocab), F32)
    whole = [pl.BlockSpec(b.shape, lambda j: (0, 0)) for b in blocks]
    column = pl.BlockSpec((n, tile), lambda j: (0, j))
    return pl.pallas_call(
        student_logits_kernel,
        grid=(vocab // tile,),
        out_shape=(part, part),
        in_specs=whole + [pl.BlockSpec((k, tile), lambda j: (0, j))],
        out_specs=(column, column),
        scratch_shapes=[pltpu.VMEM((2 * n, k), BF16)],
        compiler_params=params(),
        cost_estimate=cost(4 * n * k * vocab, 2 * k * vocab + 8 * n * vocab),
    )(*blocks, head)


def soft_cap(logits):
    return (30.0 * jnp.tanh(logits / 30.0)).astype(BF16)


def local_targets(targets_ref, z, first, rows):
    shape = (rows.shape[0], OWN)
    here = iota(shape, 1) == natural_row(rows, z)
    return jnp.sum(jnp.where(here, targets_ref[...], 0), axis=1, keepdims=True) - first


def first_column(vocab):
    y, x, z = lax.axis_index("y"), lax.axis_index("x"), lax.axis_index("z")
    return ((y * NX + x) * NZ + z) * vocab


def fold(values):
    total = values[:, :LANES]
    for start in range(LANES, values.shape[1], LANES):
        total = total + values[:, start : start + LANES]
    return total


def vocab_sums(start, own, got, t_own, t_got, targets_ref, student_ref, teacher_ref, write):
    n, vocab = own.shape
    z, first = lax.axis_index("z"), first_column(vocab)
    step = 32
    for at in range(0, n, step):
        part, t_part = pl.ds(at, step), pl.ds(start + at, step)
        student = soft_cap(own[part] + got[part])
        teacher = soft_cap(t_own[t_part] + t_got[t_part])
        student_ref[part] = student
        teacher_ref[part] = teacher
        stud_vals, teach_vals = student.astype(F32), teacher.astype(F32)
        stud_exp, teach_exp = jnp.exp(stud_vals), jnp.exp(teach_vals)
        target = local_targets(targets_ref, z, first, iota((step, 1), 0) + (start + at))
        hit = iota((step, vocab), 1) == target
        write(0, at, fold(teach_exp))
        write(1, at, fold(stud_exp))
        write(2, at, fold(teach_exp * (teach_vals - stud_vals)))
        write(3, at, fold(jnp.where(hit, stud_vals, 0.0)))


def early_sums_kernel(own, got, t_own, t_got, targets_ref, student_ref, teacher_ref, sums_ref):
    def write(kind, at, value):
        sums_ref[kind, pl.ds(at, value.shape[0])] = value

    vocab_sums(0, own, got, t_own, t_got, targets_ref, student_ref, teacher_ref, write)


def early_sums(own, got, t_own, t_got, targets):
    n, vocab = own.shape
    values = jax.ShapeDtypeStruct((n, vocab), BF16)
    return pl.pallas_call(
        early_sums_kernel,
        out_shape=(values, values, jax.ShapeDtypeStruct((4, n, LANES), F32)),
        in_specs=[VMEM] * 5,
        out_specs=(VMEM,) * 3,
        compiler_params=params(),
        cost_estimate=cost(40 * n * vocab, 20 * n * vocab, 4 * n * vocab),
    )(own, got, t_own, t_got, targets)


def last_sums_kernel(
    own, got, t_own, t_got, targets_ref, early_ref, student_ref, teacher_ref, out_ref, sums_ref
):
    def write(kind, at, value):
        sums_ref[kind, pl.ds(EARLY + at, value.shape[0])] = value

    sums_ref[:, :EARLY] = early_ref[...]
    vocab_sums(EARLY, own, got, t_own, t_got, targets_ref, student_ref, teacher_ref, write)
    z = lax.axis_index("z")
    here = iota((OWN, OWN), 1) == natural_row(iota((OWN, OWN), 0), z)
    rows = []
    for kind in range(4):
        total = jnp.sum(sums_ref[kind], axis=1, keepdims=True)
        flat = jnp.sum(jnp.where(here, total, 0.0), axis=0, keepdims=True)
        rows += [flat[:, at : at + LANES] for at in range(0, OWN, LANES)]
    tile = jnp.concatenate(rows, axis=0)
    for peer in range(out_ref.shape[0]):
        out_ref[peer] = tile


def last_sums(own, got, t_own, t_got, targets, early):
    n, vocab = own.shape
    values = jax.ShapeDtypeStruct((n, vocab), BF16)
    return pl.pallas_call(
        last_sums_kernel,
        out_shape=(values, values, jax.ShapeDtypeStruct((NY * NX, 8, LANES), F32)),
        in_specs=[VMEM] * 6,
        out_specs=(VMEM,) * 3,
        scratch_shapes=[pltpu.VMEM((4, OWN, LANES), F32)],
        compiler_params=params(),
        cost_estimate=cost(40 * n * vocab, 20 * n * vocab, 4 * n * vocab),
    )(own, got, t_own, t_got, targets, early)


def gradient_kernel(*refs):
    (
        sums_ref,
        s_own0, s_own1, t_own0, t_own1,
        s_oth0, s_oth1, t_oth0, t_oth1,
        targets_ref, oth_targets_ref, *blocks, loss_ref, out_ref, rows_ref, grad_ref,
    ) = refs
    vocab = out_ref.shape[1]

    @pl.when(pl.program_id(0) == 0)
    def _():
        z, core = lax.axis_index("z"), lax.axis_index("c")
        first = first_column(vocab)
        position = (lax.axis_index("y") * NX + lax.axis_index("x")) * NZ + z
        here = iota((OWN, OWN), 1) == natural_row(iota((OWN, OWN), 0), z)
        totals = []
        for side in range(2):
            total = sums_ref[side]
            for peer in range(1, NZ):
                total = total + sums_ref[2 * peer + side]
            totals.append(total)
        own = jnp.where(core == 0, totals[0], totals[1])
        other = jnp.where(core == 0, totals[1], totals[0])

        def flat(tile, kind):
            return jnp.concatenate([tile[2 * kind : 2 * kind + 1], tile[2 * kind + 1 : 2 * kind + 2]], axis=1)

        teach_total, stud_total, cross_sum, target_logit = (flat(own, k) for k in range(4))
        loss = cross_sum / teach_total - jnp.log(teach_total) + 2.0 * jnp.log(stud_total) - target_logit
        lane = iota((1, OWN), 1)
        picked = [
            jnp.sum(jnp.where(lane == position * ROWS + i, loss, 0.0), axis=1, keepdims=True)
            for i in range(ROWS)
        ]
        loss_ref[...] = jnp.concatenate(picked, axis=1)

        for side, tile, s_refs, t_refs, targets in (
            (0, own, (s_own0, s_own1), (t_own0, t_own1), targets_ref),
            (1, other, (s_oth0, s_oth1), (t_oth0, t_oth1), oth_targets_ref),
        ):
            teach_scale = jnp.sum(jnp.where(here, 1.0 / flat(tile, 0), 0.0), axis=1, keepdims=True)
            stud_scale = jnp.sum(jnp.where(here, 2.0 / flat(tile, 1), 0.0), axis=1, keepdims=True)
            target = local_targets(targets, z, first, iota((OWN, 1), 0))
            step = 32
            for at in range(0, OWN, step):
                which, offset = (0, at) if at < EARLY else (1, at - EARLY)
                stud_vals = s_refs[which][pl.ds(offset, step)].astype(F32)
                teach_vals = t_refs[which][pl.ds(offset, step)].astype(F32)
                rows = slice(at, at + step)
                scaled = jnp.exp(stud_vals) * stud_scale[rows] - jnp.exp(teach_vals) * teach_scale[rows]
                hit = iota((step, vocab), 1) == target[rows]
                scaled = scaled - jnp.where(hit, 1.0, 0.0)
                value = scaled * (1.0 - stud_vals * stud_vals * (1.0 / 900.0))
                grad_ref[pl.ds(side * OWN + at, step)] = value.astype(BF16)
        for q, block in enumerate(blocks[: NZ - 1]):
            rows_ref[pl.ds(q * PLANE, PLANE)] = block[:PLANE]
            rows_ref[pl.ds(OWN + q * PLANE, PLANE)] = block[PLANE:]
        rows_ref[pl.ds(EARLY, PLANE)] = blocks[NZ - 1][...]
        rows_ref[pl.ds(OWN + EARLY, PLANE)] = blocks[NZ][...]

    tile = out_ref.shape[0]
    start = pl.multiple_of(pl.program_id(0) * tile, tile)
    out_ref[...] = lax.dot_general(
        rows_ref[:, pl.ds(start, tile)],
        grad_ref[...],
        (((0,), (0,)), ((), ())),
        preferred_element_type=F32,
    ).astype(BF16)


def gradient(sums, own, other, targets, oth_targets, blocks, k, vocab):
    tile = 256
    ops = [sums, *own, *other, targets, oth_targets, *blocks]
    in_specs = [pl.BlockSpec(a.shape, functools.partial(lambda n, j: (0,) * n, a.ndim)) for a in ops]
    return pl.pallas_call(
        gradient_kernel,
        grid=(k // tile,),
        out_shape=(
            jax.ShapeDtypeStruct((1, ROWS), F32),
            jax.ShapeDtypeStruct((k, vocab), BF16),
        ),
        in_specs=in_specs,
        out_specs=(
            pl.BlockSpec((1, ROWS), lambda j: (0, 0)),
            pl.BlockSpec((tile, vocab), lambda j: (j, 0)),
        ),
        scratch_shapes=[pltpu.VMEM((2 * OWN, k), BF16), pltpu.VMEM((2 * OWN, vocab), BF16)],
        compiler_params=params(),
        cost_estimate=cost(4 * OWN * k * vocab, 2 * k * vocab + 12 * OWN * vocab),
    )(*ops)


def shards(
    student_hidden, teacher_hidden, student_gain, teacher_gain, student_head, teacher_head, targets
):
    core = lax.axis_index("c")
    k_s, vocab = student_head.shape

    sent = student_norm(student_hidden[0], student_gain)
    got = lax.all_to_all(sent, ("y", "x", "c"), 0, 0, tiled=True)
    got = got.reshape(NY * NX, 2, ROWS, k_s)
    mine = jnp.where(core == 0, got[:, 0], got[:, 1]).reshape(PLANE, k_s)
    theirs = jnp.where(core == 0, got[:, 1], got[:, 0]).reshape(PLANE, k_s)
    planes = ring(jnp.concatenate([mine, theirs]), "z", NZ)

    keep, send = teacher_norm(teacher_hidden[0], teacher_gain)
    sections = ring(jnp.concatenate([keep, swap_cores(send)]), "y", NY)
    t_own, t_send = teacher_logits(sections, teacher_head)
    t_got = swap_cores(t_send)
    oth_targets = swap_cores(targets)

    s_own0, s_send0 = student_logits(planes[: NZ - 1], student_head)
    s_got0 = swap_cores(s_send0)
    stud0, teach0, early = early_sums(s_own0, s_got0, t_own, t_got, targets)
    s_own1, s_send1 = student_logits(planes[NZ - 1 :], student_head)
    s_got1 = swap_cores(s_send1)
    stud1, teach1, sums = last_sums(s_own1, s_got1, t_own, t_got, targets, early)
    own = (stud0, stud1, teach0, teach1)
    other = tuple(swap_cores(v) for v in own)
    sums = jnp.sum(lax.all_to_all(sums, ("y", "x"), 0, 0, tiled=True), axis=0)
    sums = jnp.broadcast_to(sums[None], (2 * NZ,) + sums.shape)
    sums = lax.all_to_all(sums, ("z", "c"), 0, 0, tiled=True)

    return gradient(sums, own, other, targets, oth_targets, planes, k_s, vocab)


def solution(mesh):
    cube = mesh.devices.reshape(NY, NX, NZ, 2)
    grid = Mesh(cube, ("y", "x", "z", "c"))
    group = ("y", "x", "z")
    placed = (
        P("c", group, None),
        P("c", "y", None),
        P(),
        P(),
        P("c", group),
        P("c", group),
        P("c", None),
    )
    return jax.shard_map(
        shards,
        mesh=grid,
        in_specs=placed,
        out_specs=(P("c", group), P("c", group)),
        check_vma=False,
    )
```

time: 110 us -> 122 us (1.11)
  Pallas kernels: 0 us -> 25.9 us
  matrix products: 12.3 us -> 0 us
  waiting for transfers between devices: 21.3 us -> 32.6 us
  other arithmetic: 11.4 us -> 0.2 us
  local copies, waits for them, and re-layouts: 12.1 us -> 9.41 us
  starting transfers between devices: 39.2 us -> 40.9 us
    pallas_call x0 -> x8, Pallas kernels: none -> 25.9 us  [the longest x2 7.78 us: student_logits(): pl.pallas_call(student_logits_kernel, grid=(vocab // tile,), out_shape=(p...]
    dot_general x3 -> x0, matrix products: 12.3 us -> none  [the longest x2 6.81 us: dot(): return jnp.dot(left, right, preferred_element_type=F32)]
    ppermute x4, waiting for transfers between devices: 0.01 us -> 11.4 us  [ring(): from_high = lax.ppermute(from_high, axis, up(n, -1))]
    ppermute x4, waiting for transfers between devices: 8.89 us -> 0.01 us  [ring(): from_low = lax.ppermute(from_low, axis, up(n, 1))]
    reduce_sum x6 -> x1, other arithmetic: 4.98 us -> 0.02 us  [shards(): sums = jnp.sum(lax.all_to_all(sums, ('y', 'x'), 0, 0, tiled=True), axis=0)]
    ppermute x4, starting transfers between devices: 11.7 us -> 15.7 us  [ring(): from_high = lax.ppermute(from_high, axis, up(n, -1))]
    unnamed x25 -> x28, local copies, waits for them, and re-layouts: 3.32 us -> 7.12 us
    ppermute x4 -> x9, waiting for transfers between devices: 0.57 us -> 4.29 us  [swap_cores(): return lax.ppermute(value, 'c', [(0, 1), (1, 0)])]
  transfers between devices with their start and end apart: 18 -> 23, of which waited for: 7 -> 9; matrix products, arithmetic and copies ran while one was open for 13% -> 1% of each run, Pallas kernels for 0% -> 13%
where the time goes in v2:
time: 122 us; the launch traced here: 121 us
  starting transfers between devices  40.9 us (34%)
  waiting for transfers between devices  32.6 us (27%)
  Pallas kernels  25.9 us (21%)
  blocking collectives  11.1 us (9%)
  local copies, waits for them, and re-layouts  9.41 us (8%)
    ppermute x4, starting transfers between devices, ring(): from_high = lax.ppermute(from_high, axis, up(n, -1))  15.7 us
    ppermute x4, waiting for transfers between devices, ring(): from_high = lax.ppermute(from_high, axis, up(n, -1))  11.4 us
    all_to_all x1, blocking collectives, shards(): sums = jnp.sum(lax.all_to_all(sums, ('y', 'x'), 0, 0, tiled=True), axis=0)  11.1 us
    all_to_all x1, starting transfers between devices, shards(): got = lax.all_to_all(sent, ('y', 'x', 'c'), 0, 0, tiled=True)  8.59 us
    pallas_call x2, Pallas kernels, student_logits(): pl.pallas_call(student_logits_kernel, grid=(vocab // tile,), out_shape=(p...  7.78 us
    unnamed x28, local copies, waits for them, and re-layouts  7.12 us
    pallas_call x1, Pallas kernels, teacher_logits(): pl.pallas_call(teacher_logits_kernel, grid=(vocab // tile,), out_shape=(p...  6.72 us
    pallas_call x1, Pallas kernels, gradient(): pl.pallas_call(gradient_kernel, grid=(k // tile,), out_shape=(jax.ShapeDt...  6.7 us
  transfers between devices with their start and end apart: 23, of which 9 were waited for; matrix products, arithmetic and copies ran while one was open for 1% of the time, Pallas kernels for 13%

profile of v2, /device:TPU:1, one launch (start us, length us, event | category | flops | bytes accessed | tf_op | source)
XLA Modules:
  0.0 120.9 jit_solution(6702336660556393222)
XLA Ops:
  0.6 0.7 broadcast_in_dim.12.gain_ref
  1.4 0.0 copy-start.5
  1.4 0.7 copy-done.5
  2.1 0.8 shard_map.86
  2.9 8.6 %all-to-all-start = ((bf16[32,2,1792]{2,1,0:T(2,128)(2,1)}), bf16[32,2,1792]{2,1,0:T(2,128)(2,1)S(1)}, u32[]{:S(2)}, u32[]{:S(2)}) async-start(bf16[32,2,1792]{2,1,0:T(2,128)(2,1)} %shard_map.86), calls=%async_computation | async-start | bytes 458752 | tf_op jit(solution)/shard_map/all_to_all | solution.py:402
  11.5 0.7 broadcast_in_dim.13.gain_ref
  12.3 0.0 copy-start.4
  12.3 1.1 copy-done.4
  13.3 0.6 shard_map.88
  13.9 0.3 collective-permute-start.9
  14.2 5.8 %all-to-all-done = bf16[32,2,1792]{2,1,0:T(2,128)(2,1)S(1)} async-done(((bf16[32,2,1792]{2,1,0:T(2,128)(2,1)}), bf16[32,2,1792]{2,1,0:T(2,128)(2,1)S(1)}, u32[]{:S(2)}, u32[]{:S(2)}) %all-to-all-start) | async-done | bytes 229408 | tf_op jit(solution)/shard_map/all_to_all | solution.py:402
  20.1 0.2 broadcast_select_fusion
  20.4 1.0 collective-permute-start.11
  21.4 0.6 collective-permute-start.10
  22.0 5.7 %collective-permute-start.4 = (bf16[64,1792]{1,0:T(8,128)(2,1)S(1)}, bf16[64,1792]{1,0:T(8,128)(2,1)S(1)}, u32[]{:S(2)}, u32[]{:S(2)}) collective-permute-start(bf16[64,1792]{1,0:T(8,128)(2,1)S(1)} %constant_dynamic-update-slice_fusion.refs_0_.refs_11_), channel_id=1, source_target_pairs={{0,14},{2,0},{4,2},{6,4},{8,6},{10,8},{12,10},{14,12},{1,15},{3,1}... | collective-permute-start | bytes 688136 | tf_op jit(solution)/shard_map/ppermute | solution.py:45
  27.6 0.0 collective-permute-start
  27.7 7.6 %collective-permute-done.11.b2 = bf16[128,2304]{1,0:T(8,128)(2,1)S(1)} collective-permute-done((bf16[128,2304]{1,0:T(8,128)(2,1)S(1)}, bf16[128,2304]{1,0:T(8,128)(2,1)S(1)}, u32[]{:S(2)}, u32[]{:S(2)}) %collective-permute-start.11) | collective-permute-done | bytes 589856 | tf_op jit(solution)/shard_map/ppermute | solution.py:45
  35.3 2.4 %collective-permute-start.13 = (bf16[64,2304]{1,0:T(8,128)(2,1)S(1)}, bf16[64,2304]{1,0:T(8,128)(2,1)S(1)}, u32[]{:S(2)}, u32[]{:S(2)}) collective-permute-start(bf16[64,2304]{1,0:T(8,128)(2,1)S(1)} %slice.31), channel_id=1, source_target_pairs={{0,192},{64,0},{128,64},{192,128},{1,193},{65,1},{129,65},{193,129... | collective-permute-start | bytes 884744 | tf_op jit(solution)/shard_map/ppermute | solution.py:49
  37.6 0.0 collective-permute-done.10.b1
  37.7 0.1 collective-permute-start.12
  37.8 0.0 collective-permute-done.4.refs_2_.refs_13_
  37.8 5.7 %collective-permute-start.5 = (bf16[64,1792]{1,0:T(8,128)(2,1)S(1)}, bf16[64,1792]{1,0:T(8,128)(2,1)S(1)}, u32[]{:S(2)}, u32[]{:S(2)}) collective-permute-start(bf16[64,1792]{1,0:T(8,128)(2,1)S(1)} %collective-permute-done.4.refs_2_.refs_13_), channel_id=1, source_target_pairs={{0,14},{2,0},{4,2},{6,4},{8,6},{10,8},{12,10},{14,12},{1,15},{3,1}... | collective-permute-start | bytes 688136 | tf_op jit(solution)/shard_map/ppermute | solution.py:45
  43.4 3.8 %collective-permute-done.5.refs_4_.refs_15_ = bf16[64,1792]{1,0:T(8,128)(2,1)S(1)} collective-permute-done((bf16[64,1792]{1,0:T(8,128)(2,1)S(1)}, bf16[64,1792]{1,0:T(8,128)(2,1)S(1)}, u32[]{:S(2)}, u32[]{:S(2)}) %collective-permute-start.5) | collective-permute-done | bytes 229408 | tf_op jit(solution)/shard_map/ppermute | solution.py:45
  47.2 3.4 %collective-permute-start.6 = (bf16[64,1792]{1,0:T(8,128)(2,1)S(1)}, bf16[64,1792]{1,0:T(8,128)(2,1)S(1)}, u32[]{:S(2)}, u32[]{:S(2)}) collective-permute-start(bf16[64,1792]{1,0:T(8,128)(2,1)S(1)} %collective-permute-done.5.refs_4_.refs_15_), channel_id=1, source_target_pairs={{0,14},{2,0},{4,2},{6,4},{8,6},{10,8},{12,10},{14,12},{1,15},{3,1}... | collective-permute-start | bytes 688136 | tf_op jit(solution)/shard_map/ppermute | solution.py:45
  50.7 0.0 collective-permute-done.1.refs_3_.refs_14_
  50.7 0.0 collective-permute-start.2
  50.7 6.7 %shard_map.89 = (f32[256,1024]{1,0:T(8,128)S(1)}, f32[256,1024]{1,0:T(8,128)}) custom-call(bf16[128,2304]{1,0:T(8,128)(2,1)S(1)} %constant_dynamic-update-slice_fusion.2.b0, bf16[128,2304]{1,0:T(8,128)(2,1)S(1)} %collective-permute-done.10.b1, bf16[128,2304]{1,0:T(8,128)(2,1)S(1)} %collective-permute-done.11.b2, ...), custom_call_target="tpu_custom_call" | custom-call | flops 2415919104 | bytes 6815744 | tf_op jit(solution)/shard_map/pallas_call | solution.py:158
  57.4 1.0 copy-done
  58.4 2.3 %collective-permute-start.14 = (f32[256,1024]{1,0:T(8,128)}, f32[256,1024]{1,0:T(8,128)S(1)}, u32[]{:S(2)}, u32[]{:S(2)}) collective-permute-start(f32[256,1024]{1,0:T(8,128)} %get-tuple-element.21), channel_id=1, source_target_pairs={{0,1},{1,0},{2,3},{3,2},{4,5},{5,4},{6,7},{7,6},{8,9},{9,8},{10,11... | collective-permute-start | bytes 3145736 | tf_op jit(solution)/shard_map/ppermute | solution.py:37
  60.7 0.0 collective-permute-done.6.refs_6_.refs_17_
  60.7 0.0 collective-permute-done.2.refs_5_.refs_16_
  60.7 4.4 %shard_map.90 = (f32[224,1024]{1,0:T(8,128)S(1)}, f32[224,1024]{1,0:T(8,128)S(1)}) custom-call(bf16[64,1792]{1,0:T(8,128)(2,1)S(1)} %constant_dynamic-update-slice_fusion.refs_0_.refs_11_, bf16[64,1792]{1,0:T(8,128)(2,1)S(1)} %collective-permute-done.refs_1_.refs_12_, bf16[64,1792]{1,0:T(8,128)(2,1)S(1)} %collective-permute-done.4.refs_2_.refs_13_, ...), custom_call_target="tpu_custom_call" | custom-call | flops 1644167168 | bytes 5505024 | tf_op jit(solution)/shard_map/pallas_call | solution.py:195
  65.1 0.1 collective-permute-start.15
  65.2 2.5 %collective-permute-done.15.got = f32[224,1024]{1,0:T(8,128)S(1)} collective-permute-done((f32[224,1024]{1,0:T(8,128)S(1)}, f32[224,1024]{1,0:T(8,128)S(1)}, u32[]{:S(2)}, u32[]{:S(2)}) %collective-permute-start.15) | collective-permute-done | bytes 917536 | tf_op jit(solution)/shard_map/ppermute | solution.py:37
  67.7 0.0 collective-permute-done.14.t_got
  67.7 1.0 copy-done.2
  68.6 2.8 %shard_map.91 = (bf16[224,1024]{1,0:T(8,128)(2,1)S(1)}, bf16[224,1024]{1,0:T(8,128)(2,1)S(1)}, f32[4,224,128]{2,1,0:T(8,128)S(1)}) custom-call(f32[224,1024]{1,0:T(8,128)S(1)} %get-tuple-element.22.own, f32[224,1024]{1,0:T(8,128)S(1)} %collective-permute-done.15.got, f32[256,1024]{1,0:T(8,128)} %copy-done, f32[256,1024]{1,0:T(8,128)} %copy-done.2, ...), custom_call_target="tpu_custom_call" | custom-call | flops 9175040 | bytes 4587520 | tf_op jit(solution)/shard_map/pallas_call | solution.py:259
  71.5 0.0 copy-start.3
  71.5 0.2 collective-permute-start.16
  71.7 0.4 collective-permute-start.18
  72.1 2.9 %collective-permute-start.7 = (bf16[32,1792]{1,0:T(8,128)(2,1)S(1)}, bf16[32,1792]{1,0:T(8,128)(2,1)S(1)}, u32[]{:S(2)}, u32[]{:S(2)}) collective-permute-start(bf16[32,1792]{1,0:T(8,128)(2,1)S(1)} %slice.29), channel_id=1, source_target_pairs={{0,14},{2,0},{4,2},{6,4},{8,6},{10,8},{12,10},{14,12},{1,15},{3,1}... | collective-permute-start | bytes 344072 | tf_op jit(solution)/shard_map/ppermute | solution.py:49
  75.0 0.1 collective-permute-start.3
  75.1 2.3 %collective-permute-done.7.refs_1_.refs_19_ = bf16[32,1792]{1,0:T(8,128)(2,1)S(1)} collective-permute-done((bf16[32,1792]{1,0:T(8,128)(2,1)S(1)}, bf16[32,1792]{1,0:T(8,128)(2,1)S(1)}, u32[]{:S(2)}, u32[]{:S(2)}) %collective-permute-start.7) | collective-permute-done | bytes 114720 | tf_op jit(solution)/shard_map/ppermute | solution.py:49
  77.4 3.2 %collective-permute-done.3.refs_0_.refs_18_ = bf16[32,1792]{1,0:T(8,128)(2,1)S(1)} collective-permute-done((bf16[32,1792]{1,0:T(8,128)(2,1)S(1)}, bf16[32,1792]{1,0:T(8,128)(2,1)S(1)}, u32[]{:S(2)}, u32[]{:S(2)}) %collective-permute-start.3) | collective-permute-done | bytes 114720 | tf_op jit(solution)/shard_map/ppermute | solution.py:48
  80.6 3.4 %shard_map.87 = (f32[32,1024]{1,0:T(8,128)S(1)}, f32[32,1024]{1,0:T(8,128)S(1)}) custom-call(bf16[32,1792]{1,0:T(8,128)(2,1)S(1)} %collective-permute-done.3.refs_0_.refs_18_, bf16[32,1792]{1,0:T(8,128)(2,1)S(1)} %collective-permute-done.7.refs_1_.refs_19_, bf16[1792,1024]{1,0:T(8,128)(2,1)} %refs_7_.1), custom_call_target="tpu_custom_call" | custom-call | flops 234881024 | bytes 3932160 | tf_op jit(solution)/shard_map/pallas_call | solution.py:195
  84.0 1.4 %collective-permute-start.8 = (f32[32,1024]{1,0:T(8,128)S(1)}, f32[32,1024]{1,0:T(8,128)S(1)}, u32[]{:S(2)}, u32[]{:S(2)}) collective-permute-start(f32[32,1024]{1,0:T(8,128)S(1)} %get-tuple-element.17), channel_id=1, source_target_pairs={{0,1},{1,0},{2,3},{3,2},{4,5},{5,4},{6,7},{7,6},{8,9},{9,8},{10,11... | collective-permute-start | bytes 393224 | tf_op jit(solution)/shard_map/ppermute | solution.py:37
  85.4 1.0 collective-permute-done.8.got
  86.4 0.4 shard_map.92
  86.8 11.1 %all_to_all.15 = f32[16,8,128]{2,1,0:T(8,128)S(1)} all-to-all(f32[16,8,128]{2,1,0:T(8,128)S(1)} %get-tuple-element.25), channel_id=1, replica_groups=mesh['y'=4,'x'=4,'z'=8,'c'=2] {'y','x'}, dimensions={0} | all-to-all | bytes 131072 | tf_op jit(solution)/shard_map/all_to_all | solution.py:422
  97.9 0.6 broadcast_in_dim.14
  98.5 5.1 %all-to-all-start.2 = ((f32[16,8,128]{2,1,0:T(8,128)}), f32[16,8,128]{2,1,0:T(8,128)S(1)}, u32[]{:S(2)}, u32[]{:S(2)}) async-start(f32[16,8,128]{2,1,0:T(8,128)} %broadcast_in_dim.14), calls=%async_computation.2 | async-start | bytes 131072 | tf_op jit(solution)/shard_map/all_to_all | solution.py:424
  103.6 0.3 collective-permute-start.17
  103.9 0.2 collective-permute-start.19
  104.1 0.3 collective-permute-start.20
  104.4 0.8 collective-permute-done.20.refs_10_
  105.3 0.0 collective-permute-done.17.refs_6_
  105.3 0.0 collective-permute-done.19.refs_8_
  105.3 0.6 copy-done.11
  105.9 5.6 %all-to-all-done.2.refs_0_ = f32[16,8,128]{2,1,0:T(8,128)S(1)} async-done(((f32[16,8,128]{2,1,0:T(8,128)}), f32[16,8,128]{2,1,0:T(8,128)S(1)}, u32[]{:S(2)}, u32[]{:S(2)}) %all-to-all-start.2) | async-done | bytes 65568 | tf_op jit(solution)/shard_map/all_to_all | solution.py:424
  111.4 0.0 collective-permute-done.18.refs_7_
  111.5 0.9 copy-done.8
  112.4 0.9 copy-done.10
  113.3 0.8 copy-done.12
  114.2 6.7 %shard_map.93 = (f32[1,2]{1,0:T(1,128)}, bf16[1792,1024]{1,0:T(8,128)(2,1)}) custom-call(f32[16,8,128]{2,1,0:T(8,128)S(1)} %all-to-all-done.2.refs_0_, bf16[224,1024]{1,0:T(8,128)(2,1)S(1)} %get-tuple-element.26.refs_1_, bf16[32,1024]{1,0:T(8,128)(2,1)S(1)} %get-tuple-element.27.refs_2_, bf16[224,1024]{1,0:T(8,128)(2,1)S(1)} %get-tuple-element.28.refs_3_, ...), custom_call_target="tpu_custom_call" | custom-call | flops 1879048192 | bytes 6815744 | tf_op jit(solution)/shard_map/pallas_call | solution.py:377
  (32 shorter events, 0.3 us)
Async XLA Ops:
  1.4 0.7 copy-start.5
  2.9 17.2 %all-to-all-start = ((bf16[32,2,1792]{2,1,0:T(2,128)(2,1)}), bf16[32,2,1792]{2,1,0:T(2,128)(2,1)S(1)}, u32[]{:S(2)}, u32[]{:S(2)}) async-start(bf16[32,2,1792]{2,1,0:T(2,128)(2,1)} %shard_map.86), calls=%async_computation | async-start | bytes 458752 | tf_op jit(solution)/shard_map/all_to_all | solution.py:402
  12.3 1.1 copy-start.4
  13.9 6.5 %collective-permute-start.9 = (bf16[64,2304]{1,0:T(8,128)(2,1)S(1)}, bf16[64,2304]{1,0:T(8,128)(2,1)S(1)}, u32[]{:S(2)}, u32[]{:S(2)}) collective-permute-start(bf16[64,2304]{1,0:T(8,128)(2,1)S(1)} %get-tuple-element.19), channel_id=1, source_target_pairs={{0,1},{1,0},{2,3},{3,2},{4,5},{5,4},{6,7},{7,6},{8,9},{9,8},{10,11... | collective-permute-start | bytes 884744 | tf_op jit(solution)/shard_map/ppermute | solution.py:37
  20.4 14.8 %collective-permute-start.11 = (bf16[128,2304]{1,0:T(8,128)(2,1)S(1)}, bf16[128,2304]{1,0:T(8,128)(2,1)S(1)}, u32[]{:S(2)}, u32[]{:S(2)}) collective-permute-start(bf16[128,2304]{1,0:T(8,128)(2,1)S(1)} %constant_dynamic-update-slice_fusion.2.b0), channel_id=1, source_target_pairs={{0,192},{64,0},{128,64},{192,128},{1,193},{65,1},{129,65},{193,129... | collective-permute-start | bytes 1769480 | tf_op jit(solution)/shard_map/ppermute | solution.py:45
  21.4 16.3 %collective-permute-start.10 = (bf16[128,2304]{1,0:T(8,128)(2,1)S(1)}, bf16[128,2304]{1,0:T(8,128)(2,1)S(1)}, u32[]{:S(2)}, u32[]{:S(2)}) collective-permute-start(bf16[128,2304]{1,0:T(8,128)(2,1)S(1)} %constant_dynamic-update-slice_fusion.2.b0), channel_id=1, source_target_pairs={{0,64},{64,128},{128,192},{192,0},{1,65},{65,129},{129,193},{193,1... | collective-permute-start | bytes 1769480 | tf_op jit(solution)/shard_map/ppermute | solution.py:44
  22.0 15.8 %collective-permute-start.4 = (bf16[64,1792]{1,0:T(8,128)(2,1)S(1)}, bf16[64,1792]{1,0:T(8,128)(2,1)S(1)}, u32[]{:S(2)}, u32[]{:S(2)}) collective-permute-start(bf16[64,1792]{1,0:T(8,128)(2,1)S(1)} %constant_dynamic-update-slice_fusion.refs_0_.refs_11_), channel_id=1, source_target_pairs={{0,14},{2,0},{4,2},{6,4},{8,6},{10,8},{12,10},{14,12},{1,15},{3,1}... | collective-permute-start | bytes 688136 | tf_op jit(solution)/shard_map/ppermute | solution.py:45
  27.6 15.8 %collective-permute-start = (bf16[64,1792]{1,0:T(8,128)(2,1)S(1)}, bf16[64,1792]{1,0:T(8,128)(2,1)S(1)}, u32[]{:S(2)}, u32[]{:S(2)}) collective-permute-start(bf16[64,1792]{1,0:T(8,128)(2,1)S(1)} %constant_dynamic-update-slice_fusion.refs_0_.refs_11_), channel_id=1, source_target_pairs={{0,2},{2,4},{4,6},{6,8},{8,10},{10,12},{12,14},{14,0},{1,3},{3,5},... | collective-permute-start | bytes 688136 | tf_op jit(solution)/shard_map/ppermute | solution.py:44
  35.3 15.4 %collective-permute-start.13 = (bf16[64,2304]{1,0:T(8,128)(2,1)S(1)}, bf16[64,2304]{1,0:T(8,128)(2,1)S(1)}, u32[]{:S(2)}, u32[]{:S(2)}) collective-permute-start(bf16[64,2304]{1,0:T(8,128)(2,1)S(1)} %slice.31), channel_id=1, source_target_pairs={{0,192},{64,0},{128,64},{192,128},{1,193},{65,1},{129,65},{193,129... | collective-permute-start | bytes 884744 | tf_op jit(solution)/shard_map/ppermute | solution.py:49
  37.7 13.0 %collective-permute-start.12 = (bf16[64,2304]{1,0:T(8,128)(2,1)S(1)}, bf16[64,2304]{1,0:T(8,128)(2,1)S(1)}, u32[]{:S(2)}, u32[]{:S(2)}) collective-permute-start(bf16[64,2304]{1,0:T(8,128)(2,1)S(1)} %slice.30), channel_id=1, source_target_pairs={{0,64},{64,128},{128,192},{192,0},{1,65},{65,129},{129,193},{193,1... | collective-permute-start | bytes 884744 | tf_op jit(solution)/shard_map/ppermute | solution.py:48
  37.8 9.5 %collective-permute-start.5 = (bf16[64,1792]{1,0:T(8,128)(2,1)S(1)}, bf16[64,1792]{1,0:T(8,128)(2,1)S(1)}, u32[]{:S(2)}, u32[]{:S(2)}) collective-permute-start(bf16[64,1792]{1,0:T(8,128)(2,1)S(1)} %collective-permute-done.4.refs_2_.refs_13_), channel_id=1, source_target_pairs={{0,14},{2,0},{4,2},{6,4},{8,6},{10,8},{12,10},{14,12},{1,15},{3,1}... | collective-permute-start | bytes 688136 | tf_op jit(solution)/shard_map/ppermute | solution.py:45
  43.4 7.2 %collective-permute-start.1 = (bf16[64,1792]{1,0:T(8,128)(2,1)S(1)}, bf16[64,1792]{1,0:T(8,128)(2,1)S(1)}, u32[]{:S(2)}, u32[]{:S(2)}) collective-permute-start(bf16[64,1792]{1,0:T(8,128)(2,1)S(1)} %collective-permute-done.refs_1_.refs_12_), channel_id=1, source_target_pairs={{0,2},{2,4},{4,6},{6,8},{8,10},{10,12},{12,14},{14,0},{1,3},{3,5},... | collective-permute-start | bytes 688136 | tf_op jit(solution)/shard_map/ppermute | solution.py:44
  47.2 13.5 %copy-start.7 = (bf16[64,1792]{1,0:T(8,128)(2,1)}, bf16[64,1792]{1,0:T(8,128)(2,1)S(1)}, u32[]{:S(2)}) copy-start(bf16[64,1792]{1,0:T(8,128)(2,1)S(1)} %collective-permute-done.5.refs_4_.refs_15_) | copy-start | bytes 688132
  47.2 13.4 %collective-permute-start.6 = (bf16[64,1792]{1,0:T(8,128)(2,1)S(1)}, bf16[64,1792]{1,0:T(8,128)(2,1)S(1)}, u32[]{:S(2)}, u32[]{:S(2)}) collective-permute-start(bf16[64,1792]{1,0:T(8,128)(2,1)S(1)} %collective-permute-done.5.refs_4_.refs_15_), channel_id=1, source_target_pairs={{0,14},{2,0},{4,2},{6,4},{8,6},{10,8},{12,10},{14,12},{1,15},{3,1}... | collective-permute-start | bytes 688136 | tf_op jit(solution)/shard_map/ppermute | solution.py:45
  50.7 10.0 %copy-start.9 = (bf16[64,1792]{1,0:T(8,128)(2,1)}, bf16[64,1792]{1,0:T(8,128)(2,1)S(1)}, u32[]{:S(2)}) copy-start(bf16[64,1792]{1,0:T(8,128)(2,1)S(1)} %collective-permute-done.1.refs_3_.refs_14_) | copy-start | bytes 688132
  50.7 10.0 %collective-permute-start.2 = (bf16[64,1792]{1,0:T(8,128)(2,1)S(1)}, bf16[64,1792]{1,0:T(8,128)(2,1)S(1)}, u32[]{:S(2)}, u32[]{:S(2)}) collective-permute-start(bf16[64,1792]{1,0:T(8,128)(2,1)S(1)} %collective-permute-done.1.refs_3_.refs_14_), channel_id=1, source_target_pairs={{0,2},{2,4},{4,6},{6,8},{8,10},{10,12},{12,14},{14,0},{1,3},{3,5},... | collective-permute-start | bytes 688136 | tf_op jit(solution)/shard_map/ppermute | solution.py:44
  57.4 1.0 copy-start
  58.4 10.2 %copy-start.6 = (s32[1,256]{1,0:T(1,128)S(1)}, s32[1,256]{1,0:T(1,128)}, u32[]{:S(2)}) copy-start(s32[1,256]{1,0:T(1,128)} %refs_9_.1) | copy-start | bytes 3076
  58.4 9.3 %collective-permute-start.14 = (f32[256,1024]{1,0:T(8,128)}, f32[256,1024]{1,0:T(8,128)S(1)}, u32[]{:S(2)}, u32[]{:S(2)}) collective-permute-start(f32[256,1024]{1,0:T(8,128)} %get-tuple-element.21), channel_id=1, source_target_pairs={{0,1},{1,0},{2,3},{3,2},{4,5},{5,4},{6,7},{7,6},{8,9},{9,8},{10,11... | collective-permute-start | bytes 3145736 | tf_op jit(solution)/shard_map/ppermute | solution.py:37
  65.1 2.6 %collective-permute-start.15 = (f32[224,1024]{1,0:T(8,128)S(1)}, f32[224,1024]{1,0:T(8,128)S(1)}, u32[]{:S(2)}, u32[]{:S(2)}) collective-permute-start(f32[224,1024]{1,0:T(8,128)S(1)} %get-tuple-element.23), channel_id=1, source_target_pairs={{0,1},{1,0},{2,3},{3,2},{4,5},{5,4},{6,7},{7,6},{8,9},{9,8},{10,11... | collective-permute-start | bytes 2752520 | tf_op jit(solution)/shard_map/ppermute | solution.py:37
  67.7 1.0 copy-start.2
  68.6 17.7 %copy-start.1 = (f32[256,1024]{1,0:T(8,128)S(1)}, f32[256,1024]{1,0:T(8,128)}, u32[]{:S(2)}) copy-start(f32[256,1024]{1,0:T(8,128)} %copy-done) | copy-start | bytes 3145732
  71.5 14.9 %copy-start.3 = (f32[256,1024]{1,0:T(8,128)S(1)}, f32[256,1024]{1,0:T(8,128)}, u32[]{:S(2)}) copy-start(f32[256,1024]{1,0:T(8,128)} %copy-done.2) | copy-start | bytes 3145732
  71.5 40.0 %collective-permute-start.16 = (bf16[224,1024]{1,0:T(8,128)(2,1)S(1)}, bf16[224,1024]{1,0:T(8,128)(2,1)S(1)}, u32[]{:S(2)}, u32[]{:S(2)}) collective-permute-start(bf16[224,1024]{1,0:T(8,128)(2,1)S(1)} %get-tuple-element.26.refs_1_), channel_id=1, source_target_pairs={{0,1},{1,0},{2,3},{3,2},{4,5},{5,4},{6,7},{7,6},{8,9},{9,8},{10,11... | collective-permute-start | bytes 1376264 | tf_op jit(solution)/shard_map/ppermute | solution.py:37
  71.7 39.8 %collective-permute-start.18 = (bf16[224,1024]{1,0:T(8,128)(2,1)S(1)}, bf16[224,1024]{1,0:T(8,128)(2,1)S(1)}, u32[]{:S(2)}, u32[]{:S(2)}) collective-permute-start(bf16[224,1024]{1,0:T(8,128)(2,1)S(1)} %get-tuple-element.28.refs_3_), channel_id=1, source_target_pairs={{0,1},{1,0},{2,3},{3,2},{4,5},{5,4},{6,7},{7,6},{8,9},{9,8},{10,11... | collective-permute-start | bytes 1376264 | tf_op jit(solution)/shard_map/ppermute | solution.py:37
  72.1 5.4 %collective-permute-start.7 = (bf16[32,1792]{1,0:T(8,128)(2,1)S(1)}, bf16[32,1792]{1,0:T(8,128)(2,1)S(1)}, u32[]{:S(2)}, u32[]{:S(2)}) collective-permute-start(bf16[32,1792]{1,0:T(8,128)(2,1)S(1)} %slice.29), channel_id=1, source_target_pairs={{0,14},{2,0},{4,2},{6,4},{8,6},{10,8},{12,10},{14,12},{1,15},{3,1}... | collective-permute-start | bytes 344072 | tf_op jit(solution)/shard_map/ppermute | solution.py:49
  75.0 5.6 %collective-permute-start.3 = (bf16[32,1792]{1,0:T(8,128)(2,1)S(1)}, bf16[32,1792]{1,0:T(8,128)(2,1)S(1)}, u32[]{:S(2)}, u32[]{:S(2)}) collective-permute-start(bf16[32,1792]{1,0:T(8,128)(2,1)S(1)} %slice.28), channel_id=1, source_target_pairs={{0,2},{2,4},{4,6},{6,8},{8,10},{10,12},{12,14},{14,0},{1,3},{3,5},... | collective-permute-start | bytes 344072 | tf_op jit(solution)/shard_map/ppermute | solution.py:48
  84.0 2.3 %collective-permute-start.8 = (f32[32,1024]{1,0:T(8,128)S(1)}, f32[32,1024]{1,0:T(8,128)S(1)}, u32[]{:S(2)}, u32[]{:S(2)}) collective-permute-start(f32[32,1024]{1,0:T(8,128)S(1)} %get-tuple-element.17), channel_id=1, source_target_pairs={{0,1},{1,0},{2,3},{3,2},{4,5},{5,4},{6,7},{7,6},{8,9},{9,8},{10,11... | collective-permute-start | bytes 393224 | tf_op jit(solution)/shard_map/ppermute | solution.py:37
  98.5 12.9 %all-to-all-start.2 = ((f32[16,8,128]{2,1,0:T(8,128)}), f32[16,8,128]{2,1,0:T(8,128)S(1)}, u32[]{:S(2)}, u32[]{:S(2)}) async-start(f32[16,8,128]{2,1,0:T(8,128)} %broadcast_in_dim.14), calls=%async_computation.2 | async-start | bytes 131072 | tf_op jit(solution)/shard_map/all_to_all | solution.py:424
  103.6 1.7 %collective-permute-start.17 = (bf16[32,1024]{1,0:T(8,128)(2,1)S(1)}, bf16[32,1024]{1,0:T(8,128)(2,1)S(1)}, u32[]{:S(2)}, u32[]{:S(2)}) collective-permute-start(bf16[32,1024]{1,0:T(8,128)(2,1)S(1)} %get-tuple-element.27.refs_2_), channel_id=1, source_target_pairs={{0,1},{1,0},{2,3},{3,2},{4,5},{5,4},{6,7},{7,6},{8,9},{9,8},{10,11... | collective-permute-start | bytes 196616 | tf_op jit(solution)/shard_map/ppermute | solution.py:37
  103.9 1.4 %collective-permute-start.19 = (bf16[32,1024]{1,0:T(8,128)(2,1)S(1)}, bf16[32,1024]{1,0:T(8,128)(2,1)S(1)}, u32[]{:S(2)}, u32[]{:S(2)}) collective-permute-start(bf16[32,1024]{1,0:T(8,128)(2,1)S(1)} %get-tuple-element.29.refs_4_), channel_id=1, source_target_pairs={{0,1},{1,0},{2,3},{3,2},{4,5},{5,4},{6,7},{7,6},{8,9},{9,8},{10,11... | collective-permute-start | bytes 196616 | tf_op jit(solution)/shard_map/ppermute | solution.py:37
  104.1 1.1 collective-permute-start.20
  105.3 0.6 copy-start.11
  111.5 0.9 copy-start.8
  112.4 0.9 copy-start.10
  113.3 0.8 copy-start.12

commit v3 on v0

v3 whole, which is shorter than its diff:
```python
import jax
import jax.numpy as jnp
from jax import lax
from jax.experimental import pallas as pl
from jax.experimental.pallas import tpu as pltpu
from jax.sharding import Mesh, PartitionSpec as P

F32 = jnp.float32
BF16 = jnp.bfloat16
I32 = jnp.int32
NY, NX, NZ = 4, 4, 8
ROWS = 2
PLANE = NY * NX * ROWS
OWN = NZ * PLANE
EARLY = OWN - PLANE
STEP = 32
TILE = 256
LANES = 128
VMEM = pl.BlockSpec(memory_space=pltpu.VMEM)
SHORT = pl.CostEstimate(flops=1024, bytes_accessed=1024, transcendentals=0)


def params():
    return pltpu.CompilerParams(vmem_limit_bytes=12 * 1024 * 1024)


def struct(shape, dtype):
    return jax.ShapeDtypeStruct(shape, dtype)


def call(body, out_shape, operands, scratch=()):
    several = isinstance(out_shape, tuple)
    return pl.pallas_call(
        body,
        out_shape=out_shape,
        in_specs=[VMEM] * len(operands),
        out_specs=(VMEM,) * len(out_shape) if several else VMEM,
        scratch_shapes=scratch,
        compiler_params=params(),
        cost_estimate=SHORT,
    )(*operands)


def up(n, k):
    return [(i, (i + k) % n) for i in range(n)]


def swap_cores(value):
    return lax.ppermute(value, "c", [(0, 1), (1, 0)])


def ring(block, axis, n):
    blocks = [block]
    from_low = from_high = block
    for _ in range(n // 2 - 1):
        from_low = lax.ppermute(from_low, axis, up(n, 1))
        from_high = lax.ppermute(from_high, axis, up(n, -1))
        blocks += [from_low, from_high]
    half = block.shape[0] // 2
    blocks.append(lax.ppermute(from_low[:half], axis, up(n, 1)))
    blocks.append(lax.ppermute(from_high[half:], axis, up(n, -1)))
    return blocks


def distance(position):
    return jnp.where(position % 2 == 1, NZ - (position + 1) // 2, position // 2)


def natural_row(row, z):
    position, inner = row // PLANE, row % PLANE
    y, x, i = inner // (NX * ROWS), inner // ROWS % NX, inner % ROWS
    return ((y * NX + x) * NZ + (z + distance(position)) % NZ) * ROWS + i


def iota(shape, axis):
    return lax.broadcasted_iota(I32, shape, axis)


def normalize(hidden, gain):
    values = hidden.astype(F32)
    spread = jnp.mean(values * values, axis=-1, keepdims=True)
    return (values * lax.rsqrt(spread + 1e-06) * gain.reshape(1, -1)).astype(BF16)


def student_norm_kernel(hidden_ref, gain_ref, out_ref):
    normed = normalize(hidden_ref[...], gain_ref[...])
    for peer in range(NY * NX):
        out_ref[peer] = normed


def student_norm(hidden, gain):
    return call(student_norm_kernel, struct((NY * NX, *hidden.shape), BF16), (hidden, gain))


def teacher_norm_kernel(hidden_ref, gain_ref, _, out_ref):
    z = lax.axis_index("z")
    normed = normalize(hidden_ref[...], gain_ref[...])
    n = normed.shape[0]
    row = iota((n, n), 0)
    position, x, i = row // (NX * ROWS), row // ROWS % NX, row % ROWS
    source = (x * NZ + (z + distance(position)) % NZ) * ROWS + i
    moved = jnp.where(iota((n, n), 1) == source, 1.0, 0.0).astype(BF16)
    out_ref[...] = jnp.dot(moved, normed, preferred_element_type=F32).astype(BF16)


def teacher_norm(hidden, gain, sent):
    return call(teacher_norm_kernel, struct(hidden.shape, BF16), (hidden, gain, sent))


def halves(ref_width):
    k, core = ref_width // 2, lax.axis_index("c")
    return tuple(pl.ds(pl.multiple_of(half * k, LANES), k) for half in (core, 1 - core))


def product(rows_ref, own_w_ref, other_w_ref, columns):
    own, other = halves(rows_ref.shape[1])
    return jnp.dot(
        rows_ref[:, own], own_w_ref[:, columns], preferred_element_type=F32
    ) + jnp.dot(rows_ref[:, other], other_w_ref[:, columns], preferred_element_type=F32)


def soft_cap(logits):
    return (30.0 * jnp.tanh(logits / 30.0)).astype(BF16)


def teacher_logits_kernel(b0, b1, b2, b3, b4, own_w_ref, other_w_ref, out_ref, rows_ref):
    section = b0.shape[0]
    y = lax.axis_index("y")
    row = iota((OWN, OWN), 0)
    position, inner = row // PLANE, row % PLANE
    apart = (inner // (NX * ROWS) - y) % NY
    place = jnp.where(apart == 0, 0, jnp.where(apart == NY - 1, 1, jnp.where(apart == 1, 2, 3)))
    source = place * section + position * (NX * ROWS) + inner % (NX * ROWS)
    moved = jnp.where(iota((OWN, OWN), 1) == source, 1.0, 0.0).astype(BF16)
    whole = jnp.concatenate([b0[...], b1[...], b2[...], b3[...], b4[...]])
    rows_ref[...] = jnp.dot(moved, whole, preferred_element_type=F32).astype(BF16)
    for at in range(0, out_ref.shape[1], TILE):
        columns = pl.ds(at, TILE)
        out_ref[:, columns] = soft_cap(product(rows_ref, own_w_ref, other_w_ref, columns))


def teacher_logits(blocks, own_head, other_head):
    k, vocab = own_head.shape
    out = struct((OWN, vocab), BF16)
    scratch = [pltpu.VMEM((OWN, 2 * k), BF16)]
    return call(teacher_logits_kernel, out, (*blocks, own_head, other_head), scratch)


def local_targets(targets_ref, z, first, rows):
    shape = (rows.shape[0], OWN)
    here = iota(shape, 1) == natural_row(rows, z)
    return jnp.sum(jnp.where(here, targets_ref[...], 0), axis=1, keepdims=True) - first


def first_column(vocab):
    y, x, z = lax.axis_index("y"), lax.axis_index("x"), lax.axis_index("z")
    return ((y * NX + x) * NZ + z) * vocab


def fold(values):
    total = values[:, :LANES]
    for start in range(LANES, values.shape[1], LANES):
        total = total + values[:, start : start + LANES]
    return total


def student_part(start, rows_ref, own_w_ref, other_w_ref, teacher_ref, targets_ref, capped_ref, write):
    n, vocab = capped_ref.shape
    for at in range(0, vocab, TILE):
        columns = pl.ds(at, TILE)
        capped_ref[:, columns] = soft_cap(product(rows_ref, own_w_ref, other_w_ref, columns))
    z, first = lax.axis_index("z"), first_column(vocab)
    for at in range(0, n, STEP):
        stud_vals = capped_ref[pl.ds(at, STEP)].astype(F32)
        teach_vals = teacher_ref[pl.ds(start + at, STEP)].astype(F32)
        stud_exp, teach_exp = jnp.exp(stud_vals), jnp.exp(teach_vals)
        target = local_targets(targets_ref, z, first, iota((STEP, 1), 0) + (start + at))
        hit = iota((STEP, vocab), 1) == target
        write(0, at, fold(teach_exp))
        write(1, at, fold(stud_exp))
        write(2, at, fold(teach_exp * (teach_vals - stud_vals)))
        write(3, at, fold(jnp.where(hit, stud_vals, 0.0)))


def early_kernel(*refs):
    *blocks, own_w_ref, other_w_ref, teacher_ref, targets_ref, capped_ref, sums_ref, rows_ref = refs

    def write(kind, at, value):
        sums_ref[kind, pl.ds(at, STEP)] = value

    for q, block in enumerate(blocks):
        rows_ref[pl.ds(q * PLANE, PLANE)] = block[...]
    student_part(0, rows_ref, own_w_ref, other_w_ref, teacher_ref, targets_ref, capped_ref, write)


def early_rows(planes, own_head, other_head, teacher, targets):
    k, vocab = own_head.shape
    out = (struct((EARLY, vocab), BF16), struct((4, EARLY, LANES), F32))
    scratch = [pltpu.VMEM((EARLY, 2 * k), BF16)]
    return call(early_kernel, out, (*planes, own_head, other_head, teacher, targets), scratch)


def last_kernel(
    low, high, own_w_ref, other_w_ref, teacher_ref, targets_ref, early_ref,
    capped_ref, out_ref, rows_ref, sums_ref,
):
    def write(kind, at, value):
        sums_ref[kind, pl.ds(EARLY + at, STEP)] = value

    rows_ref[...] = jnp.concatenate([low[...], high[...]])
    sums_ref[:, :EARLY] = early_ref[...]
    student_part(EARLY, rows_ref, own_w_ref, other_w_ref, teacher_ref, targets_ref, capped_ref, write)
    z = lax.axis_index("z")
    here = iota((OWN, OWN), 1) == natural_row(iota((OWN, OWN), 0), z)
    rows = []
    for kind in range(4):
        total = jnp.sum(sums_ref[kind], axis=1, keepdims=True)
        flat = jnp.sum(jnp.where(here, total, 0.0), axis=0, keepdims=True)
        rows += [flat[:, at : at + LANES] for at in range(0, OWN, LANES)]
    tile = jnp.concatenate(rows, axis=0)
    for peer in range(out_ref.shape[0]):
        out_ref[peer] = tile


def last_rows(low, high, own_head, other_head, teacher, targets, early):
    k, vocab = own_head.shape
    out = (struct((PLANE, vocab), BF16), struct((NY * NX, 8, LANES), F32))
    scratch = [pltpu.VMEM((PLANE, 2 * k), BF16), pltpu.VMEM((4, OWN, LANES), F32)]
    operands = (low, high, own_head, other_head, teacher, targets, early)
    return call(last_kernel, out, operands, scratch)


def spread_kernel(sums_ref, out_ref):
    total = sums_ref[0]
    for peer in range(1, sums_ref.shape[0]):
        total = total + sums_ref[peer]
    for peer in range(out_ref.shape[0]):
        out_ref[peer] = total


def spread(sums):
    return call(spread_kernel, struct((2 * NZ, 8, LANES), F32), (sums,))


def collect_kernel(early_ref, last_ref, teacher_ref, _, out_ref):
    out_ref[:EARLY] = early_ref[...]
    out_ref[EARLY:OWN] = last_ref[...]
    out_ref[OWN:] = teacher_ref[...]


def collect(early, last, teacher, sums):
    out = struct((2 * OWN, teacher.shape[1]), BF16)
    return call(collect_kernel, out, (early, last, teacher, sums))


def transpose_kernel(*refs):
    *blocks, low, high, _, keep_ref, send_ref, rows_ref = refs
    for q, block in enumerate(blocks):
        rows_ref[pl.ds(q * PLANE, PLANE)] = block[...]
    rows_ref[EARLY:] = jnp.concatenate([low[...], high[...]])
    k, core = keep_ref.shape[0], lax.axis_index("c")
    for ref, half in ((keep_ref, core), (send_ref, 1 - core)):
        for at in range(0, k, TILE):
            columns = pl.ds(pl.multiple_of(half * k + at, LANES), TILE)
            ref[pl.ds(at, TILE)] = rows_ref[:, columns].T


def transposed(blocks, sums):
    width = blocks[0].shape[1]
    out = struct((width // 2, OWN), BF16)
    scratch = [pltpu.VMEM((OWN, width), BF16)]
    return call(transpose_kernel, (out, out), (*blocks, sums), scratch)


def gradient_kernel(
    sums_ref, own_ref, other_ref, targets_ref, oth_targets_ref, own_rows, other_rows,
    loss_ref, out_ref, grad_ref,
):
    vocab = out_ref.shape[1]

    @pl.when(pl.program_id(0) == 0)
    def _():
        z, core = lax.axis_index("z"), lax.axis_index("c")
        first = first_column(vocab)
        position = (lax.axis_index("y") * NX + lax.axis_index("x")) * NZ + z
        here = iota((OWN, OWN), 1) == natural_row(iota((OWN, OWN), 0), z)
        totals = []
        for side in range(2):
            total = sums_ref[side]
            for peer in range(1, NZ):
                total = total + sums_ref[2 * peer + side]
            totals.append(total)
        own = jnp.where(core == 0, totals[0], totals[1])
        other = jnp.where(core == 0, totals[1], totals[0])

        def flat(tile, kind):
            return jnp.concatenate([tile[2 * kind : 2 * kind + 1], tile[2 * kind + 1 : 2 * kind + 2]], axis=1)

        teach_total, stud_total, cross_sum, target_logit = (flat(own, k) for k in range(4))
        loss = cross_sum / teach_total - jnp.log(teach_total) + 2.0 * jnp.log(stud_total) - target_logit
        lane = iota((1, OWN), 1)
        picked = [
            jnp.sum(jnp.where(lane == position * ROWS + i, loss, 0.0), axis=1, keepdims=True)
            for i in range(ROWS)
        ]
        loss_ref[...] = jnp.concatenate(picked, axis=1)

        for side, tile, values, targets in (
            (0, own, own_ref, targets_ref),
            (1, other, other_ref, oth_targets_ref),
        ):
            teach_scale = jnp.sum(jnp.where(here, 1.0 / flat(tile, 0), 0.0), axis=1, keepdims=True)
            stud_scale = jnp.sum(jnp.where(here, 2.0 / flat(tile, 1), 0.0), axis=1, keepdims=True)
            target = local_targets(targets, z, first, iota((OWN, 1), 0))
            for at in range(0, OWN, STEP):
                stud_vals = values[pl.ds(at, STEP)].astype(F32)
                teach_vals = values[pl.ds(OWN + at, STEP)].astype(F32)
                rows = slice(at, at + STEP)
                scaled = jnp.exp(stud_vals) * stud_scale[rows] - jnp.exp(teach_vals) * teach_scale[rows]
                hit = iota((STEP, vocab), 1) == target[rows]
                scaled = scaled - jnp.where(hit, 1.0, 0.0)
                value = scaled * (1.0 - stud_vals * stud_vals * (1.0 / 900.0))
                grad_ref[pl.ds(side * OWN + at, STEP)] = value.astype(BF16)

    tile = out_ref.shape[0]
    part = pl.ds(pl.multiple_of(pl.program_id(0) * tile, tile), tile)
    out_ref[...] = (
        jnp.dot(own_rows[part], grad_ref[:OWN], preferred_element_type=F32)
        + jnp.dot(other_rows[part], grad_ref[OWN:], preferred_element_type=F32)
    ).astype(BF16)


def gradient(sums, own, other, targets, oth_targets, own_rows, other_rows):
    k, vocab = own_rows.shape[0], own.shape[1]
    operands = [sums, own, other, targets, oth_targets, own_rows, other_rows]
    return pl.pallas_call(
        gradient_kernel,
        grid=(k // TILE,),
        out_shape=(struct((1, ROWS), F32), struct((k, vocab), BF16)),
        in_specs=[VMEM] * len(operands),
        out_specs=(
            pl.BlockSpec((1, ROWS), lambda j: (0, 0)),
            pl.BlockSpec((TILE, vocab), lambda j: (j, 0)),
        ),
        scratch_shapes=[pltpu.VMEM((2 * OWN, vocab), BF16)],
        compiler_params=params(),
        cost_estimate=SHORT,
    )(*operands)


def shards(
    student_hidden, teacher_hidden, student_gain, teacher_gain, student_head, teacher_head, targets
):
    sent = student_norm(student_hidden[0], student_gain)
    got = lax.all_to_all(sent, ("y", "x"), 0, 0, tiled=True)
    planes = ring(got.reshape(PLANE, got.shape[2]), "z", NZ)

    sections = ring(teacher_norm(teacher_hidden[0], teacher_gain, sent), "y", NY)

    other_teacher_head = swap_cores(teacher_head)
    other_student_head = swap_cores(student_head)
    oth_targets = swap_cores(targets)

    teacher = teacher_logits(sections, teacher_head, other_teacher_head)
    capped, early = early_rows(
        planes[: NZ - 1], student_head, other_student_head, teacher, targets
    )
    low, high = planes[NZ - 1 :]
    capped_last, sums = last_rows(
        low, high, student_head, other_student_head, teacher, targets, early
    )

    own = collect(capped, capped_last, teacher, sums)
    other = swap_cores(own)
    own_rows, sent_rows = transposed(planes, sums)
    other_rows = swap_cores(sent_rows)
    sums = lax.all_to_all(sums, ("y", "x"), 0, 0, tiled=True)
    sums = lax.all_to_all(spread(sums), ("z", "c"), 0, 0, tiled=True)
    return gradient(sums, own, other, targets, oth_targets, own_rows, other_rows)


def solution(mesh):
    cube = mesh.devices.reshape(NY, NX, NZ, 2)
    grid = Mesh(cube, ("y", "x", "z", "c"))
    group = ("y", "x", "z")
    placed = (
        P("c", group, None),
        P("c", "y", None),
        P(),
        P(),
        P("c", group),
        P("c", group),
        P("c", None),
    )
    return jax.shard_map(
        shards,
        mesh=grid,
        in_specs=placed,
        out_specs=(P("c", group), P("c", group)),
        check_vma=False,
    )
```

time: 343 us -> 110 us (0.32)
  waiting for transfers between devices: 235 us -> 23.6 us
  Pallas kernels: 0 us -> 24.4 us
  matrix products: 19.6 us -> 0 us
  other arithmetic: 14.8 us -> 0 us
  between operations: 13.9 us -> 0.82 us
  starting transfers between devices: 27.5 us -> 32.8 us
    all_gather x4 -> x0, waiting for transfers between devices: 190 us -> none  [the longest x1 112 us: shards(): lax.all_gather(rms_norm(student_hidden[0], student_gain), ('section', 'vo...]
    ppermute x0 -> x17, starting transfers between devices: none -> 25.3 us  [the longest x4 11.2 us: ring(): from_high = lax.ppermute(from_high, axis, up(n, -1))]
    reduce_scatter x1 -> x0, waiting for transfers between devices: 24.6 us -> none  [shards(): lax.psum_scatter(contract_rows(normed_student, row_grad), 'dp', scatter_d...]
    pallas_call x0 -> x9, Pallas kernels: none -> 24.4 us  [the longest x8 16.7 us: call(): pl.pallas_call(body, out_shape=out_shape, in_specs=[VMEM] * len(operands)...]
    dot_general x3 -> x0, matrix products: 19.6 us -> none  [the longest x2 12.3 us: add_columns(): return jnp.dot(hidden, portion, preferred_element_type=jnp.float32)]
    all_to_all x2 -> x1, starting transfers between devices: 27.1 us -> 7.5 us  [shards(): sums = lax.all_to_all(spread(sums), ('z', 'c'), 0, 0, tiled=True)]
    ppermute x0 -> x17, waiting for transfers between devices: none -> 17 us  [the longest x4 9.64 us: ring(): from_high = lax.ppermute(from_high, axis, up(n, -1))]
    all_to_all x2 -> x1, waiting for transfers between devices: 19.1 us -> 6.67 us  [shards(): sums = lax.all_to_all(spread(sums), ('z', 'c'), 0, 0, tiled=True)]
  transfers between devices with their start and end apart: 7 -> 18, of which waited for: 6 -> 7; matrix products, arithmetic and copies ran while one was open for 5% -> 0% of each run, Pallas kernels for 0% -> 12%
where the time goes in v3:
time: 110 us; the launch traced here: 109 us
  starting transfers between devices  32.8 us (30%)
  Pallas kernels  24.4 us (22%)
  waiting for transfers between devices  23.6 us (21%)
  blocking collectives  22.1 us (20%)
  local copies, waits for them, and re-layouts  5.71 us (5%)
    pallas_call x8, Pallas kernels, call(): pl.pallas_call(body, out_shape=out_shape, in_specs=[VMEM] * len(operands)...  16.7 us
    all_to_all x1, blocking collectives, shards(): got = lax.all_to_all(sent, ('y', 'x'), 0, 0, tiled=True)  12.5 us
    ppermute x4, starting transfers between devices, ring(): from_high = lax.ppermute(from_high, axis, up(n, -1))  11.2 us
    ppermute x4, waiting for transfers between devices, ring(): from_high = lax.ppermute(from_high, axis, up(n, -1))  9.64 us
    all_to_all x1, blocking collectives, shards(): sums = lax.all_to_all(sums, ('y', 'x'), 0, 0, tiled=True)  9.53 us
    ppermute x5, starting transfers between devices, swap_cores(): return lax.ppermute(value, 'c', [(0, 1), (1, 0)])  8.49 us
    pallas_call x1, Pallas kernels, gradient(): pl.pallas_call(gradient_kernel, grid=(k // TILE,), out_shape=(struct((1,...  7.7 us
    all_to_all x1, starting transfers between devices, shards(): sums = lax.all_to_all(spread(sums), ('z', 'c'), 0, 0, tiled=True)  7.5 us
  transfers between devices with their start and end apart: 18, of which 7 were waited for; matrix products, arithmetic and copies ran while one was open for 0% of the time, Pallas kernels for 12%

profile of v3, /device:TPU:1, one launch (start us, length us, event | category | flops | bytes accessed | tf_op | source)
XLA Modules:
  0.0 109.5 jit_solution(5098907354265664241)
XLA Ops:
  0.6 3.3 %collective-permute-start.13 = (bf16[2304,1024]{1,0:T(8,128)(2,1)}, bf16[2304,1024]{1,0:T(8,128)(2,1)}, u32[]{:S(2)}, u32[]{:S(2)}) collective-permute-start(bf16[2304,1024]{1,0:T(8,128)(2,1)} %own_w_ref.2), channel_id=1, source_target_pairs={{0,1},{1,0},{2,3},{3,2},{4,5},{5,4},{6,7},{7,6},{8,9},{9,8},{10,11... | collective-permute-start | bytes 14155784 | tf_op jit(solution)/shard_map/ppermute | solution.py:49
  4.0 0.1 collective-permute-start.8
  4.1 0.0 copy-start.4
  4.1 0.7 copy-done.4
  4.8 0.0 copy-start.5
  4.8 0.7 copy-done.5
  5.5 0.1 shard_map.86._
  5.6 12.5 %all_to_all.15 = bf16[16,2,3584]{2,1,0:T(2,128)(2,1)S(1)} all-to-all(bf16[16,2,3584]{2,1,0:T(2,128)(2,1)S(1)} %shard_map.86._), channel_id=1, replica_groups=mesh['y'=4,'x'=4,'z'=8,'c'=2] {'y','x'}, dimensions={0} | all-to-all | bytes 458752 | tf_op jit(solution)/shard_map/all_to_all | solution.py:355
  18.2 0.1 reshape.7.refs_0_
  18.3 1.7 %collective-permute-start = (bf16[32,3584]{1,0:T(8,128)(2,1)S(1)}, bf16[32,3584]{1,0:T(8,128)(2,1)S(1)}, u32[]{:S(2)}, u32[]{:S(2)}) collective-permute-start(bf16[32,3584]{1,0:T(8,128)(2,1)S(1)} %reshape.7.refs_0_), channel_id=1, source_target_pairs={{0,2},{2,4},{4,6},{6,8},{8,10},{10,12},{12,14},{14,0},{1,3},{3,5},... | collective-permute-start | bytes 688136 | tf_op jit(solution)/shard_map/ppermute | solution.py:56
  20.0 0.0 copy-start.2
  20.0 1.1 copy-done.2
  21.1 0.0 copy-start.3
  21.1 0.7 copy-done.3
  21.8 0.5 shard_map.87.b0
  22.3 0.1 collective-permute-start.9
  22.4 2.7 %collective-permute-start.10 = (bf16[64,4608]{1,0:T(8,128)(2,1)S(1)}, bf16[64,4608]{1,0:T(8,128)(2,1)S(1)}, u32[]{:S(2)}, u32[]{:S(2)}) collective-permute-start(bf16[64,4608]{1,0:T(8,128)(2,1)S(1)} %shard_map.87.b0), channel_id=1, source_target_pairs={{0,192},{64,0},{128,64},{192,128},{1,193},{65,1},{129,65},{193,129... | collective-permute-start | bytes 1769480 | tf_op jit(solution)/shard_map/ppermute | solution.py:57
  25.1 3.2 %collective-permute-done.refs_1_ = bf16[32,3584]{1,0:T(8,128)(2,1)S(1)} collective-permute-done((bf16[32,3584]{1,0:T(8,128)(2,1)S(1)}, bf16[32,3584]{1,0:T(8,128)(2,1)S(1)}, u32[]{:S(2)}, u32[]{:S(2)}) %collective-permute-start) | collective-permute-done | bytes 229408 | tf_op jit(solution)/shard_map/ppermute | solution.py:56
  28.3 1.2 %collective-permute-start.4 = (bf16[32,3584]{1,0:T(8,128)(2,1)S(1)}, bf16[32,3584]{1,0:T(8,128)(2,1)S(1)}, u32[]{:S(2)}, u32[]{:S(2)}) collective-permute-start(bf16[32,3584]{1,0:T(8,128)(2,1)S(1)} %reshape.7.refs_0_), channel_id=1, source_target_pairs={{0,14},{2,0},{4,2},{6,4},{8,6},{10,8},{12,10},{14,12},{1,15},{3,1}... | collective-permute-start | bytes 688136 | tf_op jit(solution)/shard_map/ppermute | solution.py:57
  29.5 4.0 %collective-permute-done.4.refs_2_ = bf16[32,3584]{1,0:T(8,128)(2,1)S(1)} collective-permute-done((bf16[32,3584]{1,0:T(8,128)(2,1)S(1)}, bf16[32,3584]{1,0:T(8,128)(2,1)S(1)}, u32[]{:S(2)}, u32[]{:S(2)}) %collective-permute-start.4) | collective-permute-done | bytes 229408 | tf_op jit(solution)/shard_map/ppermute | solution.py:57
  33.4 0.0 collective-permute-start.1
  33.5 3.1 %collective-permute-done.9.b1 = bf16[64,4608]{1,0:T(8,128)(2,1)S(1)} collective-permute-done((bf16[64,4608]{1,0:T(8,128)(2,1)S(1)}, bf16[64,4608]{1,0:T(8,128)(2,1)S(1)}, u32[]{:S(2)}, u32[]{:S(2)}) %collective-permute-start.9) | collective-permute-done | bytes 589856 | tf_op jit(solution)/shard_map/ppermute | solution.py:56
  36.6 4.2 %collective-permute-start.5 = (bf16[32,3584]{1,0:T(8,128)(2,1)S(1)}, bf16[32,3584]{1,0:T(8,128)(2,1)S(1)}, u32[]{:S(2)}, u32[]{:S(2)}) collective-permute-start(bf16[32,3584]{1,0:T(8,128)(2,1)S(1)} %collective-permute-done.4.refs_2_), channel_id=1, source_target_pairs={{0,14},{2,0},{4,2},{6,4},{8,6},{10,8},{12,10},{14,12},{1,15},{3,1}... | collective-permute-start | bytes 688136 | tf_op jit(solution)/shard_map/ppermute | solution.py:57
  40.8 0.0 collective-permute-done.1.refs_3_
  40.8 0.0 collective-permute-start.2
  40.8 0.0 collective-permute-done.10.b2
  40.8 0.1 collective-permute-start.11
  40.9 2.8 %collective-permute-done.5.refs_4_ = bf16[32,3584]{1,0:T(8,128)(2,1)S(1)} collective-permute-done((bf16[32,3584]{1,0:T(8,128)(2,1)S(1)}, bf16[32,3584]{1,0:T(8,128)(2,1)S(1)}, u32[]{:S(2)}, u32[]{:S(2)}) %collective-permute-start.5) | collective-permute-done | bytes 229408 | tf_op jit(solution)/shard_map/ppermute | solution.py:57
  43.7 3.1 %collective-permute-start.6 = (bf16[32,3584]{1,0:T(8,128)(2,1)S(1)}, bf16[32,3584]{1,0:T(8,128)(2,1)S(1)}, u32[]{:S(2)}, u32[]{:S(2)}) collective-permute-start(bf16[32,3584]{1,0:T(8,128)(2,1)S(1)} %collective-permute-done.5.refs_4_), channel_id=1, source_target_pairs={{0,14},{2,0},{4,2},{6,4},{8,6},{10,8},{12,10},{14,12},{1,15},{3,1}... | collective-permute-start | bytes 688136 | tf_op jit(solution)/shard_map/ppermute | solution.py:57
  46.9 0.0 collective-permute-done.2.refs_5_
  46.9 0.1 collective-permute-start.12
  47.0 2.8 %collective-permute-done.6.refs_6_ = bf16[32,3584]{1,0:T(8,128)(2,1)S(1)} collective-permute-done((bf16[32,3584]{1,0:T(8,128)(2,1)S(1)}, bf16[32,3584]{1,0:T(8,128)(2,1)S(1)}, u32[]{:S(2)}, u32[]{:S(2)}) %collective-permute-start.6) | collective-permute-done | bytes 229408 | tf_op jit(solution)/shard_map/ppermute | solution.py:57
  49.8 0.0 collective-permute-start.3
  49.8 0.0 copy-start.6
  49.8 0.0 copy-start
  49.9 0.0 collective-permute-done.11.b3
  49.9 3.7 %collective-permute-start.7 = (bf16[16,3584]{1,0:T(8,128)(2,1)S(1)}, bf16[16,3584]{1,0:T(8,128)(2,1)S(1)}, u32[]{:S(2)}, u32[]{:S(2)}) collective-permute-start(bf16[16,3584]{1,0:T(8,128)(2,1)S(1)} %slice.17), channel_id=1, source_target_pairs={{0,14},{2,0},{4,2},{6,4},{8,6},{10,8},{12,10},{14,12},{1,15},{3,1}... | collective-permute-start | bytes 344072 | tf_op jit(solution)/shard_map/ppermute | solution.py:61
  53.5 0.0 collective-permute-done.12.b4
  53.5 0.0 collective-permute-done.13.other_w_ref
  53.5 0.0 copy-start.1
  53.5 2.3 %copy-done.1 = bf16[2304,1024]{1,0:T(8,128)(2,1)S(1)} copy-done((bf16[2304,1024]{1,0:T(8,128)(2,1)S(1)}, bf16[2304,1024]{1,0:T(8,128)(2,1)}, u32[]{:S(2)}) %copy-start.1) | copy-done | bytes 4718616
  55.9 5.7 %shard_map.88.refs_9_.teacher_ref = bf16[256,1024]{1,0:T(8,128)(2,1)S(1)} custom-call(bf16[64,4608]{1,0:T(8,128)(2,1)S(1)} %shard_map.87.b0, bf16[64,4608]{1,0:T(8,128)(2,1)S(1)} %collective-permute-done.9.b1, bf16[64,4608]{1,0:T(8,128)(2,1)S(1)} %collective-permute-done.10.b2, bf16[32,4608]{1,0:T(8,128)(2,1)S(1)} %collective-permute-done.11.b3, ...), custom_call_target="tpu_custom_call" | custom-call | flops 1024 | bytes 1024 | tf_op jit(solution)/shard_map/pallas_call | solution.py:33
  61.6 0.0 collective-permute-done.8.refs_8_.other_w_ref
  61.6 0.0 copy-done.6
  61.6 0.0 copy-done
  61.6 4.5 %shard_map.89 = (bf16[224,1024]{1,0:T(8,128)(2,1)S(1)}, f32[4,224,128]{2,1,0:T(8,128)S(1)}) custom-call(bf16[32,3584]{1,0:T(8,128)(2,1)S(1)} %reshape.7.refs_0_, bf16[32,3584]{1,0:T(8,128)(2,1)S(1)} %collective-permute-done.refs_1_, bf16[32,3584]{1,0:T(8,128)(2,1)S(1)} %collective-permute-done.4.refs_2_, ...), custom_call_target="tpu_custom_call" | custom-call | flops 1024 | bytes 1024 | tf_op jit(solution)/shard_map/pallas_call | solution.py:33
  66.1 0.0 collective-permute-done.3.low.refs_7_
  66.1 0.0 collective-permute-done.7.high.refs_8_
  66.1 3.6 %shard_map.90 = (bf16[32,1024]{1,0:T(8,128)(2,1)S(1)}, f32[16,8,128]{2,1,0:T(8,128)S(1)}) custom-call(bf16[16,3584]{1,0:T(8,128)(2,1)S(1)} %collective-permute-done.3.low.refs_7_, bf16[16,3584]{1,0:T(8,128)(2,1)S(1)} %collective-permute-done.7.high.refs_8_, bf16[1792,1024]{1,0:T(8,128)(2,1)S(1)} %copy-done, ...), custom_call_target="tpu_custom_call" | custom-call | flops 1024 | bytes 1024 | tf_op jit(solution)/shard_map/pallas_call | solution.py:33
  69.7 0.1 shard_map.92.own_ref
  69.8 4.9 %collective-permute-start.14 = (bf16[512,1024]{1,0:T(8,128)(2,1)S(1)}, bf16[512,1024]{1,0:T(8,128)(2,1)S(1)}, u32[]{:S(2)}, u32[]{:S(2)}) collective-permute-start(bf16[512,1024]{1,0:T(8,128)(2,1)S(1)} %shard_map.92.own_ref), channel_id=1, source_target_pairs={{0,1},{1,0},{2,3},{3,2},{4,5},{5,4},{6,7},{7,6},{8,9},{9,8},{10,11... | collective-permute-start | bytes 3145736 | tf_op jit(solution)/shard_map/ppermute | solution.py:49
  74.6 1.6 %shard_map.93 = (bf16[1792,256]{1,0:T(8,128)(2,1)S(1)}, bf16[1792,256]{1,0:T(8,128)(2,1)}) custom-call(bf16[32,3584]{1,0:T(8,128)(2,1)S(1)} %reshape.7.refs_0_, bf16[32,3584]{1,0:T(8,128)(2,1)S(1)} %collective-permute-done.refs_1_, bf16[32,3584]{1,0:T(8,128)(2,1)S(1)} %collective-permute-done.4.refs_2_, bf16[32,3584]{1,0:T(8,128)(2,1)S(1)} %collective-permute-done.1.refs_3_, ...), custom_call_target="tpu_custom_call" | custom-call | flops 1024 | bytes 1024 | tf_op jit(solution)/shard_map/pallas_call | solution.py:33
  76.2 0.0 collective-permute-start.16
  76.3 9.5 %all_to_all.16.sums_ref = f32[16,8,128]{2,1,0:T(8,128)S(1)} all-to-all(f32[16,8,128]{2,1,0:T(8,128)S(1)} %get-tuple-element.9._.refs_9_), channel_id=1, replica_groups=mesh['y'=4,'x'=4,'z'=8,'c'=2] {'y','x'}, dimensions={0} | all-to-all | bytes 131072 | tf_op jit(solution)/shard_map/all_to_all | solution.py:377
  85.8 0.6 shard_map.91
  86.4 7.5 %all-to-all-start.2 = ((f32[16,8,128]{2,1,0:T(8,128)}), f32[16,8,128]{2,1,0:T(8,128)S(1)}, u32[]{:S(2)}, u32[]{:S(2)}) async-start(f32[16,8,128]{2,1,0:T(8,128)} %shard_map.91), calls=%async_computation.2 | async-start | bytes 131072 | tf_op jit(solution)/shard_map/all_to_all | solution.py:378
  93.9 0.2 collective-permute-start.15
  94.1 1.0 collective-permute-done.15.oth_targets_ref
  95.1 6.7 %all-to-all-done.2.sums_ref = f32[16,8,128]{2,1,0:T(8,128)S(1)} async-done(((f32[16,8,128]{2,1,0:T(8,128)}), f32[16,8,128]{2,1,0:T(8,128)S(1)}, u32[]{:S(2)}, u32[]{:S(2)}) %all-to-all-start.2) | async-done | bytes 65568 | tf_op jit(solution)/shard_map/all_to_all | solution.py:378
  101.7 0.0 collective-permute-done.16.other_rows
  101.7 0.0 collective-permute-done.14.other_ref
  101.8 7.7 %shard_map.94 = (f32[1,2]{1,0:T(1,128)}, bf16[1792,1024]{1,0:T(8,128)(2,1)}) custom-call(f32[16,8,128]{2,1,0:T(8,128)S(1)} %all-to-all-done.2.sums_ref, bf16[512,1024]{1,0:T(8,128)(2,1)S(1)} %shard_map.92.own_ref, bf16[512,1024]{1,0:T(8,128)(2,1)S(1)} %collective-permute-done.14.other_ref, s32[1,256]{1,0:T(1,128)S(1)} %copy-done.6, ...), custom_call_target="tpu_custom_call" | custom-call | flops 1024 | bytes 1024 | tf_op jit(solution)/shard_map/pallas_call | solution.py:336
  (4 shorter events, 0.1 us)
Async XLA Ops:
  0.6 52.9 %collective-permute-start.13 = (bf16[2304,1024]{1,0:T(8,128)(2,1)}, bf16[2304,1024]{1,0:T(8,128)(2,1)}, u32[]{:S(2)}, u32[]{:S(2)}) collective-permute-start(bf16[2304,1024]{1,0:T(8,128)(2,1)} %own_w_ref.2), channel_id=1, source_target_pairs={{0,1},{1,0},{2,3},{3,2},{4,5},{5,4},{6,7},{7,6},{8,9},{9,8},{10,11... | collective-permute-start | bytes 14155784 | tf_op jit(solution)/shard_map/ppermute | solution.py:49
  4.0 57.6 %collective-permute-start.8 = (bf16[1792,1024]{1,0:T(8,128)(2,1)}, bf16[1792,1024]{1,0:T(8,128)(2,1)}, u32[]{:S(2)}, u32[]{:S(2)}) collective-permute-start(bf16[1792,1024]{1,0:T(8,128)(2,1)} %own_w_ref.3), channel_id=1, source_target_pairs={{0,1},{1,0},{2,3},{3,2},{4,5},{5,4},{6,7},{7,6},{8,9},{9,8},{10,11... | collective-permute-start | bytes 11010056 | tf_op jit(solution)/shard_map/ppermute | solution.py:49
  4.1 0.7 copy-start.4
  4.8 0.7 copy-start.5
  18.3 10.0 %collective-permute-start = (bf16[32,3584]{1,0:T(8,128)(2,1)S(1)}, bf16[32,3584]{1,0:T(8,128)(2,1)S(1)}, u32[]{:S(2)}, u32[]{:S(2)}) collective-permute-start(bf16[32,3584]{1,0:T(8,128)(2,1)S(1)} %reshape.7.refs_0_), channel_id=1, source_target_pairs={{0,2},{2,4},{4,6},{6,8},{8,10},{10,12},{12,14},{14,0},{1,3},{3,5},... | collective-permute-start | bytes 688136 | tf_op jit(solution)/shard_map/ppermute | solution.py:56
  20.0 1.1 copy-start.2
  21.1 0.7 copy-start.3
  22.3 14.3 %collective-permute-start.9 = (bf16[64,4608]{1,0:T(8,128)(2,1)S(1)}, bf16[64,4608]{1,0:T(8,128)(2,1)S(1)}, u32[]{:S(2)}, u32[]{:S(2)}) collective-permute-start(bf16[64,4608]{1,0:T(8,128)(2,1)S(1)} %shard_map.87.b0), channel_id=1, source_target_pairs={{0,64},{64,128},{128,192},{192,0},{1,65},{65,129},{129,193},{193,1... | collective-permute-start | bytes 1769480 | tf_op jit(solution)/shard_map/ppermute | solution.py:56
  22.4 18.4 %collective-permute-start.10 = (bf16[64,4608]{1,0:T(8,128)(2,1)S(1)}, bf16[64,4608]{1,0:T(8,128)(2,1)S(1)}, u32[]{:S(2)}, u32[]{:S(2)}) collective-permute-start(bf16[64,4608]{1,0:T(8,128)(2,1)S(1)} %shard_map.87.b0), channel_id=1, source_target_pairs={{0,192},{64,0},{128,64},{192,128},{1,193},{65,1},{129,65},{193,129... | collective-permute-start | bytes 1769480 | tf_op jit(solution)/shard_map/ppermute | solution.py:57
  28.3 5.2 %collective-permute-start.4 = (bf16[32,3584]{1,0:T(8,128)(2,1)S(1)}, bf16[32,3584]{1,0:T(8,128)(2,1)S(1)}, u32[]{:S(2)}, u32[]{:S(2)}) collective-permute-start(bf16[32,3584]{1,0:T(8,128)(2,1)S(1)} %reshape.7.refs_0_), channel_id=1, source_target_pairs={{0,14},{2,0},{4,2},{6,4},{8,6},{10,8},{12,10},{14,12},{1,15},{3,1}... | collective-permute-start | bytes 688136 | tf_op jit(solution)/shard_map/ppermute | solution.py:57
  33.4 7.3 %collective-permute-start.1 = (bf16[32,3584]{1,0:T(8,128)(2,1)S(1)}, bf16[32,3584]{1,0:T(8,128)(2,1)S(1)}, u32[]{:S(2)}, u32[]{:S(2)}) collective-permute-start(bf16[32,3584]{1,0:T(8,128)(2,1)S(1)} %collective-permute-done.refs_1_), channel_id=1, source_target_pairs={{0,2},{2,4},{4,6},{6,8},{8,10},{10,12},{12,14},{14,0},{1,3},{3,5},... | collective-permute-start | bytes 688136 | tf_op jit(solution)/shard_map/ppermute | solution.py:56
  36.6 7.2 %collective-permute-start.5 = (bf16[32,3584]{1,0:T(8,128)(2,1)S(1)}, bf16[32,3584]{1,0:T(8,128)(2,1)S(1)}, u32[]{:S(2)}, u32[]{:S(2)}) collective-permute-start(bf16[32,3584]{1,0:T(8,128)(2,1)S(1)} %collective-permute-done.4.refs_2_), channel_id=1, source_target_pairs={{0,14},{2,0},{4,2},{6,4},{8,6},{10,8},{12,10},{14,12},{1,15},{3,1}... | collective-permute-start | bytes 688136 | tf_op jit(solution)/shard_map/ppermute | solution.py:57
  40.8 6.1 %collective-permute-start.2 = (bf16[32,3584]{1,0:T(8,128)(2,1)S(1)}, bf16[32,3584]{1,0:T(8,128)(2,1)S(1)}, u32[]{:S(2)}, u32[]{:S(2)}) collective-permute-start(bf16[32,3584]{1,0:T(8,128)(2,1)S(1)} %collective-permute-done.1.refs_3_), channel_id=1, source_target_pairs={{0,2},{2,4},{4,6},{6,8},{8,10},{10,12},{12,14},{14,0},{1,3},{3,5},... | collective-permute-start | bytes 688136 | tf_op jit(solution)/shard_map/ppermute | solution.py:56
  40.8 9.0 %collective-permute-start.11 = (bf16[32,4608]{1,0:T(8,128)(2,1)S(1)}, bf16[32,4608]{1,0:T(8,128)(2,1)S(1)}, u32[]{:S(2)}, u32[]{:S(2)}) collective-permute-start(bf16[32,4608]{1,0:T(8,128)(2,1)S(1)} %slice.18), channel_id=1, source_target_pairs={{0,64},{64,128},{128,192},{192,0},{1,65},{65,129},{129,193},{193,1... | collective-permute-start | bytes 884744 | tf_op jit(solution)/shard_map/ppermute | solution.py:60
  43.7 6.1 %collective-permute-start.6 = (bf16[32,3584]{1,0:T(8,128)(2,1)S(1)}, bf16[32,3584]{1,0:T(8,128)(2,1)S(1)}, u32[]{:S(2)}, u32[]{:S(2)}) collective-permute-start(bf16[32,3584]{1,0:T(8,128)(2,1)S(1)} %collective-permute-done.5.refs_4_), channel_id=1, source_target_pairs={{0,14},{2,0},{4,2},{6,4},{8,6},{10,8},{12,10},{14,12},{1,15},{3,1}... | collective-permute-start | bytes 688136 | tf_op jit(solution)/shard_map/ppermute | solution.py:57
  46.9 6.6 %collective-permute-start.12 = (bf16[32,4608]{1,0:T(8,128)(2,1)S(1)}, bf16[32,4608]{1,0:T(8,128)(2,1)S(1)}, u32[]{:S(2)}, u32[]{:S(2)}) collective-permute-start(bf16[32,4608]{1,0:T(8,128)(2,1)S(1)} %slice.19), channel_id=1, source_target_pairs={{0,192},{64,0},{128,64},{192,128},{1,193},{65,1},{129,65},{193,129... | collective-permute-start | bytes 884744 | tf_op jit(solution)/shard_map/ppermute | solution.py:61
  49.8 16.3 %collective-permute-start.3 = (bf16[16,3584]{1,0:T(8,128)(2,1)S(1)}, bf16[16,3584]{1,0:T(8,128)(2,1)S(1)}, u32[]{:S(2)}, u32[]{:S(2)}) collective-permute-start(bf16[16,3584]{1,0:T(8,128)(2,1)S(1)} %slice.16), channel_id=1, source_target_pairs={{0,2},{2,4},{4,6},{6,8},{8,10},{10,12},{12,14},{14,0},{1,3},{3,5},... | collective-permute-start | bytes 344072 | tf_op jit(solution)/shard_map/ppermute | solution.py:60
  49.8 11.7 %copy-start.6 = (s32[1,256]{1,0:T(1,128)S(1)}, s32[1,256]{1,0:T(1,128)}, u32[]{:S(2)}) copy-start(s32[1,256]{1,0:T(1,128)} %targets_ref.3) | copy-start | bytes 3076
  49.8 11.7 %copy-start = (bf16[1792,1024]{1,0:T(8,128)(2,1)S(1)}, bf16[1792,1024]{1,0:T(8,128)(2,1)}, u32[]{:S(2)}) copy-start(bf16[1792,1024]{1,0:T(8,128)(2,1)} %own_w_ref.3) | copy-start | bytes 11010052
  49.9 16.3 %collective-permute-start.7 = (bf16[16,3584]{1,0:T(8,128)(2,1)S(1)}, bf16[16,3584]{1,0:T(8,128)(2,1)S(1)}, u32[]{:S(2)}, u32[]{:S(2)}) collective-permute-start(bf16[16,3584]{1,0:T(8,128)(2,1)S(1)} %slice.17), channel_id=1, source_target_pairs={{0,14},{2,0},{4,2},{6,4},{8,6},{10,8},{12,10},{14,12},{1,15},{3,1}... | collective-permute-start | bytes 344072 | tf_op jit(solution)/shard_map/ppermute | solution.py:61
  53.5 2.3 %copy-start.1 = (bf16[2304,1024]{1,0:T(8,128)(2,1)S(1)}, bf16[2304,1024]{1,0:T(8,128)(2,1)}, u32[]{:S(2)}) copy-start(bf16[2304,1024]{1,0:T(8,128)(2,1)} %own_w_ref.2) | copy-start | bytes 14155780
  69.8 32.0 %collective-permute-start.14 = (bf16[512,1024]{1,0:T(8,128)(2,1)S(1)}, bf16[512,1024]{1,0:T(8,128)(2,1)S(1)}, u32[]{:S(2)}, u32[]{:S(2)}) collective-permute-start(bf16[512,1024]{1,0:T(8,128)(2,1)S(1)} %shard_map.92.own_ref), channel_id=1, source_target_pairs={{0,1},{1,0},{2,3},{3,2},{4,5},{5,4},{6,7},{7,6},{8,9},{9,8},{10,11... | collective-permute-start | bytes 3145736 | tf_op jit(solution)/shard_map/ppermute | solution.py:49
  76.2 25.5 %collective-permute-start.16 = (bf16[1792,256]{1,0:T(8,128)(2,1)}, bf16[1792,256]{1,0:T(8,128)(2,1)}, u32[]{:S(2)}, u32[]{:S(2)}) collective-permute-start(bf16[1792,256]{1,0:T(8,128)(2,1)} %get-tuple-element.13), channel_id=1, source_target_pairs={{0,1},{1,0},{2,3},{3,2},{4,5},{5,4},{6,7},{7,6},{8,9},{9,8},{10,11... | collective-permute-start | bytes 2752520 | tf_op jit(solution)/shard_map/ppermute | solution.py:49
  86.4 15.3 %all-to-all-start.2 = ((f32[16,8,128]{2,1,0:T(8,128)}), f32[16,8,128]{2,1,0:T(8,128)S(1)}, u32[]{:S(2)}, u32[]{:S(2)}) async-start(f32[16,8,128]{2,1,0:T(8,128)} %shard_map.91), calls=%async_computation.2 | async-start | bytes 131072 | tf_op jit(solution)/shard_map/all_to_all | solution.py:378
  93.9 1.1 %collective-permute-start.15 = (s32[1,256]{1,0:T(1,128)S(1)}, s32[1,256]{1,0:T(1,128)S(1)}, u32[]{:S(2)}, u32[]{:S(2)}) collective-permute-start(s32[1,256]{1,0:T(1,128)S(1)} %copy-done.6), channel_id=1, source_target_pairs={{0,1},{1,0},{2,3},{3,2},{4,5},{5,4},{6,7},{7,6},{8,9},{9,8},{10,11... | collective-permute-start | bytes 3080 | tf_op jit(solution)/shard_map/ppermute | solution.py:49

commit v4 on v3

v4 whole, which is shorter than its diff:
```python
import jax
import jax.numpy as jnp
from jax import lax
from jax.experimental import pallas as pl
from jax.experimental.pallas import tpu as pltpu
from jax.sharding import Mesh, PartitionSpec as P

F32 = jnp.float32
BF16 = jnp.bfloat16
I32 = jnp.int32
NY, NX, NZ = 4, 4, 8
ROWS = 2
PLANE = NY * NX * ROWS
OWN = NZ * PLANE
EARLY = OWN - PLANE
STEP = 32
TILE = 256
PARTS = 8
LANES = 128
VMEM = pl.BlockSpec(memory_space=pltpu.VMEM)
ANY = pl.BlockSpec(memory_space=pl.ANY)
SHORT = pl.CostEstimate(flops=1024, bytes_accessed=1024, transcendentals=0)
LONG = pl.CostEstimate(flops=5_000_000_000, bytes_accessed=1024, transcendentals=0)


def params(mebibytes=8):
    return pltpu.CompilerParams(vmem_limit_bytes=mebibytes * 1024 * 1024)


def struct(shape, dtype):
    return jax.ShapeDtypeStruct(shape, dtype)


def call(body, out_shape, operands, scratch=(), cost=SHORT):
    several = isinstance(out_shape, tuple)
    return pl.pallas_call(
        body,
        out_shape=out_shape,
        in_specs=[VMEM] * len(operands),
        out_specs=(VMEM,) * len(out_shape) if several else VMEM,
        scratch_shapes=scratch,
        compiler_params=params(),
        cost_estimate=cost,
    )(*operands)


def each(count, width, body):
    for index in range(count):
        body(index * width)


def up(n, k):
    return [(i, (i + k) % n) for i in range(n)]


def swap_cores(value):
    return lax.ppermute(value, "c", [(0, 1), (1, 0)])


def both_ways(low, high, axis, n):
    return lax.ppermute(low, axis, up(n, 1)), lax.ppermute(high, axis, up(n, -1))


def gate_kernel(low, high, t_low, t_high, *refs):
    low_out, high_out, t_low_out, t_high_out = refs[-4:]
    low_out[...] = low[...]
    high_out[...] = high[...]
    half = t_low_out.shape[0]
    t_low_out[...] = t_low[:half]
    t_high_out[...] = t_high[half:]


def gate(low, high, t_low, t_high, *others):
    part = struct((t_low.shape[0] // 2, t_low.shape[1]), BF16)
    plane = struct(low.shape, BF16)
    return pl.pallas_call(
        gate_kernel,
        out_shape=(plane, plane, part, part),
        in_specs=[VMEM] * 4 + [ANY] * len(others),
        out_specs=(VMEM,) * 4,
        compiler_params=params(4),
        cost_estimate=LONG,
    )(low, high, t_low, t_high, *others)


def rings(plane, rows, others):
    t_low, t_high = both_ways(rows, rows, "y", NY)
    planes = [plane]
    low = high = plane
    for step in range(NZ // 2 - 1):
        if step == 2:
            low, high, t_low_half, t_high_half = gate(low, high, t_low, t_high, *others)
        low, high = both_ways(low, high, "z", NZ)
        planes += [low, high]
    sections = [rows, t_low, t_high, *both_ways(t_low_half, t_high_half, "y", NY)]
    half = plane.shape[0] // 2
    planes += both_ways(low[:half], high[half:], "z", NZ)
    return planes, sections


def distance(position):
    return jnp.where(position % 2 == 1, NZ - (position + 1) // 2, position // 2)


def natural_row(row, z):
    position, inner = row // PLANE, row % PLANE
    y, x, i = inner // (NX * ROWS), inner // ROWS % NX, inner % ROWS
    return ((y * NX + x) * NZ + (z + distance(position)) % NZ) * ROWS + i


def iota(shape, axis):
    return lax.broadcasted_iota(I32, shape, axis)


def normalize(hidden, gain):
    values = hidden.astype(F32)
    spread = jnp.mean(values * values, axis=-1, keepdims=True)
    return (values * lax.rsqrt(spread + 1e-06) * gain.reshape(1, -1)).astype(BF16)


def peers_kernel(hidden_ref, out_ref):
    for peer in range(out_ref.shape[0]):
        out_ref[peer] = hidden_ref[...]


def for_peers(hidden):
    out = struct((NY * NX, *hidden.shape), BF16)
    return call(peers_kernel, out, (hidden,), cost=LONG)


def plane_kernel(*refs):
    got_ref, gain_ref, *_, out_ref, rows_ref = refs
    for peer in range(NY * NX):
        rows_ref[pl.ds(peer * ROWS, ROWS)] = got_ref[peer].astype(F32)
    out_ref[...] = normalize(rows_ref[...], gain_ref[...])


def plane_rows(got, gain, *others):
    shape = (PLANE, got.shape[2])
    return pl.pallas_call(
        plane_kernel,
        out_shape=struct(shape, BF16),
        in_specs=[VMEM, VMEM] + [ANY] * len(others),
        out_specs=VMEM,
        scratch_shapes=[pltpu.VMEM(shape, F32)],
        compiler_params=params(),
        cost_estimate=LONG,
    )(got, gain, *others)


def teacher_norm_kernel(hidden_ref, gain_ref, _, out_ref):
    z = lax.axis_index("z")
    normed = normalize(hidden_ref[...], gain_ref[...])
    n = normed.shape[0]
    row = iota((n, n), 0)
    position, x, i = row // (NX * ROWS), row // ROWS % NX, row % ROWS
    source = (x * NZ + (z + distance(position)) % NZ) * ROWS + i
    moved = jnp.where(iota((n, n), 1) == source, 1.0, 0.0).astype(BF16)
    out_ref[...] = jnp.dot(moved, normed, preferred_element_type=F32).astype(BF16)


def teacher_norm(hidden, gain, other):
    return pl.pallas_call(
        teacher_norm_kernel,
        out_shape=struct(hidden.shape, BF16),
        in_specs=[VMEM, VMEM, ANY],
        out_specs=VMEM,
        compiler_params=params(),
        cost_estimate=LONG,
    )(hidden, gain, other)


def halves(ref_width):
    k, core = ref_width // 2, lax.axis_index("c")
    return tuple(pl.ds(pl.multiple_of(half * k, LANES), k) for half in (core, 1 - core))


def fetch_kernel(head, out_ref, sem):
    part = head.shape[0] // PARTS
    copies = []
    for index in range(PARTS):
        rows = pl.ds(index * part, part)
        copies.append(pltpu.make_async_copy(head.at[rows], out_ref.at[rows], sem.at[index]))
        copies[-1].start()
    for copy in copies:
        copy.wait()


def fetched(head):
    return pl.pallas_call(
        fetch_kernel,
        out_shape=struct(head.shape, head.dtype),
        in_specs=[ANY],
        out_specs=VMEM,
        scratch_shapes=[pltpu.SemaphoreType.DMA((PARTS,))],
        compiler_params=params(4),
        cost_estimate=LONG,
    )(head)


def logits(rows_ref, own_w_ref, other_w_ref, out_ref):
    own, other = halves(rows_ref.shape[1])
    for at in range(0, out_ref.shape[1], TILE):
        columns = pl.ds(at, TILE)
        out_ref[:, columns] = soft_cap(
            jnp.dot(rows_ref[:, own], own_w_ref[:, columns], preferred_element_type=F32)
            + jnp.dot(rows_ref[:, other], other_w_ref[:, columns], preferred_element_type=F32)
        )


def soft_cap(logits):
    return (30.0 * jnp.tanh(logits / 30.0)).astype(BF16)


def near_teacher_kernel(b0, b1, b2, own_w_ref, other_w_ref, out_ref, rows_ref):
    rows_ref[...] = jnp.concatenate([b0[...], b1[...], b2[...]])
    logits(rows_ref, own_w_ref, other_w_ref, out_ref)


def near_teacher(blocks, own_head, other_head):
    k, vocab = own_head.shape
    n = 3 * blocks[0].shape[0]
    scratch = [pltpu.VMEM((n, 2 * k), BF16)]
    out = struct((n, vocab), BF16)
    return call(near_teacher_kernel, out, (*blocks, own_head, other_head), scratch, LONG)


def far_teacher_kernel(b3, b4, near_ref, own_w_ref, other_w_ref, out_ref, rows_ref, far_ref):
    rows_ref[...] = jnp.concatenate([b3[...], b4[...]])
    logits(rows_ref, own_w_ref, other_w_ref, far_ref)
    section = rows_ref.shape[0]
    y = lax.axis_index("y")
    row = iota((OWN, OWN), 0)
    position, inner = row // PLANE, row % PLANE
    apart = (inner // (NX * ROWS) - y) % NY
    place = jnp.where(apart == 0, 0, jnp.where(apart == NY - 1, 1, jnp.where(apart == 1, 2, 3)))
    source = place * section + position * (NX * ROWS) + inner % (NX * ROWS)
    moved = jnp.where(iota((OWN, OWN), 1) == source, 1.0, 0.0).astype(BF16)
    whole = jnp.concatenate([near_ref[...], far_ref[...]])
    out_ref[...] = jnp.dot(moved, whole, preferred_element_type=F32).astype(BF16)


def far_teacher(blocks, near, own_head, other_head):
    k, vocab = own_head.shape
    n = OWN - near.shape[0]
    scratch = [pltpu.VMEM((n, 2 * k), BF16), pltpu.VMEM((n, vocab), BF16)]
    out = struct((OWN, vocab), BF16)
    return call(far_teacher_kernel, out, (*blocks, near, own_head, other_head), scratch, LONG)


def local_targets(targets_ref, z, first, rows):
    shape = (rows.shape[0], OWN)
    here = iota(shape, 1) == natural_row(rows, z)
    return jnp.sum(jnp.where(here, targets_ref[...], 0), axis=1, keepdims=True) - first


def first_column(vocab):
    y, x, z = lax.axis_index("y"), lax.axis_index("x"), lax.axis_index("z")
    return ((y * NX + x) * NZ + z) * vocab


def fold(values):
    total = values[:, :LANES]
    for start in range(LANES, values.shape[1], LANES):
        total = total + values[:, start : start + LANES]
    return total


def sums_of(start, capped_ref, teacher_ref, targets_ref):
    n, vocab = capped_ref.shape
    z, first = lax.axis_index("z"), first_column(vocab)
    totals = [[] for _ in range(4)]
    for at in range(0, n, STEP):
        stud_vals = capped_ref[pl.ds(at, STEP)].astype(F32)
        teach_vals = teacher_ref[pl.ds(start + at, STEP)].astype(F32)
        stud_exp, teach_exp = jnp.exp(stud_vals), jnp.exp(teach_vals)
        target = local_targets(targets_ref, z, first, iota((STEP, 1), 0) + (start + at))
        hit = iota((STEP, vocab), 1) == target
        totals[0].append(fold(teach_exp))
        totals[1].append(fold(stud_exp))
        totals[2].append(fold(teach_exp * (teach_vals - stud_vals)))
        totals[3].append(fold(jnp.where(hit, stud_vals, 0.0)))
    here = iota((n, OWN), 1) == natural_row(iota((n, OWN), 0) + start, z)
    rows = []
    for parts in totals:
        total = jnp.sum(jnp.concatenate(parts, axis=0), axis=1, keepdims=True)
        flat = jnp.sum(jnp.where(here, total, 0.0), axis=0, keepdims=True)
        rows += [flat[:, at : at + LANES] for at in range(0, OWN, LANES)]
    return jnp.concatenate(rows, axis=0)


def early_kernel(*refs):
    *blocks, own_w_ref, other_w_ref, teacher_ref, targets_ref, capped_ref, sums_ref, rows_ref = refs
    for q, block in enumerate(blocks):
        rows_ref[pl.ds(q * PLANE, PLANE)] = block[...]
    logits(rows_ref, own_w_ref, other_w_ref, capped_ref)
    sums_ref[...] = sums_of(0, capped_ref, teacher_ref, targets_ref)


def early_rows(planes, own_head, other_head, teacher, targets):
    k, vocab = own_head.shape
    out = (struct((EARLY, vocab), BF16), struct((8, LANES), F32))
    scratch = [pltpu.VMEM((EARLY, 2 * k), BF16)]
    return call(early_kernel, out, (*planes, own_head, other_head, teacher, targets), scratch, LONG)


def last_kernel(
    low, high, own_w_ref, other_w_ref, teacher_ref, targets_ref, early_ref,
    capped_ref, out_ref, rows_ref,
):
    rows_ref[...] = jnp.concatenate([low[...], high[...]])
    logits(rows_ref, own_w_ref, other_w_ref, capped_ref)
    tile = early_ref[...] + sums_of(EARLY, capped_ref, teacher_ref, targets_ref)
    for peer in range(out_ref.shape[0]):
        out_ref[peer] = tile


def last_rows(low, high, own_head, other_head, teacher, targets, early):
    k, vocab = own_head.shape
    out = (struct((PLANE, vocab), BF16), struct((NY * NX, 8, LANES), F32))
    operands = (low, high, own_head, other_head, teacher, targets, early)
    return call(last_kernel, out, operands, [pltpu.VMEM((PLANE, 2 * k), BF16)])


def collect_kernel(early_ref, last_ref, teacher_ref, _, out_ref):
    out_ref[:EARLY] = early_ref[...]
    out_ref[EARLY:OWN] = last_ref[...]
    out_ref[OWN:] = teacher_ref[...]


def collect(early, last, teacher, sums):
    out = struct((2 * OWN, teacher.shape[1]), BF16)
    return call(collect_kernel, out, (early, last, teacher, sums))


def transpose_kernel(*refs):
    *blocks, low, high, _, keep_ref, send_ref, rows_ref = refs
    for q, block in enumerate(blocks):
        rows_ref[pl.ds(q * PLANE, PLANE)] = block[...]
    rows_ref[EARLY:] = jnp.concatenate([low[...], high[...]])
    k, core = keep_ref.shape[0], lax.axis_index("c")

    def turn(at):
        for ref, half in ((keep_ref, core), (send_ref, 1 - core)):
            columns = pl.ds(pl.multiple_of(half * k + at, LANES), TILE)
            ref[pl.ds(at, TILE)] = rows_ref[:, columns].T

    each(k // TILE, TILE, turn)


def transposed(blocks, sums):
    width = blocks[0].shape[1]
    out = struct((width // 2, OWN), BF16)
    scratch = [pltpu.VMEM((OWN, width), BF16)]
    return call(transpose_kernel, (out, out), (*blocks, sums), scratch)


def gradient_kernel(
    sums_ref, own_ref, other_ref, targets_ref, oth_targets_ref, own_rows, other_rows,
    loss_ref, out_ref, scale_ref, target_ref,
):
    vocab = own_ref.shape[1]

    @pl.when(pl.program_id(0) == 0)
    def _():
        z, core = lax.axis_index("z"), lax.axis_index("c")
        position = (lax.axis_index("y") * NX + lax.axis_index("x")) * NZ + z
        here = iota((OWN, OWN), 1) == natural_row(iota((OWN, OWN), 0), z)
        totals = []
        for side in range(2):
            total = sums_ref[side]
            for peer in range(1, NZ):
                total = total + sums_ref[2 * peer + side]
            totals.append(total)
        own = jnp.where(core == 0, totals[0], totals[1])
        other = jnp.where(core == 0, totals[1], totals[0])

        def flat(tile, kind):
            first, second = tile[2 * kind : 2 * kind + 1], tile[2 * kind + 1 : 2 * kind + 2]
            return jnp.concatenate([first, second], axis=1)

        teach_total, stud_total, cross_sum, target_logit = (flat(own, k) for k in range(4))
        loss = cross_sum / teach_total - jnp.log(teach_total) + 2.0 * jnp.log(stud_total) - target_logit
        lane = iota((1, OWN), 1)
        picked = [
            jnp.sum(jnp.where(lane == position * ROWS + i, loss, 0.0), axis=1, keepdims=True)
            for i in range(ROWS)
        ]
        loss_ref[...] = jnp.concatenate(picked, axis=1)
        first = first_column(vocab)
        for side, tile, targets in ((0, own, targets_ref), (1, other, oth_targets_ref)):
            rows = pl.ds(side * OWN, OWN)
            target = local_targets(targets, z, first, iota((OWN, 1), 0))
            target_ref[rows] = jnp.broadcast_to(target, (OWN, LANES))
            for kind, value in ((0, 1.0 / flat(tile, 0)), (1, 2.0 / flat(tile, 1))):
                column = jnp.sum(jnp.where(here, value, 0.0), axis=1, keepdims=True)
                scale_ref[kind, rows] = jnp.broadcast_to(column, (OWN, LANES))

    tile = out_ref.shape[1]
    start = pl.multiple_of(pl.program_id(0) * tile, tile)
    columns = pl.ds(start, tile)
    grads = []
    for side, values in ((0, own_ref), (1, other_ref)):
        rows = pl.ds(side * OWN, OWN)
        teach_scale, stud_scale = (scale_ref[kind, rows, :1] for kind in range(2))
        stud_vals = values[:OWN, columns].astype(F32)
        teach_vals = values[OWN:, columns].astype(F32)
        scaled = jnp.exp(stud_vals) * stud_scale - jnp.exp(teach_vals) * teach_scale
        hit = iota((OWN, tile), 1) == target_ref[rows, :1] - start
        scaled = scaled - jnp.where(hit, 1.0, 0.0)
        grads.append((scaled * (1.0 - stud_vals * stud_vals * (1.0 / 900.0))).astype(BF16))
    out_ref[...] = (
        jnp.dot(own_rows[...], grads[0], preferred_element_type=F32)
        + jnp.dot(other_rows[...], grads[1], preferred_element_type=F32)
    ).astype(BF16)


def gradient(sums, own, other, targets, oth_targets, own_rows, other_rows):
    k, vocab = own_rows.shape[0], own.shape[1]
    operands = [sums, own, other, targets, oth_targets, own_rows, other_rows]
    return pl.pallas_call(
        gradient_kernel,
        grid=(vocab // TILE,),
        out_shape=(struct((1, ROWS), F32), struct((k, vocab), BF16)),
        in_specs=[VMEM] * len(operands),
        out_specs=(
            pl.BlockSpec((1, ROWS), lambda j: (0, 0)),
            pl.BlockSpec((k, TILE), lambda j: (0, j)),
        ),
        scratch_shapes=[pltpu.VMEM((2, 2 * OWN, LANES), F32), pltpu.VMEM((2 * OWN, LANES), I32)],
        compiler_params=params(),
        cost_estimate=SHORT,
    )(*operands)


def shards(
    student_hidden, teacher_hidden, student_gain, teacher_gain, student_head, teacher_head, targets
):
    other_teacher_head = swap_cores(teacher_head)
    other_student_head = swap_cores(student_head)
    oth_targets = swap_cores(targets)

    sent = for_peers(student_hidden[0])
    got = lax.all_to_all(sent, ("y", "x"), 0, 0, tiled=True)
    teacher_rows = teacher_norm(teacher_hidden[0], teacher_gain, sent)
    waited = (teacher_rows, other_teacher_head, other_student_head, oth_targets)
    plane = plane_rows(got, student_gain, *waited)
    other_teacher_head, other_student_head = fetched(other_teacher_head), fetched(other_student_head)
    planes, sections = rings(plane, teacher_rows, (other_teacher_head, other_student_head))

    near = near_teacher(sections[:3], teacher_head, other_teacher_head)
    teacher = far_teacher(sections[3:], near, teacher_head, other_teacher_head)
    capped, early = early_rows(
        planes[: NZ - 1], student_head, other_student_head, teacher, targets
    )
    low, high = planes[NZ - 1 :]
    capped_last, sums = last_rows(
        low, high, student_head, other_student_head, teacher, targets, early
    )

    sums = jnp.sum(lax.all_to_all(sums, ("y", "x"), 0, 0, tiled=True), axis=0)
    sums = jnp.broadcast_to(sums[None], (2 * NZ, *sums.shape))
    own = collect(capped, capped_last, teacher, sums)
    other = swap_cores(own)
    own_rows, sent_rows = transposed(planes, sums)
    other_rows = swap_cores(sent_rows)
    sums = lax.all_to_all(sums, ("z", "c"), 0, 0, tiled=True)
    return gradient(sums, own, other, targets, oth_targets, own_rows, other_rows)


def solution(mesh):
    cube = mesh.devices.reshape(NY, NX, NZ, 2)
    grid = Mesh(cube, ("y", "x", "z", "c"))
    group = ("y", "x", "z")
    placed = (
        P("c", group, None),
        P("c", "y", None),
        P(),
        P(),
        P("c", group),
        P("c", group),
        P("c", None),
    )
    return jax.shard_map(
        shards,
        mesh=grid,
        in_specs=placed,
        out_specs=(P("c", group), P("c", group)),
        check_vma=False,
    )
```

time: 110 us -> 89.1 us (0.81)
  waiting for transfers between devices: 23.6 us -> 10 us
  Pallas kernels: 24.4 us -> 20.4 us
  local copies, waits for them, and re-layouts: 5.71 us -> 1.85 us
  starting transfers between devices: 32.8 us -> 35.4 us
  blocking collectives: 22.1 us -> 20.1 us
    ppermute x12, waiting for transfers between devices: 16 us -> 5.13 us  [the longest x6 3.13 us: both_ways(): lax.ppermute(low, axis, up(n, 1))]
    pallas_call x8 -> x7, Pallas kernels: 16.7 us -> 9.8 us  [call(): pl.pallas_call(body, out_shape=out_shape, in_specs=[VMEM] * len(operands)...]
    unnamed x14 -> x20, local copies, waits for them, and re-layouts: 5.56 us -> 1.82 us
    ppermute x12, starting transfers between devices: 16.8 us -> 20 us  [the longest x6 19.8 us: both_ways(): lax.ppermute(high, axis, up(n, -1))]
    pallas_call x1 -> x6, Pallas kernels: 7.7 us -> 10.6 us  [the longest x1 5.21 us: gradient(): pl.pallas_call(gradient_kernel, grid=(vocab // TILE,), out_shape=(struct(...]
    all_to_all x1, starting transfers between devices: 7.5 us -> 5.04 us  [shards(): got = lax.all_to_all(sent, ('y', 'x'), 0, 0, tiled=True)]
    all_to_all x2, blocking collectives: 22.1 us -> 20.1 us  [the longest x1 11 us: shards(): sums = lax.all_to_all(sums, ('z', 'c'), 0, 0, tiled=True)]
    ppermute x5, starting transfers between devices: 8.49 us -> 10.4 us  [swap_cores(): return lax.ppermute(value, 'c', [(0, 1), (1, 0)])]
  transfers between devices with their start and end apart: 18 -> 18, of which waited for: 7 -> 4; matrix products, arithmetic and copies ran while one was open for 0% -> 0% of each run, Pallas kernels for 12% -> 15%
where the time goes in v4:
time: 89.1 us; the launch traced here: 88.7 us
  starting transfers between devices  35.4 us (40%)
  Pallas kernels  20.4 us (23%)
  blocking collectives  20.1 us (23%)
  waiting for transfers between devices  10 us (11%)
  local copies, waits for them, and re-layouts  1.85 us (2%)
  between operations  0.9 us (1%)
    ppermute x6, starting transfers between devices, both_ways(): lax.ppermute(high, axis, up(n, -1))  19.8 us
    all_to_all x1, blocking collectives, shards(): sums = lax.all_to_all(sums, ('z', 'c'), 0, 0, tiled=True)  11 us
    ppermute x5, starting transfers between devices, swap_cores(): return lax.ppermute(value, 'c', [(0, 1), (1, 0)])  10.4 us
    pallas_call x7, Pallas kernels, call(): pl.pallas_call(body, out_shape=out_shape, in_specs=[VMEM] * len(operands)...  9.8 us
    all_to_all x1, blocking collectives, shards(): sums = jnp.sum(lax.all_to_all(sums, ('y', 'x'), 0, 0, tiled=True), axis=0)  9.07 us
    pallas_call x1, Pallas kernels, gradient(): pl.pallas_call(gradient_kernel, grid=(vocab // TILE,), out_shape=(struct(...  5.21 us
    all_to_all x1, starting transfers between devices, shards(): got = lax.all_to_all(sent, ('y', 'x'), 0, 0, tiled=True)  5.04 us
    all_to_all x1, waiting for transfers between devices, shards(): got = lax.all_to_all(sent, ('y', 'x'), 0, 0, tiled=True)  4.89 us
  transfers between devices with their start and end apart: 18, of which 4 were waited for; matrix products, arithmetic and copies ran while one was open for 0% of the time, Pallas kernels for 15%

profile of v4, /device:TPU:1, one launch (start us, length us, event | category | flops | bytes accessed | tf_op | source)
XLA Modules:
  0.0 88.7 jit_solution(7797642657795968325)
XLA Ops:
  0.6 3.3 %collective-permute-start = (bf16[2304,1024]{1,0:T(8,128)(2,1)}, bf16[2304,1024]{1,0:T(8,128)(2,1)}, u32[]{:S(2)}, u32[]{:S(2)}) collective-permute-start(bf16[2304,1024]{1,0:T(8,128)(2,1)} %own_w_ref.4), channel_id=1, source_target_pairs={{0,1},{1,0},{2,3},{3,2},{4,5},{5,4},{6,7},{7,6},{8,9},{9,8},{10,11... | collective-permute-start | bytes 14155784 | tf_op jit(solution)/shard_map/ppermute | solution.py:57
  4.0 0.1 collective-permute-start.1
  4.1 0.4 collective-permute-start.2
  4.5 0.7 copy-done.7
  5.2 0.7 shard_map.86._
  5.9 5.0 %all-to-all-start = ((bf16[16,2,3584]{2,1,0:T(2,128)(2,1)}), bf16[16,2,3584]{2,1,0:T(2,128)(2,1)S(1)}, u32[]{:S(2)}, u32[]{:S(2)}) async-start(bf16[16,2,3584]{2,1,0:T(2,128)(2,1)} %shard_map.86._), calls=%async_computation | async-start | bytes 458752 | tf_op jit(solution)/shard_map/all_to_all | solution.py:444
  10.9 0.0 copy-done.2
  10.9 0.0 copy-done.5
  11.0 0.0 copy-start.6
  11.0 0.5 shard_map.87.refs_2_.b0
  11.5 2.7 %collective-permute-start.8 = (bf16[64,4608]{1,0:T(8,128)(2,1)S(1)}, bf16[64,4608]{1,0:T(8,128)(2,1)S(1)}, u32[]{:S(2)}, u32[]{:S(2)}) collective-permute-start(bf16[64,4608]{1,0:T(8,128)(2,1)S(1)} %shard_map.87.refs_2_.b0), channel_id=1, source_target_pairs={{0,192},{64,0},{128,64},{192,128},{1,193},{65,1},{129,65},{193,129... | collective-permute-start | bytes 1769480 | tf_op jit(solution)/shard_map/ppermute | solution.py:61
  14.1 0.0 collective-permute-start.7
  14.1 0.0 collective-permute-done.2.refs_5_.oth_targets_ref
  14.1 4.9 %all-to-all-done.refs_0_ = bf16[16,2,3584]{2,1,0:T(2,128)(2,1)S(1)} async-done(((bf16[16,2,3584]{2,1,0:T(2,128)(2,1)}), bf16[16,2,3584]{2,1,0:T(2,128)(2,1)S(1)}, u32[]{:S(2)}, u32[]{:S(2)}) %all-to-all-start) | async-done | bytes 229408 | tf_op jit(solution)/shard_map/all_to_all | solution.py:444
  19.0 0.0 collective-permute-done.1.refs_4_.head
  19.0 0.0 collective-permute-done.refs_3_.head
  19.0 0.0 copy-done.6
  19.0 0.3 shard_map.88.refs_0_
  19.3 5.7 %collective-permute-start.5 = (bf16[32,3584]{1,0:T(8,128)(2,1)S(1)}, bf16[32,3584]{1,0:T(8,128)(2,1)S(1)}, u32[]{:S(2)}, u32[]{:S(2)}) collective-permute-start(bf16[32,3584]{1,0:T(8,128)(2,1)S(1)} %shard_map.88.refs_0_), channel_id=1, source_target_pairs={{0,14},{2,0},{4,2},{6,4},{8,6},{10,8},{12,10},{14,12},{1,15},{3,1}... | collective-permute-start | bytes 688136 | tf_op jit(solution)/shard_map/ppermute | solution.py:61
  25.0 0.0 collective-permute-start.3
  25.0 2.1 %shard_map.90.refs_1_.refs_8_.other_w_ref = bf16[1792,1024]{1,0:T(8,128)(2,1)S(1)} custom-call(bf16[1792,1024]{1,0:T(8,128)(2,1)} %collective-permute-done.1.refs_4_.head), custom_call_target="tpu_custom_call" | custom-call | flops 5000000000 | bytes 1024 | tf_op jit(solution)/shard_map/pallas_call | solution.py:190
  27.1 1.6 %collective-permute-done.5.refs_2_ = bf16[32,3584]{1,0:T(8,128)(2,1)S(1)} collective-permute-done((bf16[32,3584]{1,0:T(8,128)(2,1)S(1)}, bf16[32,3584]{1,0:T(8,128)(2,1)S(1)}, u32[]{:S(2)}, u32[]{:S(2)}) %collective-permute-start.5) | collective-permute-done | bytes 229408 | tf_op jit(solution)/shard_map/ppermute | solution.py:61
  28.7 3.4 %collective-permute-start.6 = (bf16[32,3584]{1,0:T(8,128)(2,1)S(1)}, bf16[32,3584]{1,0:T(8,128)(2,1)S(1)}, u32[]{:S(2)}, u32[]{:S(2)}) collective-permute-start(bf16[32,3584]{1,0:T(8,128)(2,1)S(1)} %collective-permute-done.5.refs_2_), channel_id=1, source_target_pairs={{0,14},{2,0},{4,2},{6,4},{8,6},{10,8},{12,10},{14,12},{1,15},{3,1}... | collective-permute-start | bytes 688136 | tf_op jit(solution)/shard_map/ppermute | solution.py:61
  32.1 0.0 collective-permute-done.3.refs_1_
  32.1 0.0 collective-permute-start.4
  32.1 2.5 %shard_map.89.refs_0_.other_w_ref = bf16[2304,1024]{1,0:T(8,128)(2,1)S(1)} custom-call(bf16[2304,1024]{1,0:T(8,128)(2,1)} %collective-permute-done.refs_3_.head), custom_call_target="tpu_custom_call" | custom-call | flops 5000000000 | bytes 1024 | tf_op jit(solution)/shard_map/pallas_call | solution.py:190
  34.6 0.0 slice-start.1
  34.6 0.0 collective-permute-done.8.t_high.b2
  34.7 0.0 collective-permute-done.7.t_low.b1
  34.7 0.0 copy-start.3
  34.7 0.4 collective-permute-done.6.high.refs_4_
  35.0 3.1 %collective-permute-done.4.low.refs_3_ = bf16[32,3584]{1,0:T(8,128)(2,1)S(1)} collective-permute-done((bf16[32,3584]{1,0:T(8,128)(2,1)S(1)}, bf16[32,3584]{1,0:T(8,128)(2,1)S(1)}, u32[]{:S(2)}, u32[]{:S(2)}) %collective-permute-start.4) | collective-permute-done | bytes 229408 | tf_op jit(solution)/shard_map/ppermute | solution.py:61
  38.2 0.1 shard_map.91
  38.2 0.0 copy-done.3
  38.2 0.1 collective-permute-start.9
  38.3 2.7 %collective-permute-start.11 = (bf16[32,3584]{1,0:T(8,128)(2,1)S(1)}, bf16[32,3584]{1,0:T(8,128)(2,1)S(1)}, u32[]{:S(2)}, u32[]{:S(2)}) collective-permute-start(bf16[32,3584]{1,0:T(8,128)(2,1)S(1)} %get-tuple-element.13), channel_id=1, source_target_pairs={{0,14},{2,0},{4,2},{6,4},{8,6},{10,8},{12,10},{14,12},{1,15},{3,1}... | collective-permute-start | bytes 688136 | tf_op jit(solution)/shard_map/ppermute | solution.py:61
  41.0 0.0 collective-permute-start.13
  41.0 2.7 %collective-permute-start.14 = (bf16[32,4608]{1,0:T(8,128)(2,1)S(1)}, bf16[32,4608]{1,0:T(8,128)(2,1)S(1)}, u32[]{:S(2)}, u32[]{:S(2)}) collective-permute-start(bf16[32,4608]{1,0:T(8,128)(2,1)S(1)} %get-tuple-element.15), channel_id=1, source_target_pairs={{0,192},{64,0},{128,64},{192,128},{1,193},{65,1},{129,65},{193,129... | collective-permute-start | bytes 884744 | tf_op jit(solution)/shard_map/ppermute | solution.py:61
  43.7 0.0 slice-done
  43.7 0.0 slice-done.1
  43.7 1.1 %copy-done.4 = bf16[64,4608]{1,0:T(8,128)(2,1)S(1)} copy-done((bf16[64,4608]{1,0:T(8,128)(2,1)S(1)}, bf16[64,4608]{1,0:T(8,128)(2,1)}, u32[]{:S(2)}) %copy-start.4) | copy-done | bytes 589848
  44.8 2.2 %shard_map.92.near_ref = bf16[192,1024]{1,0:T(8,128)(2,1)S(1)} custom-call(bf16[64,4608]{1,0:T(8,128)(2,1)S(1)} %shard_map.87.refs_2_.b0, bf16[64,4608]{1,0:T(8,128)(2,1)S(1)} %copy-done.4, bf16[64,4608]{1,0:T(8,128)(2,1)S(1)} %collective-permute-done.8.t_high.b2, bf16[2304,1024]{1,0:T(8,128)(2,1)S(1)} %bitcast.3, ...), custom_call_target="tpu_custom_call" | custom-call | flops 5000000000 | bytes 1024 | tf_op jit(solution)/shard_map/pallas_call | solution.py:36
  46.9 0.0 collective-permute-done.9.refs_5_
  47.0 0.1 collective-permute-start.10
  47.0 0.0 collective-permute-done.11.refs_6_
  47.1 0.0 copy-start
  47.1 0.0 copy-start.1
  47.1 2.7 %collective-permute-start.12 = (bf16[16,3584]{1,0:T(8,128)(2,1)S(1)}, bf16[16,3584]{1,0:T(8,128)(2,1)S(1)}, u32[]{:S(2)}, u32[]{:S(2)}) collective-permute-start(bf16[16,3584]{1,0:T(8,128)(2,1)S(1)} %slice.9), channel_id=1, source_target_pairs={{0,14},{2,0},{4,2},{6,4},{8,6},{10,8},{12,10},{14,12},{1,15},{3,1}... | collective-permute-start | bytes 344072 | tf_op jit(solution)/shard_map/ppermute | solution.py:61
  49.8 0.0 collective-permute-done.13.b3
  49.8 0.0 collective-permute-done.14.b4
  49.8 2.0 %shard_map.93.refs_9_.teacher_ref = bf16[256,1024]{1,0:T(8,128)(2,1)S(1)} custom-call(bf16[32,4608]{1,0:T(8,128)(2,1)S(1)} %collective-permute-done.13.b3, bf16[32,4608]{1,0:T(8,128)(2,1)S(1)} %collective-permute-done.14.b4, bf16[192,1024]{1,0:T(8,128)(2,1)S(1)} %shard_map.92.near_ref, bf16[2304,1024]{1,0:T(8,128)(2,1)S(1)} %bitcast.3, ...), custom_call_target="tpu_custom_call" | custom-call | flops 5000000000 | bytes 1024 | tf_op jit(solution)/shard_map/pallas_call | solution.py:36
  51.9 2.5 %shard_map.94 = (bf16[224,1024]{1,0:T(8,128)(2,1)S(1)}, f32[8,128]{1,0:T(8,128)S(1)}) custom-call(bf16[32,3584]{1,0:T(8,128)(2,1)S(1)} %shard_map.88.refs_0_, bf16[32,3584]{1,0:T(8,128)(2,1)S(1)} %collective-permute-done.3.refs_1_, bf16[32,3584]{1,0:T(8,128)(2,1)S(1)} %collective-permute-done.5.refs_2_, ...), custom_call_target="tpu_custom_call" | custom-call | flops 5000000000 | bytes 1024 | tf_op jit(solution)/shard_map/pallas_call | solution.py:36
  54.4 0.0 collective-permute-done.10.low.refs_7_
  54.4 0.0 collective-permute-done.12.high.refs_8_
  54.4 1.5 %shard_map.95 = (bf16[32,1024]{1,0:T(8,128)(2,1)S(1)}, f32[16,8,128]{2,1,0:T(8,128)S(1)}) custom-call(bf16[16,3584]{1,0:T(8,128)(2,1)S(1)} %collective-permute-done.10.low.refs_7_, bf16[16,3584]{1,0:T(8,128)(2,1)S(1)} %collective-permute-done.12.high.refs_8_, bf16[1792,1024]{1,0:T(8,128)(2,1)S(1)} %copy-done, ...), custom_call_target="tpu_custom_call" | custom-call | flops 1024 | bytes 1024 | tf_op jit(solution)/shard_map/pallas_call | solution.py:36
  55.9 9.1 %all_to_all.15 = f32[16,8,128]{2,1,0:T(8,128)S(1)} all-to-all(f32[16,8,128]{2,1,0:T(8,128)S(1)} %get-tuple-element.17), channel_id=1, replica_groups=mesh['y'=4,'x'=4,'z'=8,'c'=2] {'y','x'}, dimensions={0} | all-to-all | bytes 131072 | tf_op jit(solution)/shard_map/all_to_all | solution.py:461
  65.0 0.1 shard_map.96.own_ref
  65.1 6.4 %collective-permute-start.15 = (bf16[512,1024]{1,0:T(8,128)(2,1)S(1)}, bf16[512,1024]{1,0:T(8,128)(2,1)S(1)}, u32[]{:S(2)}, u32[]{:S(2)}) collective-permute-start(bf16[512,1024]{1,0:T(8,128)(2,1)S(1)} %shard_map.96.own_ref), channel_id=1, source_target_pairs={{0,1},{1,0},{2,3},{3,2},{4,5},{5,4},{6,7},{7,6},{8,9},{9,8},{10,11... | collective-permute-start | bytes 3145736 | tf_op jit(solution)/shard_map/ppermute | solution.py:57
  71.6 0.8 shard_map.97
  72.4 0.1 collective-permute-start.16
  72.5 11.0 %all_to_all.16.sums_ref = f32[16,8,128]{2,1,0:T(8,128)S(1)} all-to-all(f32[16,8,128]{2,1,0:T(8,128)S(1)} %broadcast_in_dim.2._.refs_9_), channel_id=1, replica_groups=mesh['y'=4,'x'=4,'z'=8,'c'=2] {'z','c'}, dimensions={0} | all-to-all | bytes 131072 | tf_op jit(solution)/shard_map/all_to_all | solution.py:467
  83.5 0.0 collective-permute-done.16.other_rows
  83.5 0.0 collective-permute-done.15.other_ref
  83.5 5.2 %shard_map.98 = (f32[1,2]{1,0:T(1,128)}, bf16[1792,1024]{1,0:T(8,128)(2,1)}) custom-call(f32[16,8,128]{2,1,0:T(8,128)S(1)} %all_to_all.16.sums_ref, bf16[512,1024]{1,0:T(8,128)(2,1)S(1)} %shard_map.96.own_ref, bf16[512,1024]{1,0:T(8,128)(2,1)S(1)} %collective-permute-done.15.other_ref, s32[1,256]{1,0:T(1,128)S(1)} %copy-done.1, ...), custom_call_target="tpu_custom_call" | custom-call | flops 1024 | bytes 1024 | tf_op jit(solution)/shard_map/pallas_call | solution.py:421
  (12 shorter events, 0.1 us)
Async XLA Ops:
  0.6 18.4 %collective-permute-start = (bf16[2304,1024]{1,0:T(8,128)(2,1)}, bf16[2304,1024]{1,0:T(8,128)(2,1)}, u32[]{:S(2)}, u32[]{:S(2)}) collective-permute-start(bf16[2304,1024]{1,0:T(8,128)(2,1)} %own_w_ref.4), channel_id=1, source_target_pairs={{0,1},{1,0},{2,3},{3,2},{4,5},{5,4},{6,7},{7,6},{8,9},{9,8},{10,11... | collective-permute-start | bytes 14155784 | tf_op jit(solution)/shard_map/ppermute | solution.py:57
  4.0 15.1 %collective-permute-start.1 = (bf16[1792,1024]{1,0:T(8,128)(2,1)}, bf16[1792,1024]{1,0:T(8,128)(2,1)}, u32[]{:S(2)}, u32[]{:S(2)}) collective-permute-start(bf16[1792,1024]{1,0:T(8,128)(2,1)} %own_w_ref.5), channel_id=1, source_target_pairs={{0,1},{1,0},{2,3},{3,2},{4,5},{5,4},{6,7},{7,6},{8,9},{9,8},{10,11... | collective-permute-start | bytes 11010056 | tf_op jit(solution)/shard_map/ppermute | solution.py:57
  4.1 10.1 %collective-permute-start.2 = (s32[1,256]{1,0:T(1,128)}, s32[1,256]{1,0:T(1,128)S(1)}, u32[]{:S(2)}, u32[]{:S(2)}) collective-permute-start(s32[1,256]{1,0:T(1,128)} %targets_ref.3), channel_id=1, source_target_pairs={{0,1},{1,0},{2,3},{3,2},{4,5},{5,4},{6,7},{7,6},{8,9},{9,8},{10,11... | collective-permute-start | bytes 3080 | tf_op jit(solution)/shard_map/ppermute | solution.py:57
  4.5 0.7 copy-start.7
  5.2 5.8 %copy-start.2 = (bf16[1,64,4608]{2,1,0:T(8,128)(2,1)S(1)}, bf16[1,64,4608]{2,1,0:T(8,128)(2,1)}, u32[]{:S(2)}) copy-start(bf16[1,64,4608]{2,1,0:T(8,128)(2,1)} %param.8) | copy-start | bytes 1769476
  5.2 5.8 %copy-start.5 = (f32[4608]{0:T(1024)S(1)}, f32[4608]{0:T(1024)}, u32[]{:S(2)}) copy-start(f32[4608]{0:T(1024)} %gain_ref.1) | copy-start | bytes 55300
  5.9 13.1 %all-to-all-start = ((bf16[16,2,3584]{2,1,0:T(2,128)(2,1)}), bf16[16,2,3584]{2,1,0:T(2,128)(2,1)S(1)}, u32[]{:S(2)}, u32[]{:S(2)}) async-start(bf16[16,2,3584]{2,1,0:T(2,128)(2,1)} %shard_map.86._), calls=%async_computation | async-start | bytes 458752 | tf_op jit(solution)/shard_map/all_to_all | solution.py:444
  11.0 8.1 %copy-start.6 = (f32[3584]{0:T(1024)S(1)}, f32[3584]{0:T(1024)}, u32[]{:S(2)}) copy-start(f32[3584]{0:T(1024)} %refs_1_.1) | copy-start | bytes 43012
  11.5 23.2 %collective-permute-start.8 = (bf16[64,4608]{1,0:T(8,128)(2,1)S(1)}, bf16[64,4608]{1,0:T(8,128)(2,1)S(1)}, u32[]{:S(2)}, u32[]{:S(2)}) collective-permute-start(bf16[64,4608]{1,0:T(8,128)(2,1)S(1)} %shard_map.87.refs_2_.b0), channel_id=1, source_target_pairs={{0,192},{64,0},{128,64},{192,128},{1,193},{65,1},{129,65},{193,129... | collective-permute-start | bytes 1769480 | tf_op jit(solution)/shard_map/ppermute | solution.py:61
  14.1 20.5 %collective-permute-start.7 = (bf16[64,4608]{1,0:T(8,128)(2,1)S(1)}, bf16[64,4608]{1,0:T(8,128)(2,1)S(1)}, u32[]{:S(2)}, u32[]{:S(2)}) collective-permute-start(bf16[64,4608]{1,0:T(8,128)(2,1)S(1)} %shard_map.87.refs_2_.b0), channel_id=1, source_target_pairs={{0,64},{64,128},{128,192},{192,0},{1,65},{65,129},{129,193},{193,1... | collective-permute-start | bytes 1769480 | tf_op jit(solution)/shard_map/ppermute | solution.py:61
  19.3 9.3 %collective-permute-start.5 = (bf16[32,3584]{1,0:T(8,128)(2,1)S(1)}, bf16[32,3584]{1,0:T(8,128)(2,1)S(1)}, u32[]{:S(2)}, u32[]{:S(2)}) collective-permute-start(bf16[32,3584]{1,0:T(8,128)(2,1)S(1)} %shard_map.88.refs_0_), channel_id=1, source_target_pairs={{0,14},{2,0},{4,2},{6,4},{8,6},{10,8},{12,10},{14,12},{1,15},{3,1}... | collective-permute-start | bytes 688136 | tf_op jit(solution)/shard_map/ppermute | solution.py:61
  25.0 7.1 %collective-permute-start.3 = (bf16[32,3584]{1,0:T(8,128)(2,1)S(1)}, bf16[32,3584]{1,0:T(8,128)(2,1)S(1)}, u32[]{:S(2)}, u32[]{:S(2)}) collective-permute-start(bf16[32,3584]{1,0:T(8,128)(2,1)S(1)} %shard_map.88.refs_0_), channel_id=1, source_target_pairs={{0,2},{2,4},{4,6},{6,8},{8,10},{10,12},{12,14},{14,0},{1,3},{3,5},... | collective-permute-start | bytes 688136 | tf_op jit(solution)/shard_map/ppermute | solution.py:61
  28.7 6.4 %collective-permute-start.6 = (bf16[32,3584]{1,0:T(8,128)(2,1)S(1)}, bf16[32,3584]{1,0:T(8,128)(2,1)S(1)}, u32[]{:S(2)}, u32[]{:S(2)}) collective-permute-start(bf16[32,3584]{1,0:T(8,128)(2,1)S(1)} %collective-permute-done.5.refs_2_), channel_id=1, source_target_pairs={{0,14},{2,0},{4,2},{6,4},{8,6},{10,8},{12,10},{14,12},{1,15},{3,1}... | collective-permute-start | bytes 688136 | tf_op jit(solution)/shard_map/ppermute | solution.py:61
  32.1 6.1 %collective-permute-start.4 = (bf16[32,3584]{1,0:T(8,128)(2,1)S(1)}, bf16[32,3584]{1,0:T(8,128)(2,1)S(1)}, u32[]{:S(2)}, u32[]{:S(2)}) collective-permute-start(bf16[32,3584]{1,0:T(8,128)(2,1)S(1)} %collective-permute-done.3.refs_1_), channel_id=1, source_target_pairs={{0,2},{2,4},{4,6},{6,8},{8,10},{10,12},{12,14},{14,0},{1,3},{3,5},... | collective-permute-start | bytes 688136 | tf_op jit(solution)/shard_map/ppermute | solution.py:61
  32.1 11.6 %slice-start = ((s8[4718592]{0:T(1024)(128)(4,1)}), s8[4194304]{0:T(1024)(128)(4,1)S(1)}, s32[]{:S(2)}) async-start(s8[4718592]{0:T(1024)(128)(4,1)} %bitcast.2), calls=%async_computation.3 | async-start | bytes 8388608
  34.6 9.1 %slice-start.1 = ((s8[4718592]{0:T(1024)(128)(4,1)}), s8[524288]{0:T(1024)(128)(4,1)S(1)}, s32[]{:S(2)}) async-start(s8[4718592]{0:T(1024)(128)(4,1)} %bitcast.2), calls=%async_computation.4 | async-start | bytes 1048576
  34.7 3.6 %copy-start.3 = (bf16[64,4608]{1,0:T(8,128)(2,1)}, bf16[64,4608]{1,0:T(8,128)(2,1)S(1)}, u32[]{:S(2)}) copy-start(bf16[64,4608]{1,0:T(8,128)(2,1)S(1)} %collective-permute-done.7.t_low.b1) | copy-start | bytes 1769476
  38.2 8.7 %collective-permute-start.9 = (bf16[32,3584]{1,0:T(8,128)(2,1)S(1)}, bf16[32,3584]{1,0:T(8,128)(2,1)S(1)}, u32[]{:S(2)}, u32[]{:S(2)}) collective-permute-start(bf16[32,3584]{1,0:T(8,128)(2,1)S(1)} %get-tuple-element.12), channel_id=1, source_target_pairs={{0,2},{2,4},{4,6},{6,8},{8,10},{10,12},{12,14},{14,0},{1,3},{3,5},... | collective-permute-start | bytes 688136 | tf_op jit(solution)/shard_map/ppermute | solution.py:61
  38.3 8.7 %collective-permute-start.11 = (bf16[32,3584]{1,0:T(8,128)(2,1)S(1)}, bf16[32,3584]{1,0:T(8,128)(2,1)S(1)}, u32[]{:S(2)}, u32[]{:S(2)}) collective-permute-start(bf16[32,3584]{1,0:T(8,128)(2,1)S(1)} %get-tuple-element.13), channel_id=1, source_target_pairs={{0,14},{2,0},{4,2},{6,4},{8,6},{10,8},{12,10},{14,12},{1,15},{3,1}... | collective-permute-start | bytes 688136 | tf_op jit(solution)/shard_map/ppermute | solution.py:61
  41.0 8.8 %collective-permute-start.13 = (bf16[32,4608]{1,0:T(8,128)(2,1)S(1)}, bf16[32,4608]{1,0:T(8,128)(2,1)S(1)}, u32[]{:S(2)}, u32[]{:S(2)}) collective-permute-start(bf16[32,4608]{1,0:T(8,128)(2,1)S(1)} %get-tuple-element.14), channel_id=1, source_target_pairs={{0,64},{64,128},{128,192},{192,0},{1,65},{65,129},{129,193},{193,1... | collective-permute-start | bytes 884744 | tf_op jit(solution)/shard_map/ppermute | solution.py:61
  41.0 8.8 %collective-permute-start.14 = (bf16[32,4608]{1,0:T(8,128)(2,1)S(1)}, bf16[32,4608]{1,0:T(8,128)(2,1)S(1)}, u32[]{:S(2)}, u32[]{:S(2)}) collective-permute-start(bf16[32,4608]{1,0:T(8,128)(2,1)S(1)} %get-tuple-element.15), channel_id=1, source_target_pairs={{0,192},{64,0},{128,64},{192,128},{1,193},{65,1},{129,65},{193,129... | collective-permute-start | bytes 884744 | tf_op jit(solution)/shard_map/ppermute | solution.py:61
  43.7 1.1 %copy-start.4 = (bf16[64,4608]{1,0:T(8,128)(2,1)S(1)}, bf16[64,4608]{1,0:T(8,128)(2,1)}, u32[]{:S(2)}) copy-start(bf16[64,4608]{1,0:T(8,128)(2,1)} %copy-done.3) | copy-start | bytes 1769476
  47.0 7.4 %collective-permute-start.10 = (bf16[16,3584]{1,0:T(8,128)(2,1)S(1)}, bf16[16,3584]{1,0:T(8,128)(2,1)S(1)}, u32[]{:S(2)}, u32[]{:S(2)}) collective-permute-start(bf16[16,3584]{1,0:T(8,128)(2,1)S(1)} %slice.8), channel_id=1, source_target_pairs={{0,2},{2,4},{4,6},{6,8},{8,10},{10,12},{12,14},{14,0},{1,3},{3,5},... | collective-permute-start | bytes 344072 | tf_op jit(solution)/shard_map/ppermute | solution.py:61
  47.1 4.8 %copy-start = (bf16[1792,1024]{1,0:T(8,128)(2,1)S(1)}, bf16[1792,1024]{1,0:T(8,128)(2,1)}, u32[]{:S(2)}) copy-start(bf16[1792,1024]{1,0:T(8,128)(2,1)} %own_w_ref.5) | copy-start | bytes 11010052
  47.1 4.8 %copy-start.1 = (s32[1,256]{1,0:T(1,128)S(1)}, s32[1,256]{1,0:T(1,128)}, u32[]{:S(2)}) copy-start(s32[1,256]{1,0:T(1,128)} %targets_ref.3) | copy-start | bytes 3076
  47.1 7.3 %collective-permute-start.12 = (bf16[16,3584]{1,0:T(8,128)(2,1)S(1)}, bf16[16,3584]{1,0:T(8,128)(2,1)S(1)}, u32[]{:S(2)}, u32[]{:S(2)}) collective-permute-start(bf16[16,3584]{1,0:T(8,128)(2,1)S(1)} %slice.9), channel_id=1, source_target_pairs={{0,14},{2,0},{4,2},{6,4},{8,6},{10,8},{12,10},{14,12},{1,15},{3,1}... | collective-permute-start | bytes 344072 | tf_op jit(solution)/shard_map/ppermute | solution.py:61
  65.1 18.4 %collective-permute-start.15 = (bf16[512,1024]{1,0:T(8,128)(2,1)S(1)}, bf16[512,1024]{1,0:T(8,128)(2,1)S(1)}, u32[]{:S(2)}, u32[]{:S(2)}) collective-permute-start(bf16[512,1024]{1,0:T(8,128)(2,1)S(1)} %shard_map.96.own_ref), channel_id=1, source_target_pairs={{0,1},{1,0},{2,3},{3,2},{4,5},{5,4},{6,7},{7,6},{8,9},{9,8},{10,11... | collective-permute-start | bytes 3145736 | tf_op jit(solution)/shard_map/ppermute | solution.py:57
  72.4 11.1 %collective-permute-start.16 = (bf16[1792,256]{1,0:T(8,128)(2,1)S(1)}, bf16[1792,256]{1,0:T(8,128)(2,1)S(1)}, u32[]{:S(2)}, u32[]{:S(2)}) collective-permute-start(bf16[1792,256]{1,0:T(8,128)(2,1)S(1)} %get-tuple-element.21), channel_id=1, source_target_pairs={{0,1},{1,0},{2,3},{3,2},{4,5},{5,4},{6,7},{7,6},{8,9},{9,8},{10,11... | collective-permute-start | bytes 2752520 | tf_op jit(solution)/shard_map/ppermute | solution.py:57

commit v5 on v4

v5 whole, which is shorter than its diff:
```python
import jax
import jax.numpy as jnp
from jax import lax
from jax.experimental import pallas as pl
from jax.experimental.pallas import tpu as pltpu
from jax.sharding import Mesh, PartitionSpec as P

F32 = jnp.float32
BF16 = jnp.bfloat16
I32 = jnp.int32
NY, NX, NZ = 4, 4, 8
ROWS = 2
PLANE = NY * NX * ROWS
OWN = NZ * PLANE
EARLY = OWN - PLANE
STEP = 32
TILE = 256
PARTS = 8
LANES = 128
VMEM = pl.BlockSpec(memory_space=pltpu.VMEM)
ANY = pl.BlockSpec(memory_space=pl.ANY)
SHORT = pl.CostEstimate(flops=1024, bytes_accessed=1024, transcendentals=0)
LONG = pl.CostEstimate(flops=5_000_000_000, bytes_accessed=1024, transcendentals=0)


def params(mebibytes=8):
    return pltpu.CompilerParams(vmem_limit_bytes=mebibytes * 1024 * 1024)


def struct(shape, dtype):
    return jax.ShapeDtypeStruct(shape, dtype)


def call(body, out_shape, operands, scratch=(), cost=SHORT):
    several = isinstance(out_shape, tuple)
    return pl.pallas_call(
        body,
        out_shape=out_shape,
        in_specs=[VMEM] * len(operands),
        out_specs=(VMEM,) * len(out_shape) if several else VMEM,
        scratch_shapes=scratch,
        compiler_params=params(),
        cost_estimate=cost,
    )(*operands)


def each(count, width, body):
    for index in range(count):
        body(index * width)


def up(n, k):
    return [(i, (i + k) % n) for i in range(n)]


def swap_cores(value):
    return lax.ppermute(value, "c", [(0, 1), (1, 0)])


def both_ways(low, high, axis, n):
    return lax.ppermute(low, axis, up(n, 1)), lax.ppermute(high, axis, up(n, -1))


def gate_kernel(low, high, rows, t_low, t_high, *refs):
    low_out, high_out, t_low_out, t_high_out, near_out = refs[-5:]
    for index, block in enumerate((rows, t_low, t_high)):
        near_out[pl.ds(index * rows.shape[0], rows.shape[0])] = block[...]
    low_out[...] = low[...]
    high_out[...] = high[...]
    half = t_low_out.shape[0]
    t_low_out[...] = t_low[:half]
    t_high_out[...] = t_high[half:]


def gate(low, high, rows, t_low, t_high, *others):
    part = struct((t_low.shape[0] // 2, t_low.shape[1]), BF16)
    near = struct((3 * t_low.shape[0], t_low.shape[1]), BF16)
    plane = struct(low.shape, BF16)
    return pl.pallas_call(
        gate_kernel,
        out_shape=(plane, plane, part, part, near),
        in_specs=[VMEM] * 5 + [ANY] * len(others),
        out_specs=(VMEM,) * 5,
        compiler_params=params(4),
        cost_estimate=LONG,
    )(low, high, rows, t_low, t_high, *others)


def rings(plane, rows, others):
    t_low, t_high = both_ways(rows, rows, "y", NY)
    planes = [plane]
    low = high = plane
    for step in range(NZ // 2 - 1):
        if step == 2:
            low, high, t_low_half, t_high_half, near = gate(low, high, rows, t_low, t_high, *others)
        low, high = both_ways(low, high, "z", NZ)
        planes += [low, high]
    far = both_ways(t_low_half, t_high_half, "y", NY)
    half = plane.shape[0] // 2
    planes += both_ways(low[:half], high[half:], "z", NZ)
    return planes, near, far


def distance(position):
    return jnp.where(position % 2 == 1, NZ - (position + 1) // 2, position // 2)


def natural_row(row, z):
    position, inner = row // PLANE, row % PLANE
    y, x, i = inner // (NX * ROWS), inner // ROWS % NX, inner % ROWS
    return ((y * NX + x) * NZ + (z + distance(position)) % NZ) * ROWS + i


def iota(shape, axis):
    return lax.broadcasted_iota(I32, shape, axis)


def normalize(hidden, gain):
    values = hidden.astype(F32)
    spread = jnp.mean(values * values, axis=-1, keepdims=True)
    return (values * lax.rsqrt(spread + 1e-06) * gain.reshape(1, -1)).astype(BF16)


def peers_kernel(hidden_ref, out_ref):
    for peer in range(out_ref.shape[0]):
        out_ref[peer] = hidden_ref[...]


def for_peers(hidden):
    out = struct((NY * NX, *hidden.shape), BF16)
    return call(peers_kernel, out, (hidden,), cost=LONG)


def plane_kernel(*refs):
    got_ref, gain_ref, *_, out_ref, rows_ref = refs
    for peer in range(NY * NX):
        rows_ref[pl.ds(peer * ROWS, ROWS)] = got_ref[peer].astype(F32)
    out_ref[...] = normalize(rows_ref[...], gain_ref[...])


def plane_rows(got, gain, *others):
    shape = (PLANE, got.shape[2])
    return pl.pallas_call(
        plane_kernel,
        out_shape=struct(shape, BF16),
        in_specs=[VMEM, VMEM] + [ANY] * len(others),
        out_specs=VMEM,
        scratch_shapes=[pltpu.VMEM(shape, F32)],
        compiler_params=params(),
        cost_estimate=LONG,
    )(got, gain, *others)


def teacher_norm_kernel(hidden_ref, gain_ref, _, out_ref):
    z = lax.axis_index("z")
    normed = normalize(hidden_ref[...], gain_ref[...])
    n = normed.shape[0]
    row = iota((n, n), 0)
    position, x, i = row // (NX * ROWS), row // ROWS % NX, row % ROWS
    source = (x * NZ + (z + distance(position)) % NZ) * ROWS + i
    moved = jnp.where(iota((n, n), 1) == source, 1.0, 0.0).astype(BF16)
    out_ref[...] = jnp.dot(moved, normed, preferred_element_type=F32).astype(BF16)


def teacher_norm(hidden, gain, other):
    return pl.pallas_call(
        teacher_norm_kernel,
        out_shape=struct(hidden.shape, BF16),
        in_specs=[VMEM, VMEM, ANY],
        out_specs=VMEM,
        compiler_params=params(),
        cost_estimate=LONG,
    )(hidden, gain, other)


def halves(ref_width):
    k, core = ref_width // 2, lax.axis_index("c")
    return tuple(pl.ds(pl.multiple_of(half * k, LANES), k) for half in (core, 1 - core))


def fetch_kernel(head, out_ref, sem):
    part = head.shape[0] // PARTS
    copies = []
    for index in range(PARTS):
        rows = pl.ds(index * part, part)
        copies.append(pltpu.make_async_copy(head.at[rows], out_ref.at[rows], sem.at[index]))
        copies[-1].start()
    for copy in copies:
        copy.wait()


def fetched(head):
    return pl.pallas_call(
        fetch_kernel,
        out_shape=struct(head.shape, head.dtype),
        in_specs=[ANY],
        out_specs=VMEM,
        scratch_shapes=[pltpu.SemaphoreType.DMA((PARTS,))],
        compiler_params=params(4),
        cost_estimate=LONG,
    )(head)


def logits(rows_ref, own_w_ref, other_w_ref, out_ref):
    own, other = halves(rows_ref.shape[1])
    for at in range(0, out_ref.shape[1], TILE):
        columns = pl.ds(at, TILE)
        out_ref[:, columns] = soft_cap(
            jnp.dot(rows_ref[:, own], own_w_ref[:, columns], preferred_element_type=F32)
            + jnp.dot(rows_ref[:, other], other_w_ref[:, columns], preferred_element_type=F32)
        )


def soft_cap(logits):
    return (30.0 * jnp.tanh(logits / 30.0)).astype(BF16)


def near_teacher_kernel(rows_ref, own_w_ref, other_w_ref, out_ref):
    logits(rows_ref, own_w_ref, other_w_ref, out_ref)


def near_teacher(rows, own_head, other_head):
    out = struct((rows.shape[0], own_head.shape[1]), BF16)
    return call(near_teacher_kernel, out, (rows, own_head, other_head), cost=LONG)


def local_targets(targets_ref, z, first, rows):
    shape = (rows.shape[0], OWN)
    here = iota(shape, 1) == natural_row(rows, z)
    return jnp.sum(jnp.where(here, targets_ref[...], 0), axis=1, keepdims=True) - first


def first_column(vocab):
    y, x, z = lax.axis_index("y"), lax.axis_index("x"), lax.axis_index("z")
    return ((y * NX + x) * NZ + z) * vocab


def fold(values):
    total = values[:, :LANES]
    for start in range(LANES, values.shape[1], LANES):
        total = total + values[:, start : start + LANES]
    return total


def folded(totals):
    return [jnp.concatenate(parts, axis=0) if parts else None for parts in totals]


def tile_of(totals, start):
    z = lax.axis_index("z")
    rows = []
    for total in folded(totals):
        if total is None:
            flat = jnp.zeros((1, OWN), F32)
        else:
            n = total.shape[0]
            here = iota((n, OWN), 1) == natural_row(iota((n, OWN), 0) + start, z)
            column = jnp.sum(total, axis=1, keepdims=True)
            flat = jnp.sum(jnp.where(here, column, 0.0), axis=0, keepdims=True)
        rows += [flat[:, at : at + LANES] for at in range(0, OWN, LANES)]
    return jnp.concatenate(rows, axis=0)


def add_student(totals, start, capped_ref, targets_ref):
    n, vocab = capped_ref.shape
    z, first = lax.axis_index("z"), first_column(vocab)
    for at in range(0, n, STEP):
        stud_vals = capped_ref[pl.ds(at, STEP)].astype(F32)
        target = local_targets(targets_ref, z, first, iota((STEP, 1), 0) + (start + at))
        hit = iota((STEP, vocab), 1) == target
        totals[1].append(fold(jnp.exp(stud_vals)))
        totals[3].append(fold(jnp.where(hit, stud_vals, 0.0)))


def add_teacher(totals, start, stop, teacher_ref, capped_ref):
    for at in range(start, stop, STEP):
        teach_vals = teacher_ref[pl.ds(at, STEP)].astype(F32)
        teach_exp = jnp.exp(teach_vals)
        totals[0].append(fold(teach_exp))
        if at - start < capped_ref.shape[0]:
            stud_vals = capped_ref[pl.ds(at - start, STEP)].astype(F32)
            totals[2].append(fold(teach_exp * (teach_vals - stud_vals)))


def early_kernel(*refs):
    *blocks, own_w_ref, other_w_ref, targets_ref, capped_ref, sums_ref, rows_ref = refs
    for q, block in enumerate(blocks):
        rows_ref[pl.ds(q * PLANE, PLANE)] = block[...]
    logits(rows_ref, own_w_ref, other_w_ref, capped_ref)
    totals = [[], [], [], []]
    add_student(totals, 0, capped_ref, targets_ref)
    sums_ref[...] = tile_of(totals, 0)


def early_rows(planes, own_head, other_head, targets):
    k, vocab = own_head.shape
    out = (struct((EARLY, vocab), BF16), struct((8, LANES), F32))
    scratch = [pltpu.VMEM((EARLY, 2 * k), BF16)]
    return call(early_kernel, out, (*planes, own_head, other_head, targets), scratch, LONG)


def far_teacher_kernel(
    b3, b4, near_ref, own_w_ref, other_w_ref, capped_ref, early_ref,
    out_ref, sums_ref, rows_ref, far_ref,
):
    rows_ref[...] = jnp.concatenate([b3[...], b4[...]])
    logits(rows_ref, own_w_ref, other_w_ref, far_ref)
    section = rows_ref.shape[0]
    y = lax.axis_index("y")
    row = iota((OWN, OWN), 0)
    position, inner = row // PLANE, row % PLANE
    apart = (inner // (NX * ROWS) - y) % NY
    place = jnp.where(apart == 0, 0, jnp.where(apart == NY - 1, 1, jnp.where(apart == 1, 2, 3)))
    source = place * section + position * (NX * ROWS) + inner % (NX * ROWS)
    moved = jnp.where(iota((OWN, OWN), 1) == source, 1.0, 0.0).astype(BF16)
    whole = jnp.concatenate([near_ref[...], far_ref[...]])
    out_ref[...] = jnp.dot(moved, whole, preferred_element_type=F32).astype(BF16)
    totals = [[], [], [], []]
    add_teacher(totals, 0, EARLY, out_ref, capped_ref)
    sums_ref[...] = early_ref[...] + tile_of(totals, 0)


def far_teacher(blocks, near, own_head, other_head, capped, early):
    k, vocab = own_head.shape
    n = OWN - near.shape[0]
    scratch = [pltpu.VMEM((n, 2 * k), BF16), pltpu.VMEM((n, vocab), BF16)]
    out = (struct((OWN, vocab), BF16), struct((8, LANES), F32))
    operands = (*blocks, near, own_head, other_head, capped, early)
    return call(far_teacher_kernel, out, operands, scratch, LONG)


def last_kernel(
    low, high, own_w_ref, other_w_ref, teacher_ref, targets_ref, sums_ref,
    capped_ref, out_ref, rows_ref,
):
    rows_ref[...] = jnp.concatenate([low[...], high[...]])
    logits(rows_ref, own_w_ref, other_w_ref, capped_ref)
    totals = [[], [], [], []]
    add_student(totals, EARLY, capped_ref, targets_ref)
    add_teacher(totals, EARLY, OWN, teacher_ref, capped_ref)
    tile = sums_ref[...] + tile_of(totals, EARLY)
    for peer in range(out_ref.shape[0]):
        out_ref[peer] = tile


def last_rows(low, high, own_head, other_head, teacher, targets, sums):
    k, vocab = own_head.shape
    out = (struct((PLANE, vocab), BF16), struct((NY * NX, 8, LANES), F32))
    operands = (low, high, own_head, other_head, teacher, targets, sums)
    return call(last_kernel, out, operands, [pltpu.VMEM((PLANE, 2 * k), BF16)])


def collect_kernel(early_ref, last_ref, teacher_ref, _, out_ref):
    out_ref[:EARLY] = early_ref[...]
    out_ref[EARLY:OWN] = last_ref[...]
    out_ref[OWN:] = teacher_ref[...]


def collect(early, last, teacher, sums):
    out = struct((2 * OWN, teacher.shape[1]), BF16)
    return call(collect_kernel, out, (early, last, teacher, sums))


def transpose_kernel(*refs):
    *blocks, low, high, _, keep_ref, send_ref, rows_ref = refs
    for q, block in enumerate(blocks):
        rows_ref[pl.ds(q * PLANE, PLANE)] = block[...]
    rows_ref[EARLY:] = jnp.concatenate([low[...], high[...]])
    k, core = keep_ref.shape[0], lax.axis_index("c")

    def turn(at):
        for ref, half in ((keep_ref, core), (send_ref, 1 - core)):
            columns = pl.ds(pl.multiple_of(half * k + at, LANES), TILE)
            ref[pl.ds(at, TILE)] = rows_ref[:, columns].T

    each(k // TILE, TILE, turn)


def transposed(blocks, sums):
    width = blocks[0].shape[1]
    out = struct((width // 2, OWN), BF16)
    scratch = [pltpu.VMEM((OWN, width), BF16)]
    return call(transpose_kernel, (out, out), (*blocks, sums), scratch)


def gradient_kernel(
    sums_ref, own_ref, other_ref, targets_ref, oth_targets_ref, own_rows, other_rows,
    loss_ref, out, scale_ref, target_ref, grad_ref, out_ref, sems,
):
    vocab = own_ref.shape[1]

    z, core = lax.axis_index("z"), lax.axis_index("c")
    position = (lax.axis_index("y") * NX + lax.axis_index("x")) * NZ + z
    here = iota((OWN, OWN), 1) == natural_row(iota((OWN, OWN), 0), z)
    totals = []
    for side in range(2):
        total = sums_ref[side]
        for peer in range(1, NZ):
            total = total + sums_ref[2 * peer + side]
        totals.append(total)
    own = jnp.where(core == 0, totals[0], totals[1])
    other = jnp.where(core == 0, totals[1], totals[0])

    def flat(tile, kind):
        first, second = tile[2 * kind : 2 * kind + 1], tile[2 * kind + 1 : 2 * kind + 2]
        return jnp.concatenate([first, second], axis=1)

    teach_total, stud_total, cross_sum, target_logit = (flat(own, k) for k in range(4))
    loss = cross_sum / teach_total - jnp.log(teach_total) + 2.0 * jnp.log(stud_total) - target_logit
    lane = iota((1, OWN), 1)
    picked = [
        jnp.sum(jnp.where(lane == position * ROWS + i, loss, 0.0), axis=1, keepdims=True)
        for i in range(ROWS)
    ]
    loss_ref[...] = jnp.concatenate(picked, axis=1)
    first = first_column(vocab)
    for side, tile, targets in ((0, own, targets_ref), (1, other, oth_targets_ref)):
        rows = pl.ds(side * OWN, OWN)
        target = local_targets(targets, z, first, iota((OWN, 1), 0))
        target_ref[rows] = jnp.broadcast_to(target, (OWN, LANES))
        for kind, value in ((0, 1.0 / flat(tile, 0)), (1, 2.0 / flat(tile, 1))):
            column = jnp.sum(jnp.where(here, value, 0.0), axis=1, keepdims=True)
            scale_ref[kind, rows] = jnp.broadcast_to(column, (OWN, LANES))

    for start in range(0, vocab, TILE):
        columns = pl.ds(start, TILE)
        for side, values in ((0, own_ref), (1, other_ref)):
            rows = pl.ds(side * OWN, OWN)
            teach_scale, stud_scale = (scale_ref[kind, rows, :1] for kind in range(2))
            stud_vals = values[:OWN, columns].astype(F32)
            teach_vals = values[OWN:, columns].astype(F32)
            scaled = jnp.exp(stud_vals) * stud_scale - jnp.exp(teach_vals) * teach_scale
            hit = iota((OWN, TILE), 1) == target_ref[rows, :1] - start
            scaled = scaled - jnp.where(hit, 1.0, 0.0)
            value = scaled * (1.0 - stud_vals * stud_vals * (1.0 / 900.0))
            grad_ref[rows, columns] = value.astype(BF16)
    k = out_ref.shape[0]
    parts = [(0, k, start) for start in range(0, vocab - TILE, TILE)]
    parts += [(at, k // 2, vocab - TILE) for at in (0, k // 2)]
    copies = []
    for index, (at, count, start) in enumerate(parts):
        rows, columns = pl.ds(at, count), pl.ds(start, TILE)
        out_ref[rows, columns] = (
            jnp.dot(own_rows[rows], grad_ref[:OWN, columns], preferred_element_type=F32)
            + jnp.dot(other_rows[rows], grad_ref[OWN:, columns], preferred_element_type=F32)
        ).astype(BF16)
        copies.append(
            pltpu.make_async_copy(out_ref.at[rows, columns], out.at[rows, columns], sems.at[index])
        )
        copies[-1].start()
    for copy in copies:
        copy.wait()


def gradient(sums, own, other, targets, oth_targets, own_rows, other_rows):
    k, vocab = own_rows.shape[0], own.shape[1]
    operands = (sums, own, other, targets, oth_targets, own_rows, other_rows)
    return pl.pallas_call(
        gradient_kernel,
        out_shape=(struct((1, ROWS), F32), struct((k, vocab), BF16)),
        in_specs=[VMEM] * len(operands),
        out_specs=(VMEM, ANY),
        scratch_shapes=[
            pltpu.VMEM((2, 2 * OWN, LANES), F32),
            pltpu.VMEM((2 * OWN, LANES), I32),
            pltpu.VMEM((2 * OWN, vocab), BF16),
            pltpu.VMEM((k, vocab), BF16),
            pltpu.SemaphoreType.DMA((vocab // TILE + 1,)),
        ],
        compiler_params=params(12),
        cost_estimate=SHORT,
    )(*operands)


def shards(
    student_hidden, teacher_hidden, student_gain, teacher_gain, student_head, teacher_head, targets
):
    other_teacher_head = swap_cores(teacher_head)
    other_student_head = swap_cores(student_head)
    oth_targets = swap_cores(targets)

    sent = for_peers(student_hidden[0])
    got = lax.all_to_all(sent, ("y", "x"), 0, 0, tiled=True)
    teacher_rows = teacher_norm(teacher_hidden[0], teacher_gain, sent)
    waited = (teacher_rows, other_teacher_head, other_student_head, oth_targets)
    plane = plane_rows(got, student_gain, *waited)
    other_teacher_head, other_student_head = fetched(other_teacher_head), fetched(other_student_head)
    planes, near, far = rings(plane, teacher_rows, (other_teacher_head, other_student_head))

    near = near_teacher(near, teacher_head, other_teacher_head)
    capped, early = early_rows(planes[: NZ - 1], student_head, other_student_head, targets)
    teacher, early = far_teacher(far, near, teacher_head, other_teacher_head, capped, early)
    low, high = planes[NZ - 1 :]
    capped_last, sums = last_rows(
        low, high, student_head, other_student_head, teacher, targets, early
    )

    sums = jnp.sum(lax.all_to_all(sums, ("y", "x"), 0, 0, tiled=True), axis=0)
    sums = jnp.broadcast_to(sums[None], (2 * NZ, *sums.shape))
    own = collect(capped, capped_last, teacher, sums)
    other = swap_cores(own)
    own_rows, sent_rows = transposed(planes, sums)
    other_rows = swap_cores(sent_rows)
    sums = lax.all_to_all(sums, ("z", "c"), 0, 0, tiled=True)
    return gradient(sums, own, other, targets, oth_targets, own_rows, other_rows)


def solution(mesh):
    cube = mesh.devices.reshape(NY, NX, NZ, 2)
    grid = Mesh(cube, ("y", "x", "z", "c"))
    group = ("y", "x", "z")
    placed = (
        P("c", group, None),
        P("c", "y", None),
        P(),
        P(),
        P("c", group),
        P("c", group),
        P("c", None),
    )
    return jax.shard_map(
        shards,
        mesh=grid,
        in_specs=placed,
        out_specs=(P("c", group), P("c", group)),
        check_vma=False,
    )
```

time: 89.1 us -> 88 us (0.988)
  local copies, waits for them, and re-layouts: 1.85 us -> 0.77 us
    unnamed x20 -> x16, local copies, waits for them, and re-layouts: 1.82 us -> 0.75 us
where the time goes in v5:
time: 88 us; the launch traced here: 87.7 us
  starting transfers between devices  35.4 us (40%)
  Pallas kernels  20.2 us (23%)
  blocking collectives  20.1 us (23%)
  waiting for transfers between devices  10 us (11%)
  between operations  1.06 us (1%)
    ppermute x6, starting transfers between devices, both_ways(): lax.ppermute(high, axis, up(n, -1))  19.8 us
    all_to_all x1, blocking collectives, shards(): sums = lax.all_to_all(sums, ('z', 'c'), 0, 0, tiled=True)  11 us
    ppermute x5, starting transfers between devices, swap_cores(): return lax.ppermute(value, 'c', [(0, 1), (1, 0)])  10.4 us
    pallas_call x7, Pallas kernels, call(): pl.pallas_call(body, out_shape=out_shape, in_specs=[VMEM] * len(operands)...  9.8 us
    all_to_all x1, blocking collectives, shards(): sums = jnp.sum(lax.all_to_all(sums, ('y', 'x'), 0, 0, tiled=True), axis=0)  9.07 us
    all_to_all x1, starting transfers between devices, shards(): got = lax.all_to_all(sent, ('y', 'x'), 0, 0, tiled=True)  5.04 us
    pallas_call x1, Pallas kernels, gradient(): pl.pallas_call(gradient_kernel, out_shape=(struct((1, ROWS), F32), struct...  4.9 us
    all_to_all x1, waiting for transfers between devices, shards(): got = lax.all_to_all(sent, ('y', 'x'), 0, 0, tiled=True)  4.89 us
  transfers between devices with their start and end apart: 18, of which 4 were waited for; matrix products, arithmetic and copies ran while one was open for 0% of the time, Pallas kernels for 15%

profile of v5, /device:TPU:1, one launch (start us, length us, event | category | flops | bytes accessed | tf_op | source)
XLA Modules:
  0.0 87.7 jit_solution(9797481669702062607)
XLA Ops:
  0.6 3.3 %collective-permute-start = (bf16[2304,1024]{1,0:T(8,128)(2,1)}, bf16[2304,1024]{1,0:T(8,128)(2,1)}, u32[]{:S(2)}, u32[]{:S(2)}) collective-permute-start(bf16[2304,1024]{1,0:T(8,128)(2,1)} %own_w_ref.4), channel_id=1, source_target_pairs={{0,1},{1,0},{2,3},{3,2},{4,5},{5,4},{6,7},{7,6},{8,9},{9,8},{10,11... | collective-permute-start | bytes 14155784 | tf_op jit(solution)/shard_map/ppermute | solution.py:57
  4.0 0.1 collective-permute-start.1
  4.1 0.4 collective-permute-start.2
  4.5 0.0 copy-start.5
  4.5 0.7 copy-done.5
  5.2 0.0 copy-start.2
  5.2 0.7 shard_map.86._
  5.9 5.0 %all-to-all-start = ((bf16[16,2,3584]{2,1,0:T(2,128)(2,1)}), bf16[16,2,3584]{2,1,0:T(2,128)(2,1)S(1)}, u32[]{:S(2)}, u32[]{:S(2)}) async-start(bf16[16,2,3584]{2,1,0:T(2,128)(2,1)} %shard_map.86._), calls=%async_computation | async-start | bytes 458752 | tf_op jit(solution)/shard_map/all_to_all | solution.py:483
  10.9 0.0 copy-done.2
  10.9 0.0 copy-done.3
  11.0 0.0 copy-start.4
  11.0 0.5 shard_map.87.refs_2_.rows
  11.5 2.7 %collective-permute-start.8 = (bf16[64,4608]{1,0:T(8,128)(2,1)S(1)}, bf16[64,4608]{1,0:T(8,128)(2,1)S(1)}, u32[]{:S(2)}, u32[]{:S(2)}) collective-permute-start(bf16[64,4608]{1,0:T(8,128)(2,1)S(1)} %shard_map.87.refs_2_.rows), channel_id=1, source_target_pairs={{0,192},{64,0},{128,64},{192,128},{1,193},{65,1},{129,65},{193,129... | collective-permute-start | bytes 1769480 | tf_op jit(solution)/shard_map/ppermute | solution.py:61
  14.1 0.0 collective-permute-start.7
  14.1 0.0 collective-permute-done.2.refs_5_.oth_targets_ref
  14.1 4.9 %all-to-all-done.refs_0_ = bf16[16,2,3584]{2,1,0:T(2,128)(2,1)S(1)} async-done(((bf16[16,2,3584]{2,1,0:T(2,128)(2,1)}), bf16[16,2,3584]{2,1,0:T(2,128)(2,1)S(1)}, u32[]{:S(2)}, u32[]{:S(2)}) %all-to-all-start) | async-done | bytes 229408 | tf_op jit(solution)/shard_map/all_to_all | solution.py:483
  19.0 0.0 collective-permute-done.1.refs_4_.head
  19.0 0.0 collective-permute-done.refs_3_.head
  19.0 0.0 copy-done.4
  19.0 0.3 shard_map.88.refs_0_
  19.3 5.7 %collective-permute-start.5 = (bf16[32,3584]{1,0:T(8,128)(2,1)S(1)}, bf16[32,3584]{1,0:T(8,128)(2,1)S(1)}, u32[]{:S(2)}, u32[]{:S(2)}) collective-permute-start(bf16[32,3584]{1,0:T(8,128)(2,1)S(1)} %shard_map.88.refs_0_), channel_id=1, source_target_pairs={{0,14},{2,0},{4,2},{6,4},{8,6},{10,8},{12,10},{14,12},{1,15},{3,1}... | collective-permute-start | bytes 688136 | tf_op jit(solution)/shard_map/ppermute | solution.py:61
  25.0 0.0 collective-permute-start.3
  25.0 2.1 %shard_map.90.refs_1_.refs_8_.other_w_ref = bf16[1792,1024]{1,0:T(8,128)(2,1)S(1)} custom-call(bf16[1792,1024]{1,0:T(8,128)(2,1)} %collective-permute-done.1.refs_4_.head), custom_call_target="tpu_custom_call" | custom-call | flops 5000000000 | bytes 1024 | tf_op jit(solution)/shard_map/pallas_call | solution.py:193
  27.1 1.6 %collective-permute-done.5.refs_2_ = bf16[32,3584]{1,0:T(8,128)(2,1)S(1)} collective-permute-done((bf16[32,3584]{1,0:T(8,128)(2,1)S(1)}, bf16[32,3584]{1,0:T(8,128)(2,1)S(1)}, u32[]{:S(2)}, u32[]{:S(2)}) %collective-permute-start.5) | collective-permute-done | bytes 229408 | tf_op jit(solution)/shard_map/ppermute | solution.py:61
  28.7 3.4 %collective-permute-start.6 = (bf16[32,3584]{1,0:T(8,128)(2,1)S(1)}, bf16[32,3584]{1,0:T(8,128)(2,1)S(1)}, u32[]{:S(2)}, u32[]{:S(2)}) collective-permute-start(bf16[32,3584]{1,0:T(8,128)(2,1)S(1)} %collective-permute-done.5.refs_2_), channel_id=1, source_target_pairs={{0,14},{2,0},{4,2},{6,4},{8,6},{10,8},{12,10},{14,12},{1,15},{3,1}... | collective-permute-start | bytes 688136 | tf_op jit(solution)/shard_map/ppermute | solution.py:61
  32.1 0.0 collective-permute-done.3.refs_1_
  32.1 0.0 collective-permute-start.4
  32.1 2.5 %shard_map.89.refs_0_.other_w_ref = bf16[2304,1024]{1,0:T(8,128)(2,1)S(1)} custom-call(bf16[2304,1024]{1,0:T(8,128)(2,1)} %collective-permute-done.refs_3_.head), custom_call_target="tpu_custom_call" | custom-call | flops 5000000000 | bytes 1024 | tf_op jit(solution)/shard_map/pallas_call | solution.py:193
  34.6 0.0 slice-start.1
  34.6 0.0 collective-permute-done.8.t_high
  34.7 0.0 collective-permute-done.7.t_low
  34.7 0.4 collective-permute-done.6.high.refs_4_
  35.0 3.1 %collective-permute-done.4.low.refs_3_ = bf16[32,3584]{1,0:T(8,128)(2,1)S(1)} collective-permute-done((bf16[32,3584]{1,0:T(8,128)(2,1)S(1)}, bf16[32,3584]{1,0:T(8,128)(2,1)S(1)}, u32[]{:S(2)}, u32[]{:S(2)}) %collective-permute-start.4) | collective-permute-done | bytes 229408 | tf_op jit(solution)/shard_map/ppermute | solution.py:61
  38.2 0.2 shard_map.91
  38.4 0.1 collective-permute-start.9
  38.4 2.7 %collective-permute-start.11 = (bf16[32,3584]{1,0:T(8,128)(2,1)S(1)}, bf16[32,3584]{1,0:T(8,128)(2,1)S(1)}, u32[]{:S(2)}, u32[]{:S(2)}) collective-permute-start(bf16[32,3584]{1,0:T(8,128)(2,1)S(1)} %get-tuple-element.16), channel_id=1, source_target_pairs={{0,14},{2,0},{4,2},{6,4},{8,6},{10,8},{12,10},{14,12},{1,15},{3,1}... | collective-permute-start | bytes 688136 | tf_op jit(solution)/shard_map/ppermute | solution.py:61
  41.1 0.0 collective-permute-start.13
  41.1 2.7 %collective-permute-start.14 = (bf16[32,4608]{1,0:T(8,128)(2,1)S(1)}, bf16[32,4608]{1,0:T(8,128)(2,1)S(1)}, u32[]{:S(2)}, u32[]{:S(2)}) collective-permute-start(bf16[32,4608]{1,0:T(8,128)(2,1)S(1)} %get-tuple-element.18), channel_id=1, source_target_pairs={{0,192},{64,0},{128,64},{192,128},{1,193},{65,1},{129,65},{193,129... | collective-permute-start | bytes 884744 | tf_op jit(solution)/shard_map/ppermute | solution.py:61
  43.8 0.0 slice-done
  43.8 0.0 slice-done.1
  43.8 0.0 copy-start.1
  43.8 2.1 %shard_map.92.near_ref = bf16[192,1024]{1,0:T(8,128)(2,1)S(1)} custom-call(bf16[192,4608]{1,0:T(8,128)(2,1)S(1)} %get-tuple-element.19.rows_ref, bf16[2304,1024]{1,0:T(8,128)(2,1)S(1)} %bitcast.3, bf16[2304,1024]{1,0:T(8,128)(2,1)S(1)} %shard_map.89.refs_0_.other_w_ref), custom_call_target="tpu_custom_call" | custom-call | flops 5000000000 | bytes 1024 | tf_op jit(solution)/shard_map/pallas_call | solution.py:36
  45.9 0.0 collective-permute-done.9.refs_5_
  45.9 0.1 collective-permute-start.10
  46.0 0.0 collective-permute-done.11.refs_6_
  46.0 2.7 %collective-permute-start.12 = (bf16[16,3584]{1,0:T(8,128)(2,1)S(1)}, bf16[16,3584]{1,0:T(8,128)(2,1)S(1)}, u32[]{:S(2)}, u32[]{:S(2)}) collective-permute-start(bf16[16,3584]{1,0:T(8,128)(2,1)S(1)} %slice.9), channel_id=1, source_target_pairs={{0,14},{2,0},{4,2},{6,4},{8,6},{10,8},{12,10},{14,12},{1,15},{3,1}... | collective-permute-start | bytes 344072 | tf_op jit(solution)/shard_map/ppermute | solution.py:61
  48.7 0.0 copy-done
  48.8 0.0 copy-done.1
  48.8 2.3 %shard_map.93 = (bf16[224,1024]{1,0:T(8,128)(2,1)S(1)}, f32[8,128]{1,0:T(8,128)S(1)}) custom-call(bf16[32,3584]{1,0:T(8,128)(2,1)S(1)} %shard_map.88.refs_0_, bf16[32,3584]{1,0:T(8,128)(2,1)S(1)} %collective-permute-done.3.refs_1_, bf16[32,3584]{1,0:T(8,128)(2,1)S(1)} %collective-permute-done.5.refs_2_, ...), custom_call_target="tpu_custom_call" | custom-call | flops 5000000000 | bytes 1024 | tf_op jit(solution)/shard_map/pallas_call | solution.py:36
  51.1 0.0 collective-permute-done.13.b3
  51.1 0.0 collective-permute-done.14.b4
  51.1 2.3 %shard_map.94 = (bf16[256,1024]{1,0:T(8,128)(2,1)S(1)}, f32[8,128]{1,0:T(8,128)S(1)}) custom-call(bf16[32,4608]{1,0:T(8,128)(2,1)S(1)} %collective-permute-done.13.b3, bf16[32,4608]{1,0:T(8,128)(2,1)S(1)} %collective-permute-done.14.b4, bf16[192,1024]{1,0:T(8,128)(2,1)S(1)} %shard_map.92.near_ref, bf16[2304,1024]{1,0:T(8,128)(2,1)S(1)} %bitcast.3, ...), custom_call_target="tpu_custom_call" | custom-call | flops 5000000000 | bytes 1024 | tf_op jit(solution)/shard_map/pallas_call | solution.py:36
  53.4 0.0 collective-permute-done.10.low.refs_7_
  53.4 0.0 collective-permute-done.12.high.refs_8_
  53.4 1.5 %shard_map.95 = (bf16[32,1024]{1,0:T(8,128)(2,1)S(1)}, f32[16,8,128]{2,1,0:T(8,128)S(1)}) custom-call(bf16[16,3584]{1,0:T(8,128)(2,1)S(1)} %collective-permute-done.10.low.refs_7_, bf16[16,3584]{1,0:T(8,128)(2,1)S(1)} %collective-permute-done.12.high.refs_8_, bf16[1792,1024]{1,0:T(8,128)(2,1)S(1)} %copy-done, ...), custom_call_target="tpu_custom_call" | custom-call | flops 1024 | bytes 1024 | tf_op jit(solution)/shard_map/pallas_call | solution.py:36
  55.0 9.1 %all_to_all.15 = f32[16,8,128]{2,1,0:T(8,128)S(1)} all-to-all(f32[16,8,128]{2,1,0:T(8,128)S(1)} %get-tuple-element.24), channel_id=1, replica_groups=mesh['y'=4,'x'=4,'z'=8,'c'=2] {'y','x'}, dimensions={0} | all-to-all | bytes 131072 | tf_op jit(solution)/shard_map/all_to_all | solution.py:498
  64.1 0.1 shard_map.96.own_ref
  64.1 6.5 %collective-permute-start.15 = (bf16[512,1024]{1,0:T(8,128)(2,1)S(1)}, bf16[512,1024]{1,0:T(8,128)(2,1)S(1)}, u32[]{:S(2)}, u32[]{:S(2)}) collective-permute-start(bf16[512,1024]{1,0:T(8,128)(2,1)S(1)} %shard_map.96.own_ref), channel_id=1, source_target_pairs={{0,1},{1,0},{2,3},{3,2},{4,5},{5,4},{6,7},{7,6},{8,9},{9,8},{10,11... | collective-permute-start | bytes 3145736 | tf_op jit(solution)/shard_map/ppermute | solution.py:57
  70.6 0.8 shard_map.97
  71.5 0.1 collective-permute-start.16
  71.6 11.0 %all_to_all.16.sums_ref = f32[16,8,128]{2,1,0:T(8,128)S(1)} all-to-all(f32[16,8,128]{2,1,0:T(8,128)S(1)} %broadcast_in_dim.2._.refs_9_), channel_id=1, replica_groups=mesh['y'=4,'x'=4,'z'=8,'c'=2] {'z','c'}, dimensions={0} | all-to-all | bytes 131072 | tf_op jit(solution)/shard_map/all_to_all | solution.py:504
  82.6 0.0 collective-permute-done.16.other_rows
  82.6 0.0 collective-permute-done.15.other_ref
  82.6 4.9 %shard_map.98 = (f32[1,2]{1,0:T(1,128)}, bf16[1792,1024]{1,0:T(8,128)(2,1)}) custom-call(f32[16,8,128]{2,1,0:T(8,128)S(1)} %all_to_all.16.sums_ref, bf16[512,1024]{1,0:T(8,128)(2,1)S(1)} %shard_map.96.own_ref, bf16[512,1024]{1,0:T(8,128)(2,1)S(1)} %collective-permute-done.15.other_ref, s32[1,256]{1,0:T(1,128)S(1)} %copy-done.1, ...), custom_call_target="tpu_custom_call" | custom-call | flops 1024 | bytes 1024 | tf_op jit(solution)/shard_map/pallas_call | solution.py:458
  (8 shorter events, 0.1 us)
Async XLA Ops:
  0.6 18.4 %collective-permute-start = (bf16[2304,1024]{1,0:T(8,128)(2,1)}, bf16[2304,1024]{1,0:T(8,128)(2,1)}, u32[]{:S(2)}, u32[]{:S(2)}) collective-permute-start(bf16[2304,1024]{1,0:T(8,128)(2,1)} %own_w_ref.4), channel_id=1, source_target_pairs={{0,1},{1,0},{2,3},{3,2},{4,5},{5,4},{6,7},{7,6},{8,9},{9,8},{10,11... | collective-permute-start | bytes 14155784 | tf_op jit(solution)/shard_map/ppermute | solution.py:57
  4.0 15.1 %collective-permute-start.1 = (bf16[1792,1024]{1,0:T(8,128)(2,1)}, bf16[1792,1024]{1,0:T(8,128)(2,1)}, u32[]{:S(2)}, u32[]{:S(2)}) collective-permute-start(bf16[1792,1024]{1,0:T(8,128)(2,1)} %own_w_ref.5), channel_id=1, source_target_pairs={{0,1},{1,0},{2,3},{3,2},{4,5},{5,4},{6,7},{7,6},{8,9},{9,8},{10,11... | collective-permute-start | bytes 11010056 | tf_op jit(solution)/shard_map/ppermute | solution.py:57
  4.1 10.1 %collective-permute-start.2 = (s32[1,256]{1,0:T(1,128)}, s32[1,256]{1,0:T(1,128)S(1)}, u32[]{:S(2)}, u32[]{:S(2)}) collective-permute-start(s32[1,256]{1,0:T(1,128)} %targets_ref.3), channel_id=1, source_target_pairs={{0,1},{1,0},{2,3},{3,2},{4,5},{5,4},{6,7},{7,6},{8,9},{9,8},{10,11... | collective-permute-start | bytes 3080 | tf_op jit(solution)/shard_map/ppermute | solution.py:57
  4.5 0.7 copy-start.5
  5.2 5.8 %copy-start.2 = (bf16[1,64,4608]{2,1,0:T(8,128)(2,1)S(1)}, bf16[1,64,4608]{2,1,0:T(8,128)(2,1)}, u32[]{:S(2)}) copy-start(bf16[1,64,4608]{2,1,0:T(8,128)(2,1)} %param.8) | copy-start | bytes 1769476
  5.2 5.8 %copy-start.3 = (f32[4608]{0:T(1024)S(1)}, f32[4608]{0:T(1024)}, u32[]{:S(2)}) copy-start(f32[4608]{0:T(1024)} %gain_ref.1) | copy-start | bytes 55300
  5.9 13.1 %all-to-all-start = ((bf16[16,2,3584]{2,1,0:T(2,128)(2,1)}), bf16[16,2,3584]{2,1,0:T(2,128)(2,1)S(1)}, u32[]{:S(2)}, u32[]{:S(2)}) async-start(bf16[16,2,3584]{2,1,0:T(2,128)(2,1)} %shard_map.86._), calls=%async_computation | async-start | bytes 458752 | tf_op jit(solution)/shard_map/all_to_all | solution.py:483
  11.0 8.1 %copy-start.4 = (f32[3584]{0:T(1024)S(1)}, f32[3584]{0:T(1024)}, u32[]{:S(2)}) copy-start(f32[3584]{0:T(1024)} %refs_1_.1) | copy-start | bytes 43012
  11.5 23.2 %collective-permute-start.8 = (bf16[64,4608]{1,0:T(8,128)(2,1)S(1)}, bf16[64,4608]{1,0:T(8,128)(2,1)S(1)}, u32[]{:S(2)}, u32[]{:S(2)}) collective-permute-start(bf16[64,4608]{1,0:T(8,128)(2,1)S(1)} %shard_map.87.refs_2_.rows), channel_id=1, source_target_pairs={{0,192},{64,0},{128,64},{192,128},{1,193},{65,1},{129,65},{193,129... | collective-permute-start | bytes 1769480 | tf_op jit(solution)/shard_map/ppermute | solution.py:61
  14.1 20.5 %collective-permute-start.7 = (bf16[64,4608]{1,0:T(8,128)(2,1)S(1)}, bf16[64,4608]{1,0:T(8,128)(2,1)S(1)}, u32[]{:S(2)}, u32[]{:S(2)}) collective-permute-start(bf16[64,4608]{1,0:T(8,128)(2,1)S(1)} %shard_map.87.refs_2_.rows), channel_id=1, source_target_pairs={{0,64},{64,128},{128,192},{192,0},{1,65},{65,129},{129,193},{193,1... | collective-permute-start | bytes 1769480 | tf_op jit(solution)/shard_map/ppermute | solution.py:61
  19.3 9.3 %collective-permute-start.5 = (bf16[32,3584]{1,0:T(8,128)(2,1)S(1)}, bf16[32,3584]{1,0:T(8,128)(2,1)S(1)}, u32[]{:S(2)}, u32[]{:S(2)}) collective-permute-start(bf16[32,3584]{1,0:T(8,128)(2,1)S(1)} %shard_map.88.refs_0_), channel_id=1, source_target_pairs={{0,14},{2,0},{4,2},{6,4},{8,6},{10,8},{12,10},{14,12},{1,15},{3,1}... | collective-permute-start | bytes 688136 | tf_op jit(solution)/shard_map/ppermute | solution.py:61
  25.0 7.1 %collective-permute-start.3 = (bf16[32,3584]{1,0:T(8,128)(2,1)S(1)}, bf16[32,3584]{1,0:T(8,128)(2,1)S(1)}, u32[]{:S(2)}, u32[]{:S(2)}) collective-permute-start(bf16[32,3584]{1,0:T(8,128)(2,1)S(1)} %shard_map.88.refs_0_), channel_id=1, source_target_pairs={{0,2},{2,4},{4,6},{6,8},{8,10},{10,12},{12,14},{14,0},{1,3},{3,5},... | collective-permute-start | bytes 688136 | tf_op jit(solution)/shard_map/ppermute | solution.py:61
  28.7 6.4 %collective-permute-start.6 = (bf16[32,3584]{1,0:T(8,128)(2,1)S(1)}, bf16[32,3584]{1,0:T(8,128)(2,1)S(1)}, u32[]{:S(2)}, u32[]{:S(2)}) collective-permute-start(bf16[32,3584]{1,0:T(8,128)(2,1)S(1)} %collective-permute-done.5.refs_2_), channel_id=1, source_target_pairs={{0,14},{2,0},{4,2},{6,4},{8,6},{10,8},{12,10},{14,12},{1,15},{3,1}... | collective-permute-start | bytes 688136 | tf_op jit(solution)/shard_map/ppermute | solution.py:61
  32.1 6.1 %collective-permute-start.4 = (bf16[32,3584]{1,0:T(8,128)(2,1)S(1)}, bf16[32,3584]{1,0:T(8,128)(2,1)S(1)}, u32[]{:S(2)}, u32[]{:S(2)}) collective-permute-start(bf16[32,3584]{1,0:T(8,128)(2,1)S(1)} %collective-permute-done.3.refs_1_), channel_id=1, source_target_pairs={{0,2},{2,4},{4,6},{6,8},{8,10},{10,12},{12,14},{14,0},{1,3},{3,5},... | collective-permute-start | bytes 688136 | tf_op jit(solution)/shard_map/ppermute | solution.py:61
  32.1 11.7 %slice-start = ((s8[4718592]{0:T(1024)(128)(4,1)}), s8[4194304]{0:T(1024)(128)(4,1)S(1)}, s32[]{:S(2)}) async-start(s8[4718592]{0:T(1024)(128)(4,1)} %bitcast.2), calls=%async_computation.3 | async-start | bytes 8388608
  34.6 9.2 %slice-start.1 = ((s8[4718592]{0:T(1024)(128)(4,1)}), s8[524288]{0:T(1024)(128)(4,1)S(1)}, s32[]{:S(2)}) async-start(s8[4718592]{0:T(1024)(128)(4,1)} %bitcast.2), calls=%async_computation.4 | async-start | bytes 1048576
  38.4 7.5 %collective-permute-start.9 = (bf16[32,3584]{1,0:T(8,128)(2,1)S(1)}, bf16[32,3584]{1,0:T(8,128)(2,1)S(1)}, u32[]{:S(2)}, u32[]{:S(2)}) collective-permute-start(bf16[32,3584]{1,0:T(8,128)(2,1)S(1)} %get-tuple-element.15), channel_id=1, source_target_pairs={{0,2},{2,4},{4,6},{6,8},{8,10},{10,12},{12,14},{14,0},{1,3},{3,5},... | collective-permute-start | bytes 688136 | tf_op jit(solution)/shard_map/ppermute | solution.py:61
  38.4 7.5 %collective-permute-start.11 = (bf16[32,3584]{1,0:T(8,128)(2,1)S(1)}, bf16[32,3584]{1,0:T(8,128)(2,1)S(1)}, u32[]{:S(2)}, u32[]{:S(2)}) collective-permute-start(bf16[32,3584]{1,0:T(8,128)(2,1)S(1)} %get-tuple-element.16), channel_id=1, source_target_pairs={{0,14},{2,0},{4,2},{6,4},{8,6},{10,8},{12,10},{14,12},{1,15},{3,1}... | collective-permute-start | bytes 688136 | tf_op jit(solution)/shard_map/ppermute | solution.py:61
  41.1 10.0 %collective-permute-start.13 = (bf16[32,4608]{1,0:T(8,128)(2,1)S(1)}, bf16[32,4608]{1,0:T(8,128)(2,1)S(1)}, u32[]{:S(2)}, u32[]{:S(2)}) collective-permute-start(bf16[32,4608]{1,0:T(8,128)(2,1)S(1)} %get-tuple-element.17), channel_id=1, source_target_pairs={{0,64},{64,128},{128,192},{192,0},{1,65},{65,129},{129,193},{193,1... | collective-permute-start | bytes 884744 | tf_op jit(solution)/shard_map/ppermute | solution.py:61
  41.1 10.0 %collective-permute-start.14 = (bf16[32,4608]{1,0:T(8,128)(2,1)S(1)}, bf16[32,4608]{1,0:T(8,128)(2,1)S(1)}, u32[]{:S(2)}, u32[]{:S(2)}) collective-permute-start(bf16[32,4608]{1,0:T(8,128)(2,1)S(1)} %get-tuple-element.18), channel_id=1, source_target_pairs={{0,192},{64,0},{128,64},{192,128},{1,193},{65,1},{129,65},{193,129... | collective-permute-start | bytes 884744 | tf_op jit(solution)/shard_map/ppermute | solution.py:61
  43.8 5.0 %copy-start = (bf16[1792,1024]{1,0:T(8,128)(2,1)S(1)}, bf16[1792,1024]{1,0:T(8,128)(2,1)}, u32[]{:S(2)}) copy-start(bf16[1792,1024]{1,0:T(8,128)(2,1)} %own_w_ref.5) | copy-start | bytes 11010052
  43.8 5.0 %copy-start.1 = (s32[1,256]{1,0:T(1,128)S(1)}, s32[1,256]{1,0:T(1,128)}, u32[]{:S(2)}) copy-start(s32[1,256]{1,0:T(1,128)} %targets_ref.3) | copy-start | bytes 3076
  45.9 7.5 %collective-permute-start.10 = (bf16[16,3584]{1,0:T(8,128)(2,1)S(1)}, bf16[16,3584]{1,0:T(8,128)(2,1)S(1)}, u32[]{:S(2)}, u32[]{:S(2)}) collective-permute-start(bf16[16,3584]{1,0:T(8,128)(2,1)S(1)} %slice.8), channel_id=1, source_target_pairs={{0,2},{2,4},{4,6},{6,8},{8,10},{10,12},{12,14},{14,0},{1,3},{3,5},... | collective-permute-start | bytes 344072 | tf_op jit(solution)/shard_map/ppermute | solution.py:61
  46.0 7.4 %collective-permute-start.12 = (bf16[16,3584]{1,0:T(8,128)(2,1)S(1)}, bf16[16,3584]{1,0:T(8,128)(2,1)S(1)}, u32[]{:S(2)}, u32[]{:S(2)}) collective-permute-start(bf16[16,3584]{1,0:T(8,128)(2,1)S(1)} %slice.9), channel_id=1, source_target_pairs={{0,14},{2,0},{4,2},{6,4},{8,6},{10,8},{12,10},{14,12},{1,15},{3,1}... | collective-permute-start | bytes 344072 | tf_op jit(solution)/shard_map/ppermute | solution.py:61
  64.1 18.4 %collective-permute-start.15 = (bf16[512,1024]{1,0:T(8,128)(2,1)S(1)}, bf16[512,1024]{1,0:T(8,128)(2,1)S(1)}, u32[]{:S(2)}, u32[]{:S(2)}) collective-permute-start(bf16[512,1024]{1,0:T(8,128)(2,1)S(1)} %shard_map.96.own_ref), channel_id=1, source_target_pairs={{0,1},{1,0},{2,3},{3,2},{4,5},{5,4},{6,7},{7,6},{8,9},{9,8},{10,11... | collective-permute-start | bytes 3145736 | tf_op jit(solution)/shard_map/ppermute | solution.py:57
  71.5 11.1 %collective-permute-start.16 = (bf16[1792,256]{1,0:T(8,128)(2,1)S(1)}, bf16[1792,256]{1,0:T(8,128)(2,1)S(1)}, u32[]{:S(2)}, u32[]{:S(2)}) collective-permute-start(bf16[1792,256]{1,0:T(8,128)(2,1)S(1)} %get-tuple-element.27), channel_id=1, source_target_pairs={{0,1},{1,0},{2,3},{3,2},{4,5},{5,4},{6,7},{7,6},{8,9},{9,8},{10,11... | collective-permute-start | bytes 2752520 | tf_op jit(solution)/shard_map/ppermute | solution.py:57

commit v6 on v5

--- a/solution.py
+++ b/solution.py
@@ -61,10 +61,8 @@
     return lax.ppermute(low, axis, up(n, 1)), lax.ppermute(high, axis, up(n, -1))
 
 
-def gate_kernel(low, high, rows, t_low, t_high, *refs):
-    low_out, high_out, t_low_out, t_high_out, near_out = refs[-5:]
-    for index, block in enumerate((rows, t_low, t_high)):
-        near_out[pl.ds(index * rows.shape[0], rows.shape[0])] = block[...]
+def gate_kernel(low, high, t_low, t_high, *refs):
+    low_out, high_out, t_low_out, t_high_out = refs[-4:]
     low_out[...] = low[...]
     high_out[...] = high[...]
     half = t_low_out.shape[0]
@@ -72,33 +70,34 @@
     t_high_out[...] = t_high[half:]
 
 
-def gate(low, high, rows, t_low, t_high, *others):
+def gate(low, high, t_low, t_high, *others):
     part = struct((t_low.shape[0] // 2, t_low.shape[1]), BF16)
-    near = struct((3 * t_low.shape[0], t_low.shape[1]), BF16)
     plane = struct(low.shape, BF16)
     return pl.pallas_call(
         gate_kernel,
-        out_shape=(plane, plane, part, part, near),
-        in_specs=[VMEM] * 5 + [ANY] * len(others),
-        out_specs=(VMEM,) * 5,
+        out_shape=(plane, plane, part, part),
+        in_specs=[VMEM] * 4 + [ANY] * len(others),
+        out_specs=(VMEM,) * 4,
         compiler_params=params(4),
         cost_estimate=LONG,
-    )(low, high, rows, t_low, t_high, *others)
-
-
-def rings(plane, rows, others):
+    )(low, high, t_low, t_high, *others)
+
+
+def rings(plane, rows, teacher_head, other_teacher_head, other_student_head):
     t_low, t_high = both_ways(rows, rows, "y", NY)
     planes = [plane]
     low = high = plane
     for step in range(NZ // 2 - 1):
         if step == 2:
-            low, high, t_low_half, t_high_half, near = gate(low, high, rows, t_low, t_high, *others)
+            near = near_teacher((rows, t_low, t_high), teacher_head, other_teacher_head)
+            waited = (near, other_student_head)
+            low, high, t_low_half, t_high_half = gate(low, high, t_low, t_high, *waited)
         low, high = both_ways(low, high, "z", NZ)
         planes += [low, high]
     far = both_ways(t_low_half, t_high_half, "y", NY)
     half = plane.shape[0] // 2
     planes += both_ways(low[:half], high[half:], "z", NZ)
-    return planes, near, far
+    return planes, far, near
 
 
 def distance(position):
@@ -178,7 +177,7 @@
     return tuple(pl.ds(pl.multiple_of(half * k, LANES), k) for half in (core, 1 - core))
 
 
-def fetch_kernel(head, out_ref, sem):
+def fetch_kernel(head, _, out_ref, sem):
     part = head.shape[0] // PARTS
     copies = []
     for index in range(PARTS):
@@ -189,16 +188,16 @@
         copy.wait()
 
 
-def fetched(head):
+def fetched(head, other):
     return pl.pallas_call(
         fetch_kernel,
         out_shape=struct(head.shape, head.dtype),
-        in_specs=[ANY],
+        in_specs=[ANY, ANY],
         out_specs=VMEM,
         scratch_shapes=[pltpu.SemaphoreType.DMA((PARTS,))],
         compiler_params=params(4),
         cost_estimate=LONG,
-    )(head)
+    )(head, other)
 
 
 def logits(rows_ref, own_w_ref, other_w_ref, out_ref):
@@ -215,13 +214,17 @@
     return (30.0 * jnp.tanh(logits / 30.0)).astype(BF16)
 
 
-def near_teacher_kernel(rows_ref, own_w_ref, other_w_ref, out_ref):
+def near_teacher_kernel(b0, b1, b2, own_w_ref, other_w_ref, out_ref, rows_ref):
+    rows_ref[...] = jnp.concatenate([b0[...], b1[...], b2[...]])
     logits(rows_ref, own_w_ref, other_w_ref, out_ref)
 
 
-def near_teacher(rows, own_head, other_head):
-    out = struct((rows.shape[0], own_head.shape[1]), BF16)
-    return call(near_teacher_kernel, out, (rows, own_head, other_head), cost=LONG)
+def near_teacher(blocks, own_head, other_head):
+    k, vocab = own_head.shape
+    n = 3 * blocks[0].shape[0]
+    scratch = [pltpu.VMEM((n, 2 * k), BF16)]
+    out = struct((n, vocab), BF16)
+    return call(near_teacher_kernel, out, (*blocks, own_head, other_head), scratch, LONG)
 
 
 def local_targets(targets_ref, z, first, rows):
@@ -484,10 +487,12 @@
     teacher_rows = teacher_norm(teacher_hidden[0], teacher_gain, sent)
     waited = (teacher_rows, other_teacher_head, other_student_head, oth_targets)
     plane = plane_rows(got, student_gain, *waited)
-    other_teacher_head, other_student_head = fetched(other_teacher_head), fetched(other_student_head)
-    planes, near, far = rings(plane, teacher_rows, (other_teacher_head, other_student_head))
-
-    near = near_teacher(near, teacher_head, other_teacher_head)
+    other_teacher_head = fetched(other_teacher_head, plane)
+    other_student_head = fetched(other_student_head, plane)
+    planes, far, near = rings(
+        plane, teacher_rows, teacher_head, other_teacher_head, other_student_head
+    )
+
     capped, early = early_rows(planes[: NZ - 1], student_head, other_student_head, targets)
     teacher, early = far_teacher(far, near, teacher_head, other_teacher_head, capped, early)
     low, high = planes[NZ - 1 :]

time: 88 us -> 87.4 us (level)
  blocking collectives: 20.1 us -> 24.8 us
  waiting for transfers between devices: 10 us -> 5.6 us
  starting transfers between devices: 35.4 us -> 34.4 us
    ppermute x6, starting transfers between devices: 19.8 us -> 15.4 us  [both_ways(): lax.ppermute(high, axis, up(n, -1))]
    ppermute x6, starting transfers between devices: 0.18 us -> 4.41 us  [both_ways(): lax.ppermute(low, axis, up(n, 1))]
    all_to_all x1, waiting for transfers between devices: 4.89 us -> 1.49 us  [shards(): got = lax.all_to_all(sent, ('y', 'x'), 0, 0, tiled=True)]
    all_to_all x1, blocking collectives: 9.07 us -> 11.5 us  [shards(): sums = jnp.sum(lax.all_to_all(sums, ('y', 'x'), 0, 0, tiled=True), axis=0)]
    all_to_all x1, blocking collectives: 11 us -> 13.3 us  [shards(): sums = lax.all_to_all(sums, ('z', 'c'), 0, 0, tiled=True)]
    ppermute x6, waiting for transfers between devices: 2.01 us -> 0.02 us  [both_ways(): lax.ppermute(high, axis, up(n, -1))]
    ppermute x5, waiting for transfers between devices: 0.01 us -> 1.89 us  [swap_cores(): return lax.ppermute(value, 'c', [(0, 1), (1, 0)])]
    ppermute x6, waiting for transfers between devices: 3.13 us -> 2.2 us  [both_ways(): lax.ppermute(low, axis, up(n, 1))]
  transfers between devices with their start and end apart: 18 -> 18, of which waited for: 4 -> 4; matrix products, arithmetic and copies ran while one was open for 0% -> 0% of each run, Pallas kernels for 15% -> 16%
where the time goes in v6:
time: 87.4 us; the launch traced here: 87 us
  starting transfers between devices  34.4 us (39%)
  blocking collectives  24.8 us (28%)
  Pallas kernels  20.4 us (23%)
  waiting for transfers between devices  5.6 us (6%)
  between operations  1.03 us (1%)
    ppermute x6, starting transfers between devices, both_ways(): lax.ppermute(high, axis, up(n, -1))  15.4 us
    all_to_all x1, blocking collectives, shards(): sums = lax.all_to_all(sums, ('z', 'c'), 0, 0, tiled=True)  13.3 us
    all_to_all x1, blocking collectives, shards(): sums = jnp.sum(lax.all_to_all(sums, ('y', 'x'), 0, 0, tiled=True), axis=0)  11.5 us
    pallas_call x7, Pallas kernels, call(): pl.pallas_call(body, out_shape=out_shape, in_specs=[VMEM] * len(operands)...  9.94 us
    ppermute x5, starting transfers between devices, swap_cores(): return lax.ppermute(value, 'c', [(0, 1), (1, 0)])  9.55 us
    all_to_all x1, starting transfers between devices, shards(): got = lax.all_to_all(sent, ('y', 'x'), 0, 0, tiled=True)  5.02 us
    pallas_call x1, Pallas kernels, gradient(): pl.pallas_call(gradient_kernel, out_shape=(struct((1, ROWS), F32), struct...  4.9 us
    pallas_call x2, Pallas kernels, fetched(): pl.pallas_call(fetch_kernel, out_shape=struct(head.shape, head.dtype), in...  4.73 us
  transfers between devices with their start and end apart: 18, of which 4 were waited for; matrix products, arithmetic and copies ran while one was open for 0% of the time, Pallas kernels for 16%

profile of v6, /device:TPU:1, one launch (start us, length us, event | category | flops | bytes accessed | tf_op | source)
XLA Modules:
  0.0 87.0 jit_solution(5719751072653694191)
XLA Ops:
  0.6 3.3 %collective-permute-start = (bf16[2304,1024]{1,0:T(8,128)(2,1)}, bf16[2304,1024]{1,0:T(8,128)(2,1)}, u32[]{:S(2)}, u32[]{:S(2)}) collective-permute-start(bf16[2304,1024]{1,0:T(8,128)(2,1)} %own_w_ref.4), channel_id=1, source_target_pairs={{0,1},{1,0},{2,3},{3,2},{4,5},{5,4},{6,7},{7,6},{8,9},{9,8},{10,11... | collective-permute-start | bytes 14155784 | tf_op jit(solution)/shard_map/ppermute | solution.py:57
  4.0 0.1 collective-permute-start.1
  4.1 0.0 copy-start.5
  4.1 0.7 copy-done.5
  4.8 0.0 copy-start.2
  4.8 0.0 copy-start.3
  4.8 0.7 shard_map.86._
  5.5 5.0 %all-to-all-start = ((bf16[16,2,3584]{2,1,0:T(2,128)(2,1)}), bf16[16,2,3584]{2,1,0:T(2,128)(2,1)S(1)}, u32[]{:S(2)}, u32[]{:S(2)}) async-start(bf16[16,2,3584]{2,1,0:T(2,128)(2,1)} %shard_map.86._), calls=%async_computation | async-start | bytes 458752 | tf_op jit(solution)/shard_map/all_to_all | solution.py:486
  10.5 0.0 copy-done.1
  10.5 0.8 collective-permute-start.2
  11.3 0.0 copy-done.2
  11.3 0.0 copy-done.3
  11.3 0.5 shard_map.87.refs_2_.b0
  11.8 1.7 %collective-permute-start.7 = (bf16[64,4608]{1,0:T(8,128)(2,1)S(1)}, bf16[64,4608]{1,0:T(8,128)(2,1)S(1)}, u32[]{:S(2)}, u32[]{:S(2)}) collective-permute-start(bf16[64,4608]{1,0:T(8,128)(2,1)S(1)} %shard_map.87.refs_2_.b0), channel_id=1, source_target_pairs={{0,64},{64,128},{128,192},{192,0},{1,65},{65,129},{129,193},{193,1... | collective-permute-start | bytes 1769480 | tf_op jit(solution)/shard_map/ppermute | solution.py:61
  13.5 1.3 %collective-permute-start.8 = (bf16[64,4608]{1,0:T(8,128)(2,1)S(1)}, bf16[64,4608]{1,0:T(8,128)(2,1)S(1)}, u32[]{:S(2)}, u32[]{:S(2)}) collective-permute-start(bf16[64,4608]{1,0:T(8,128)(2,1)S(1)} %shard_map.87.refs_2_.b0), channel_id=1, source_target_pairs={{0,192},{64,0},{128,64},{192,128},{1,193},{65,1},{129,65},{193,129... | collective-permute-start | bytes 1769480 | tf_op jit(solution)/shard_map/ppermute | solution.py:61
  14.9 1.9 %collective-permute-done.2.refs_5_.oth_targets_ref = s32[1,256]{1,0:T(1,128)S(1)} collective-permute-done((s32[1,256]{1,0:T(1,128)S(1)}, s32[1,256]{1,0:T(1,128)S(1)}, u32[]{:S(2)}, u32[]{:S(2)}) %collective-permute-start.2) | collective-permute-done | bytes 1056 | tf_op jit(solution)/shard_map/ppermute | solution.py:57
  16.7 1.5 %all-to-all-done.refs_0_ = bf16[16,2,3584]{2,1,0:T(2,128)(2,1)S(1)} async-done(((bf16[16,2,3584]{2,1,0:T(2,128)(2,1)}), bf16[16,2,3584]{2,1,0:T(2,128)(2,1)S(1)}, u32[]{:S(2)}, u32[]{:S(2)}) %all-to-all-start) | async-done | bytes 229408 | tf_op jit(solution)/shard_map/all_to_all | solution.py:486
  18.2 0.0 collective-permute-done.1.refs_4_.head
  18.2 0.0 collective-permute-done.refs_3_.head
  18.2 0.0 copy-done.4
  18.2 0.3 shard_map.88._.refs_0_
  18.5 1.7 %collective-permute-start.3 = (bf16[32,3584]{1,0:T(8,128)(2,1)S(1)}, bf16[32,3584]{1,0:T(8,128)(2,1)S(1)}, u32[]{:S(2)}, u32[]{:S(2)}) collective-permute-start(bf16[32,3584]{1,0:T(8,128)(2,1)S(1)} %shard_map.88._.refs_0_), channel_id=1, source_target_pairs={{0,2},{2,4},{4,6},{6,8},{8,10},{10,12},{12,14},{14,0},{1,3},{3,5},... | collective-permute-start | bytes 688136 | tf_op jit(solution)/shard_map/ppermute | solution.py:61
  20.2 4.0 %collective-permute-start.5 = (bf16[32,3584]{1,0:T(8,128)(2,1)S(1)}, bf16[32,3584]{1,0:T(8,128)(2,1)S(1)}, u32[]{:S(2)}, u32[]{:S(2)}) collective-permute-start(bf16[32,3584]{1,0:T(8,128)(2,1)S(1)} %shard_map.88._.refs_0_), channel_id=1, source_target_pairs={{0,14},{2,0},{4,2},{6,4},{8,6},{10,8},{12,10},{14,12},{1,15},{3,1}... | collective-permute-start | bytes 688136 | tf_op jit(solution)/shard_map/ppermute | solution.py:61
  24.3 2.5 %shard_map.89.other_w_ref = bf16[2304,1024]{1,0:T(8,128)(2,1)S(1)} custom-call(bf16[2304,1024]{1,0:T(8,128)(2,1)} %collective-permute-done.refs_3_.head, bf16[32,3584]{1,0:T(8,128)(2,1)S(1)} %shard_map.88._.refs_0_), custom_call_target="tpu_custom_call" | custom-call | flops 5000000000 | bytes 1024 | tf_op jit(solution)/shard_map/pallas_call | solution.py:192
  26.8 0.0 slice-start.1
  26.8 2.2 %shard_map.91.refs_1_.refs_8_.other_w_ref = bf16[1792,1024]{1,0:T(8,128)(2,1)S(1)} custom-call(bf16[1792,1024]{1,0:T(8,128)(2,1)} %collective-permute-done.1.refs_4_.head, bf16[32,3584]{1,0:T(8,128)(2,1)S(1)} %shard_map.88._.refs_0_), custom_call_target="tpu_custom_call" | custom-call | flops 5000000000 | bytes 1024 | tf_op jit(solution)/shard_map/pallas_call | solution.py:192
  29.0 0.0 collective-permute-done.3.refs_1_
  29.0 0.1 collective-permute-start.4
  29.1 0.0 collective-permute-done.5.refs_2_
  29.1 2.7 %collective-permute-start.6 = (bf16[32,3584]{1,0:T(8,128)(2,1)S(1)}, bf16[32,3584]{1,0:T(8,128)(2,1)S(1)}, u32[]{:S(2)}, u32[]{:S(2)}) collective-permute-start(bf16[32,3584]{1,0:T(8,128)(2,1)S(1)} %collective-permute-done.5.refs_2_), channel_id=1, source_target_pairs={{0,14},{2,0},{4,2},{6,4},{8,6},{10,8},{12,10},{14,12},{1,15},{3,1}... | collective-permute-start | bytes 688136 | tf_op jit(solution)/shard_map/ppermute | solution.py:61
  31.8 0.0 collective-permute-done.7.b1.t_low
  31.8 0.0 collective-permute-done.8.b2.t_high
  31.8 0.0 slice-done
  31.8 0.0 slice-done.1
  31.8 2.2 %shard_map.90.refs_0_.near_ref = bf16[192,1024]{1,0:T(8,128)(2,1)S(1)} custom-call(bf16[64,4608]{1,0:T(8,128)(2,1)S(1)} %shard_map.87.refs_2_.b0, bf16[64,4608]{1,0:T(8,128)(2,1)S(1)} %collective-permute-done.7.b1.t_low, bf16[64,4608]{1,0:T(8,128)(2,1)S(1)} %collective-permute-done.8.b2.t_high, bf16[2304,1024]{1,0:T(8,128)(2,1)S(1)} %bitcast.3, ...), custom_call_target="tpu_custom_call" | custom-call | flops 5000000000 | bytes 1024 | tf_op jit(solution)/shard_map/pallas_call | solution.py:36
  34.0 0.0 copy-start
  34.0 1.5 %collective-permute-done.4.low.refs_3_ = bf16[32,3584]{1,0:T(8,128)(2,1)S(1)} collective-permute-done((bf16[32,3584]{1,0:T(8,128)(2,1)S(1)}, bf16[32,3584]{1,0:T(8,128)(2,1)S(1)}, u32[]{:S(2)}, u32[]{:S(2)}) %collective-permute-start.4) | collective-permute-done | bytes 229408 | tf_op jit(solution)/shard_map/ppermute | solution.py:61
  35.6 0.0 collective-permute-done.6.high.refs_4_
  35.6 0.1 shard_map.92
  35.6 0.1 collective-permute-start.9
  35.7 2.7 %collective-permute-start.11 = (bf16[32,3584]{1,0:T(8,128)(2,1)S(1)}, bf16[32,3584]{1,0:T(8,128)(2,1)S(1)}, u32[]{:S(2)}, u32[]{:S(2)}) collective-permute-start(bf16[32,3584]{1,0:T(8,128)(2,1)S(1)} %get-tuple-element.15), channel_id=1, source_target_pairs={{0,14},{2,0},{4,2},{6,4},{8,6},{10,8},{12,10},{14,12},{1,15},{3,1}... | collective-permute-start | bytes 688136 | tf_op jit(solution)/shard_map/ppermute | solution.py:61
  38.5 0.7 collective-permute-start.13
  39.2 2.0 %collective-permute-start.14 = (bf16[32,4608]{1,0:T(8,128)(2,1)S(1)}, bf16[32,4608]{1,0:T(8,128)(2,1)S(1)}, u32[]{:S(2)}, u32[]{:S(2)}) collective-permute-start(bf16[32,4608]{1,0:T(8,128)(2,1)S(1)} %get-tuple-element.17), channel_id=1, source_target_pairs={{0,192},{64,0},{128,64},{192,128},{1,193},{65,1},{129,65},{193,129... | collective-permute-start | bytes 884744 | tf_op jit(solution)/shard_map/ppermute | solution.py:61
  41.2 0.6 collective-permute-done.9.refs_5_
  41.8 0.1 collective-permute-start.10
  41.9 0.0 collective-permute-done.11.refs_6_
  41.9 2.7 %collective-permute-start.12 = (bf16[16,3584]{1,0:T(8,128)(2,1)S(1)}, bf16[16,3584]{1,0:T(8,128)(2,1)S(1)}, u32[]{:S(2)}, u32[]{:S(2)}) collective-permute-start(bf16[16,3584]{1,0:T(8,128)(2,1)S(1)} %slice.9), channel_id=1, source_target_pairs={{0,14},{2,0},{4,2},{6,4},{8,6},{10,8},{12,10},{14,12},{1,15},{3,1}... | collective-permute-start | bytes 344072 | tf_op jit(solution)/shard_map/ppermute | solution.py:61
  44.7 0.0 copy-done
  44.7 2.4 %shard_map.93 = (bf16[224,1024]{1,0:T(8,128)(2,1)S(1)}, f32[8,128]{1,0:T(8,128)S(1)}) custom-call(bf16[32,3584]{1,0:T(8,128)(2,1)S(1)} %shard_map.88._.refs_0_, bf16[32,3584]{1,0:T(8,128)(2,1)S(1)} %collective-permute-done.3.refs_1_, bf16[32,3584]{1,0:T(8,128)(2,1)S(1)} %collective-permute-done.5.refs_2_, ...), custom_call_target="tpu_custom_call" | custom-call | flops 5000000000 | bytes 1024 | tf_op jit(solution)/shard_map/pallas_call | solution.py:36
  47.0 0.0 collective-permute-done.13.b3
  47.0 0.0 collective-permute-done.14.b4
  47.1 2.3 %shard_map.94 = (bf16[256,1024]{1,0:T(8,128)(2,1)S(1)}, f32[8,128]{1,0:T(8,128)S(1)}) custom-call(bf16[32,4608]{1,0:T(8,128)(2,1)S(1)} %collective-permute-done.13.b3, bf16[32,4608]{1,0:T(8,128)(2,1)S(1)} %collective-permute-done.14.b4, bf16[192,1024]{1,0:T(8,128)(2,1)S(1)} %shard_map.90.refs_0_.near_ref, bf16[2304,1024]{1,0:T(8,128)(2,1)S(1)} %bitcast.3, ...), custom_call_target="tpu_custom_call" | custom-call | flops 5000000000 | bytes 1024 | tf_op jit(solution)/shard_map/pallas_call | solution.py:36
  49.4 0.0 collective-permute-done.10.low.refs_7_
  49.4 0.0 collective-permute-done.12.high.refs_8_
  49.4 1.5 %shard_map.95 = (bf16[32,1024]{1,0:T(8,128)(2,1)S(1)}, f32[16,8,128]{2,1,0:T(8,128)S(1)}) custom-call(bf16[16,3584]{1,0:T(8,128)(2,1)S(1)} %collective-permute-done.10.low.refs_7_, bf16[16,3584]{1,0:T(8,128)(2,1)S(1)} %collective-permute-done.12.high.refs_8_, bf16[1792,1024]{1,0:T(8,128)(2,1)S(1)} %copy-done, ...), custom_call_target="tpu_custom_call" | custom-call | flops 1024 | bytes 1024 | tf_op jit(solution)/shard_map/pallas_call | solution.py:36
  50.9 11.5 %all_to_all.15 = f32[16,8,128]{2,1,0:T(8,128)S(1)} all-to-all(f32[16,8,128]{2,1,0:T(8,128)S(1)} %get-tuple-element.22), channel_id=1, replica_groups=mesh['y'=4,'x'=4,'z'=8,'c'=2] {'y','x'}, dimensions={0} | all-to-all | bytes 131072 | tf_op jit(solution)/shard_map/all_to_all | solution.py:503
  62.4 0.1 shard_map.96.own_ref
  62.5 5.2 %collective-permute-start.15 = (bf16[512,1024]{1,0:T(8,128)(2,1)S(1)}, bf16[512,1024]{1,0:T(8,128)(2,1)S(1)}, u32[]{:S(2)}, u32[]{:S(2)}) collective-permute-start(bf16[512,1024]{1,0:T(8,128)(2,1)S(1)} %shard_map.96.own_ref), channel_id=1, source_target_pairs={{0,1},{1,0},{2,3},{3,2},{4,5},{5,4},{6,7},{7,6},{8,9},{9,8},{10,11... | collective-permute-start | bytes 3145736 | tf_op jit(solution)/shard_map/ppermute | solution.py:57
  67.7 0.8 shard_map.97
  68.5 0.1 collective-permute-start.16
  68.6 13.3 %all_to_all.16.sums_ref = f32[16,8,128]{2,1,0:T(8,128)S(1)} all-to-all(f32[16,8,128]{2,1,0:T(8,128)S(1)} %broadcast_in_dim.2._.refs_9_), channel_id=1, replica_groups=mesh['y'=4,'x'=4,'z'=8,'c'=2] {'z','c'}, dimensions={0} | all-to-all | bytes 131072 | tf_op jit(solution)/shard_map/all_to_all | solution.py:509
  82.0 0.0 collective-permute-done.16.other_rows
  82.0 0.0 collective-permute-done.15.other_ref
  82.0 4.9 %shard_map.98 = (f32[1,2]{1,0:T(1,128)}, bf16[1792,1024]{1,0:T(8,128)(2,1)}) custom-call(f32[16,8,128]{2,1,0:T(8,128)S(1)} %all_to_all.16.sums_ref, bf16[512,1024]{1,0:T(8,128)(2,1)S(1)} %shard_map.96.own_ref, bf16[512,1024]{1,0:T(8,128)(2,1)S(1)} %collective-permute-done.15.other_ref, s32[1,256]{1,0:T(1,128)S(1)} %copy-done.1, ...), custom_call_target="tpu_custom_call" | custom-call | flops 1024 | bytes 1024 | tf_op jit(solution)/shard_map/pallas_call | solution.py:461
  (8 shorter events, 0.1 us)
Async XLA Ops:
  0.6 17.6 %collective-permute-start = (bf16[2304,1024]{1,0:T(8,128)(2,1)}, bf16[2304,1024]{1,0:T(8,128)(2,1)}, u32[]{:S(2)}, u32[]{:S(2)}) collective-permute-start(bf16[2304,1024]{1,0:T(8,128)(2,1)} %own_w_ref.4), channel_id=1, source_target_pairs={{0,1},{1,0},{2,3},{3,2},{4,5},{5,4},{6,7},{7,6},{8,9},{9,8},{10,11... | collective-permute-start | bytes 14155784 | tf_op jit(solution)/shard_map/ppermute | solution.py:57
  4.0 14.3 %collective-permute-start.1 = (bf16[1792,1024]{1,0:T(8,128)(2,1)}, bf16[1792,1024]{1,0:T(8,128)(2,1)}, u32[]{:S(2)}, u32[]{:S(2)}) collective-permute-start(bf16[1792,1024]{1,0:T(8,128)(2,1)} %own_w_ref.5), channel_id=1, source_target_pairs={{0,1},{1,0},{2,3},{3,2},{4,5},{5,4},{6,7},{7,6},{8,9},{9,8},{10,11... | collective-permute-start | bytes 11010056 | tf_op jit(solution)/shard_map/ppermute | solution.py:57
  4.1 0.7 copy-start.5
  4.8 5.7 %copy-start.1 = (s32[1,256]{1,0:T(1,128)S(1)}, s32[1,256]{1,0:T(1,128)}, u32[]{:S(2)}) copy-start(s32[1,256]{1,0:T(1,128)} %targets_ref.3) | copy-start | bytes 3076
  4.8 6.5 %copy-start.2 = (bf16[1,64,4608]{2,1,0:T(8,128)(2,1)S(1)}, bf16[1,64,4608]{2,1,0:T(8,128)(2,1)}, u32[]{:S(2)}) copy-start(bf16[1,64,4608]{2,1,0:T(8,128)(2,1)} %param.8) | copy-start | bytes 1769476
  4.8 6.5 %copy-start.3 = (f32[4608]{0:T(1024)S(1)}, f32[4608]{0:T(1024)}, u32[]{:S(2)}) copy-start(f32[4608]{0:T(1024)} %gain_ref.1) | copy-start | bytes 55300
  5.5 12.7 %all-to-all-start = ((bf16[16,2,3584]{2,1,0:T(2,128)(2,1)}), bf16[16,2,3584]{2,1,0:T(2,128)(2,1)S(1)}, u32[]{:S(2)}, u32[]{:S(2)}) async-start(bf16[16,2,3584]{2,1,0:T(2,128)(2,1)} %shard_map.86._), calls=%async_computation | async-start | bytes 458752 | tf_op jit(solution)/shard_map/all_to_all | solution.py:486
  10.5 6.2 %collective-permute-start.2 = (s32[1,256]{1,0:T(1,128)S(1)}, s32[1,256]{1,0:T(1,128)S(1)}, u32[]{:S(2)}, u32[]{:S(2)}) collective-permute-start(s32[1,256]{1,0:T(1,128)S(1)} %copy-done.1), channel_id=1, source_target_pairs={{0,1},{1,0},{2,3},{3,2},{4,5},{5,4},{6,7},{7,6},{8,9},{9,8},{10,11... | collective-permute-start | bytes 3080 | tf_op jit(solution)/shard_map/ppermute | solution.py:57
  11.3 6.9 %copy-start.4 = (f32[3584]{0:T(1024)S(1)}, f32[3584]{0:T(1024)}, u32[]{:S(2)}) copy-start(f32[3584]{0:T(1024)} %refs_1_.1) | copy-start | bytes 43012
  11.8 20.0 %collective-permute-start.7 = (bf16[64,4608]{1,0:T(8,128)(2,1)S(1)}, bf16[64,4608]{1,0:T(8,128)(2,1)S(1)}, u32[]{:S(2)}, u32[]{:S(2)}) collective-permute-start(bf16[64,4608]{1,0:T(8,128)(2,1)S(1)} %shard_map.87.refs_2_.b0), channel_id=1, source_target_pairs={{0,64},{64,128},{128,192},{192,0},{1,65},{65,129},{129,193},{193,1... | collective-permute-start | bytes 1769480 | tf_op jit(solution)/shard_map/ppermute | solution.py:61
  13.5 18.3 %collective-permute-start.8 = (bf16[64,4608]{1,0:T(8,128)(2,1)S(1)}, bf16[64,4608]{1,0:T(8,128)(2,1)S(1)}, u32[]{:S(2)}, u32[]{:S(2)}) collective-permute-start(bf16[64,4608]{1,0:T(8,128)(2,1)S(1)} %shard_map.87.refs_2_.b0), channel_id=1, source_target_pairs={{0,192},{64,0},{128,64},{192,128},{1,193},{65,1},{129,65},{193,129... | collective-permute-start | bytes 1769480 | tf_op jit(solution)/shard_map/ppermute | solution.py:61
  18.5 10.5 %collective-permute-start.3 = (bf16[32,3584]{1,0:T(8,128)(2,1)S(1)}, bf16[32,3584]{1,0:T(8,128)(2,1)S(1)}, u32[]{:S(2)}, u32[]{:S(2)}) collective-permute-start(bf16[32,3584]{1,0:T(8,128)(2,1)S(1)} %shard_map.88._.refs_0_), channel_id=1, source_target_pairs={{0,2},{2,4},{4,6},{6,8},{8,10},{10,12},{12,14},{14,0},{1,3},{3,5},... | collective-permute-start | bytes 688136 | tf_op jit(solution)/shard_map/ppermute | solution.py:61
  20.2 8.9 %collective-permute-start.5 = (bf16[32,3584]{1,0:T(8,128)(2,1)S(1)}, bf16[32,3584]{1,0:T(8,128)(2,1)S(1)}, u32[]{:S(2)}, u32[]{:S(2)}) collective-permute-start(bf16[32,3584]{1,0:T(8,128)(2,1)S(1)} %shard_map.88._.refs_0_), channel_id=1, source_target_pairs={{0,14},{2,0},{4,2},{6,4},{8,6},{10,8},{12,10},{14,12},{1,15},{3,1}... | collective-permute-start | bytes 688136 | tf_op jit(solution)/shard_map/ppermute | solution.py:61
  24.3 7.5 %slice-start = ((s8[4718592]{0:T(1024)(128)(4,1)}), s8[4194304]{0:T(1024)(128)(4,1)S(1)}, s32[]{:S(2)}) async-start(s8[4718592]{0:T(1024)(128)(4,1)} %bitcast.2), calls=%async_computation.3 | async-start | bytes 8388608
  26.8 5.0 %slice-start.1 = ((s8[4718592]{0:T(1024)(128)(4,1)}), s8[524288]{0:T(1024)(128)(4,1)S(1)}, s32[]{:S(2)}) async-start(s8[4718592]{0:T(1024)(128)(4,1)} %bitcast.2), calls=%async_computation.4 | async-start | bytes 1048576
  29.0 6.5 %collective-permute-start.4 = (bf16[32,3584]{1,0:T(8,128)(2,1)S(1)}, bf16[32,3584]{1,0:T(8,128)(2,1)S(1)}, u32[]{:S(2)}, u32[]{:S(2)}) collective-permute-start(bf16[32,3584]{1,0:T(8,128)(2,1)S(1)} %collective-permute-done.3.refs_1_), channel_id=1, source_target_pairs={{0,2},{2,4},{4,6},{6,8},{8,10},{10,12},{12,14},{14,0},{1,3},{3,5},... | collective-permute-start | bytes 688136 | tf_op jit(solution)/shard_map/ppermute | solution.py:61
  29.1 6.4 %collective-permute-start.6 = (bf16[32,3584]{1,0:T(8,128)(2,1)S(1)}, bf16[32,3584]{1,0:T(8,128)(2,1)S(1)}, u32[]{:S(2)}, u32[]{:S(2)}) collective-permute-start(bf16[32,3584]{1,0:T(8,128)(2,1)S(1)} %collective-permute-done.5.refs_2_), channel_id=1, source_target_pairs={{0,14},{2,0},{4,2},{6,4},{8,6},{10,8},{12,10},{14,12},{1,15},{3,1}... | collective-permute-start | bytes 688136 | tf_op jit(solution)/shard_map/ppermute | solution.py:61
  34.0 10.7 %copy-start = (bf16[1792,1024]{1,0:T(8,128)(2,1)S(1)}, bf16[1792,1024]{1,0:T(8,128)(2,1)}, u32[]{:S(2)}) copy-start(bf16[1792,1024]{1,0:T(8,128)(2,1)} %own_w_ref.5) | copy-start | bytes 11010052
  35.6 6.2 %collective-permute-start.9 = (bf16[32,3584]{1,0:T(8,128)(2,1)S(1)}, bf16[32,3584]{1,0:T(8,128)(2,1)S(1)}, u32[]{:S(2)}, u32[]{:S(2)}) collective-permute-start(bf16[32,3584]{1,0:T(8,128)(2,1)S(1)} %get-tuple-element.14), channel_id=1, source_target_pairs={{0,2},{2,4},{4,6},{6,8},{8,10},{10,12},{12,14},{14,0},{1,3},{3,5},... | collective-permute-start | bytes 688136 | tf_op jit(solution)/shard_map/ppermute | solution.py:61
  35.7 6.2 %collective-permute-start.11 = (bf16[32,3584]{1,0:T(8,128)(2,1)S(1)}, bf16[32,3584]{1,0:T(8,128)(2,1)S(1)}, u32[]{:S(2)}, u32[]{:S(2)}) collective-permute-start(bf16[32,3584]{1,0:T(8,128)(2,1)S(1)} %get-tuple-element.15), channel_id=1, source_target_pairs={{0,14},{2,0},{4,2},{6,4},{8,6},{10,8},{12,10},{14,12},{1,15},{3,1}... | collective-permute-start | bytes 688136 | tf_op jit(solution)/shard_map/ppermute | solution.py:61
  38.5 8.6 %collective-permute-start.13 = (bf16[32,4608]{1,0:T(8,128)(2,1)S(1)}, bf16[32,4608]{1,0:T(8,128)(2,1)S(1)}, u32[]{:S(2)}, u32[]{:S(2)}) collective-permute-start(bf16[32,4608]{1,0:T(8,128)(2,1)S(1)} %get-tuple-element.16), channel_id=1, source_target_pairs={{0,64},{64,128},{128,192},{192,0},{1,65},{65,129},{129,193},{193,1... | collective-permute-start | bytes 884744 | tf_op jit(solution)/shard_map/ppermute | solution.py:61
  39.2 7.8 %collective-permute-start.14 = (bf16[32,4608]{1,0:T(8,128)(2,1)S(1)}, bf16[32,4608]{1,0:T(8,128)(2,1)S(1)}, u32[]{:S(2)}, u32[]{:S(2)}) collective-permute-start(bf16[32,4608]{1,0:T(8,128)(2,1)S(1)} %get-tuple-element.17), channel_id=1, source_target_pairs={{0,192},{64,0},{128,64},{192,128},{1,193},{65,1},{129,65},{193,129... | collective-permute-start | bytes 884744 | tf_op jit(solution)/shard_map/ppermute | solution.py:61
  41.8 7.5 %collective-permute-start.10 = (bf16[16,3584]{1,0:T(8,128)(2,1)S(1)}, bf16[16,3584]{1,0:T(8,128)(2,1)S(1)}, u32[]{:S(2)}, u32[]{:S(2)}) collective-permute-start(bf16[16,3584]{1,0:T(8,128)(2,1)S(1)} %slice.8), channel_id=1, source_target_pairs={{0,2},{2,4},{4,6},{6,8},{8,10},{10,12},{12,14},{14,0},{1,3},{3,5},... | collective-permute-start | bytes 344072 | tf_op jit(solution)/shard_map/ppermute | solution.py:61
  41.9 7.4 %collective-permute-start.12 = (bf16[16,3584]{1,0:T(8,128)(2,1)S(1)}, bf16[16,3584]{1,0:T(8,128)(2,1)S(1)}, u32[]{:S(2)}, u32[]{:S(2)}) collective-permute-start(bf16[16,3584]{1,0:T(8,128)(2,1)S(1)} %slice.9), channel_id=1, source_target_pairs={{0,14},{2,0},{4,2},{6,4},{8,6},{10,8},{12,10},{14,12},{1,15},{3,1}... | collective-permute-start | bytes 344072 | tf_op jit(solution)/shard_map/ppermute | solution.py:61
  62.5 19.5 %collective-permute-start.15 = (bf16[512,1024]{1,0:T(8,128)(2,1)S(1)}, bf16[512,1024]{1,0:T(8,128)(2,1)S(1)}, u32[]{:S(2)}, u32[]{:S(2)}) collective-permute-start(bf16[512,1024]{1,0:T(8,128)(2,1)S(1)} %shard_map.96.own_ref), channel_id=1, source_target_pairs={{0,1},{1,0},{2,3},{3,2},{4,5},{5,4},{6,7},{7,6},{8,9},{9,8},{10,11... | collective-permute-start | bytes 3145736 | tf_op jit(solution)/shard_map/ppermute | solution.py:57
  68.5 13.4 %collective-permute-start.16 = (bf16[1792,256]{1,0:T(8,128)(2,1)S(1)}, bf16[1792,256]{1,0:T(8,128)(2,1)S(1)}, u32[]{:S(2)}, u32[]{:S(2)}) collective-permute-start(bf16[1792,256]{1,0:T(8,128)(2,1)S(1)} %get-tuple-element.25), channel_id=1, source_target_pairs={{0,1},{1,0},{2,3},{3,2},{4,5},{5,4},{6,7},{7,6},{8,9},{9,8},{10,11... | collective-permute-start | bytes 2752520 | tf_op jit(solution)/shard_map/ppermute | solution.py:57

commit v7 on v6

--- a/solution.py
+++ b/solution.py
@@ -89,7 +89,9 @@
     low = high = plane
     for step in range(NZ // 2 - 1):
         if step == 2:
-            near = near_teacher((rows, t_low, t_high), teacher_head, other_teacher_head)
+            other_student_head = fetched(other_student_head, planes[1])
+            blocks = (rows, t_low, t_high)
+            near = near_teacher(blocks, teacher_head, other_teacher_head, other_student_head)
             waited = (near, other_student_head)
             low, high, t_low_half, t_high_half = gate(low, high, t_low, t_high, *waited)
         low, high = both_ways(low, high, "z", NZ)
@@ -97,7 +99,7 @@
     far = both_ways(t_low_half, t_high_half, "y", NY)
     half = plane.shape[0] // 2
     planes += both_ways(low[:half], high[half:], "z", NZ)
-    return planes, far, near
+    return planes, far, near, other_student_head
 
 
 def distance(position):
@@ -214,17 +216,17 @@
     return (30.0 * jnp.tanh(logits / 30.0)).astype(BF16)
 
 
-def near_teacher_kernel(b0, b1, b2, own_w_ref, other_w_ref, out_ref, rows_ref):
+def near_teacher_kernel(b0, b1, b2, own_w_ref, other_w_ref, _, out_ref, rows_ref):
     rows_ref[...] = jnp.concatenate([b0[...], b1[...], b2[...]])
     logits(rows_ref, own_w_ref, other_w_ref, out_ref)
 
 
-def near_teacher(blocks, own_head, other_head):
+def near_teacher(blocks, own_head, other_head, other):
     k, vocab = own_head.shape
     n = 3 * blocks[0].shape[0]
     scratch = [pltpu.VMEM((n, 2 * k), BF16)]
     out = struct((n, vocab), BF16)
-    return call(near_teacher_kernel, out, (*blocks, own_head, other_head), scratch, LONG)
+    return call(near_teacher_kernel, out, (*blocks, own_head, other_head, other), scratch, LONG)
 
 
 def local_targets(targets_ref, z, first, rows):
@@ -488,8 +490,7 @@
     waited = (teacher_rows, other_teacher_head, other_student_head, oth_targets)
     plane = plane_rows(got, student_gain, *waited)
     other_teacher_head = fetched(other_teacher_head, plane)
-    other_student_head = fetched(other_student_head, plane)
-    planes, far, near = rings(
+    planes, far, near, other_student_head = rings(
         plane, teacher_rows, teacher_head, other_teacher_head, other_student_head
     )
 

time: 87.4 us -> 87.4 us (level)
  no operation moved by 1% of the time
where the time goes in v7:
time: 87.4 us; the launch traced here: 87.1 us
  starting transfers between devices  34.4 us (39%)
  blocking collectives  24.8 us (28%)
  Pallas kernels  20.3 us (23%)
  waiting for transfers between devices  5.74 us (7%)
  between operations  1.05 us (1%)
    ppermute x6, starting transfers between devices, both_ways(): lax.ppermute(high, axis, up(n, -1))  15.5 us
    all_to_all x1, blocking collectives, shards(): sums = lax.all_to_all(sums, ('z', 'c'), 0, 0, tiled=True)  13.3 us
    all_to_all x1, blocking collectives, shards(): sums = jnp.sum(lax.all_to_all(sums, ('y', 'x'), 0, 0, tiled=True), axis=0)  11.5 us
    pallas_call x7, Pallas kernels, call(): pl.pallas_call(body, out_shape=out_shape, in_specs=[VMEM] * len(operands)...  9.9 us
    ppermute x5, starting transfers between devices, swap_cores(): return lax.ppermute(value, 'c', [(0, 1), (1, 0)])  9.55 us
    all_to_all x1, starting transfers between devices, shards(): got = lax.all_to_all(sent, ('y', 'x'), 0, 0, tiled=True)  5.02 us
    pallas_call x1, Pallas kernels, gradient(): pl.pallas_call(gradient_kernel, out_shape=(struct((1, ROWS), F32), struct...  4.93 us
    pallas_call x2, Pallas kernels, fetched(): pl.pallas_call(fetch_kernel, out_shape=struct(head.shape, head.dtype), in...  4.58 us
  transfers between devices with their start and end apart: 18, of which 4 were waited for; matrix products, arithmetic and copies ran while one was open for 0% of the time, Pallas kernels for 16%

profile of v7, /device:TPU:1, one launch (start us, length us, event | category | flops | bytes accessed | tf_op | source)
XLA Modules:
  0.0 87.1 jit_solution(4323010137877752585)
XLA Ops:
  0.6 3.3 %collective-permute-start = (bf16[2304,1024]{1,0:T(8,128)(2,1)}, bf16[2304,1024]{1,0:T(8,128)(2,1)}, u32[]{:S(2)}, u32[]{:S(2)}) collective-permute-start(bf16[2304,1024]{1,0:T(8,128)(2,1)} %own_w_ref.4), channel_id=1, source_target_pairs={{0,1},{1,0},{2,3},{3,2},{4,5},{5,4},{6,7},{7,6},{8,9},{9,8},{10,11... | collective-permute-start | bytes 14155784 | tf_op jit(solution)/shard_map/ppermute | solution.py:57
  4.0 0.1 collective-permute-start.1
  4.1 0.0 copy-start.5
  4.1 0.7 copy-done.5
  4.8 0.0 copy-start.2
  4.8 0.0 copy-start.3
  4.8 0.7 shard_map.86._
  5.5 5.0 %all-to-all-start = ((bf16[16,2,3584]{2,1,0:T(2,128)(2,1)}), bf16[16,2,3584]{2,1,0:T(2,128)(2,1)S(1)}, u32[]{:S(2)}, u32[]{:S(2)}) async-start(bf16[16,2,3584]{2,1,0:T(2,128)(2,1)} %shard_map.86._), calls=%async_computation | async-start | bytes 458752 | tf_op jit(solution)/shard_map/all_to_all | solution.py:488
  10.5 0.0 copy-done.1
  10.5 0.8 collective-permute-start.2
  11.3 0.0 copy-done.2
  11.3 0.0 copy-done.3
  11.3 0.5 shard_map.87.refs_2_.b0
  11.8 1.7 %collective-permute-start.7 = (bf16[64,4608]{1,0:T(8,128)(2,1)S(1)}, bf16[64,4608]{1,0:T(8,128)(2,1)S(1)}, u32[]{:S(2)}, u32[]{:S(2)}) collective-permute-start(bf16[64,4608]{1,0:T(8,128)(2,1)S(1)} %shard_map.87.refs_2_.b0), channel_id=1, source_target_pairs={{0,64},{64,128},{128,192},{192,0},{1,65},{65,129},{129,193},{193,1... | collective-permute-start | bytes 1769480 | tf_op jit(solution)/shard_map/ppermute | solution.py:61
  13.5 1.3 %collective-permute-start.8 = (bf16[64,4608]{1,0:T(8,128)(2,1)S(1)}, bf16[64,4608]{1,0:T(8,128)(2,1)S(1)}, u32[]{:S(2)}, u32[]{:S(2)}) collective-permute-start(bf16[64,4608]{1,0:T(8,128)(2,1)S(1)} %shard_map.87.refs_2_.b0), channel_id=1, source_target_pairs={{0,192},{64,0},{128,64},{192,128},{1,193},{65,1},{129,65},{193,129... | collective-permute-start | bytes 1769480 | tf_op jit(solution)/shard_map/ppermute | solution.py:61
  14.9 1.9 %collective-permute-done.2.refs_5_.oth_targets_ref = s32[1,256]{1,0:T(1,128)S(1)} collective-permute-done((s32[1,256]{1,0:T(1,128)S(1)}, s32[1,256]{1,0:T(1,128)S(1)}, u32[]{:S(2)}, u32[]{:S(2)}) %collective-permute-start.2) | collective-permute-done | bytes 1056 | tf_op jit(solution)/shard_map/ppermute | solution.py:57
  16.7 1.5 %all-to-all-done.refs_0_ = bf16[16,2,3584]{2,1,0:T(2,128)(2,1)S(1)} async-done(((bf16[16,2,3584]{2,1,0:T(2,128)(2,1)}), bf16[16,2,3584]{2,1,0:T(2,128)(2,1)S(1)}, u32[]{:S(2)}, u32[]{:S(2)}) %all-to-all-start) | async-done | bytes 229408 | tf_op jit(solution)/shard_map/all_to_all | solution.py:488
  18.2 0.0 collective-permute-done.1.refs_4_.head
  18.2 0.0 collective-permute-done.refs_3_.head
  18.2 0.0 copy-done.4
  18.2 0.3 shard_map.88._.refs_0_
  18.5 1.7 %collective-permute-start.3 = (bf16[32,3584]{1,0:T(8,128)(2,1)S(1)}, bf16[32,3584]{1,0:T(8,128)(2,1)S(1)}, u32[]{:S(2)}, u32[]{:S(2)}) collective-permute-start(bf16[32,3584]{1,0:T(8,128)(2,1)S(1)} %shard_map.88._.refs_0_), channel_id=1, source_target_pairs={{0,2},{2,4},{4,6},{6,8},{8,10},{10,12},{12,14},{14,0},{1,3},{3,5},... | collective-permute-start | bytes 688136 | tf_op jit(solution)/shard_map/ppermute | solution.py:61
  20.2 4.0 %collective-permute-start.5 = (bf16[32,3584]{1,0:T(8,128)(2,1)S(1)}, bf16[32,3584]{1,0:T(8,128)(2,1)S(1)}, u32[]{:S(2)}, u32[]{:S(2)}) collective-permute-start(bf16[32,3584]{1,0:T(8,128)(2,1)S(1)} %shard_map.88._.refs_0_), channel_id=1, source_target_pairs={{0,14},{2,0},{4,2},{6,4},{8,6},{10,8},{12,10},{14,12},{1,15},{3,1}... | collective-permute-start | bytes 688136 | tf_op jit(solution)/shard_map/ppermute | solution.py:61
  24.3 2.5 %shard_map.89.other_w_ref = bf16[2304,1024]{1,0:T(8,128)(2,1)S(1)} custom-call(bf16[2304,1024]{1,0:T(8,128)(2,1)} %collective-permute-done.refs_3_.head, bf16[32,3584]{1,0:T(8,128)(2,1)S(1)} %shard_map.88._.refs_0_), custom_call_target="tpu_custom_call" | custom-call | flops 5000000000 | bytes 1024 | tf_op jit(solution)/shard_map/pallas_call | solution.py:194
  26.8 0.0 slice-start.1
  26.8 1.7 %collective-permute-done.3._.refs_1_ = bf16[32,3584]{1,0:T(8,128)(2,1)S(1)} collective-permute-done((bf16[32,3584]{1,0:T(8,128)(2,1)S(1)}, bf16[32,3584]{1,0:T(8,128)(2,1)S(1)}, u32[]{:S(2)}, u32[]{:S(2)}) %collective-permute-start.3) | collective-permute-done | bytes 229408 | tf_op jit(solution)/shard_map/ppermute | solution.py:61
  28.5 0.0 collective-permute-start.4
  28.5 0.0 collective-permute-done.5.refs_2_
  28.5 2.7 %collective-permute-start.6 = (bf16[32,3584]{1,0:T(8,128)(2,1)S(1)}, bf16[32,3584]{1,0:T(8,128)(2,1)S(1)}, u32[]{:S(2)}, u32[]{:S(2)}) collective-permute-start(bf16[32,3584]{1,0:T(8,128)(2,1)S(1)} %collective-permute-done.5.refs_2_), channel_id=1, source_target_pairs={{0,14},{2,0},{4,2},{6,4},{8,6},{10,8},{12,10},{14,12},{1,15},{3,1}... | collective-permute-start | bytes 688136 | tf_op jit(solution)/shard_map/ppermute | solution.py:61
  31.2 2.1 %shard_map.90._.refs_1_.refs_8_.other_w_ref = bf16[1792,1024]{1,0:T(8,128)(2,1)S(1)} custom-call(bf16[1792,1024]{1,0:T(8,128)(2,1)} %collective-permute-done.1.refs_4_.head, bf16[32,3584]{1,0:T(8,128)(2,1)S(1)} %collective-permute-done.3._.refs_1_), custom_call_target="tpu_custom_call" | custom-call | flops 5000000000 | bytes 1024 | tf_op jit(solution)/shard_map/pallas_call | solution.py:194
  33.3 0.0 collective-permute-done.7.b1.t_low
  33.3 0.0 collective-permute-done.8.b2.t_high
  33.3 0.0 slice-done
  33.3 0.0 slice-done.1
  33.3 2.2 %shard_map.91.refs_0_.near_ref = bf16[192,1024]{1,0:T(8,128)(2,1)S(1)} custom-call(bf16[64,4608]{1,0:T(8,128)(2,1)S(1)} %shard_map.87.refs_2_.b0, bf16[64,4608]{1,0:T(8,128)(2,1)S(1)} %collective-permute-done.7.b1.t_low, bf16[64,4608]{1,0:T(8,128)(2,1)S(1)} %collective-permute-done.8.b2.t_high, bf16[2304,1024]{1,0:T(8,128)(2,1)S(1)} %bitcast.3, ...), custom_call_target="tpu_custom_call" | custom-call | flops 5000000000 | bytes 1024 | tf_op jit(solution)/shard_map/pallas_call | solution.py:36
  35.5 0.0 copy-start
  35.5 0.0 collective-permute-done.4.low.refs_3_
  35.5 0.0 collective-permute-done.6.high.refs_4_
  35.5 0.1 shard_map.92
  35.6 0.1 collective-permute-start.9
  35.7 2.8 %collective-permute-start.11 = (bf16[32,3584]{1,0:T(8,128)(2,1)S(1)}, bf16[32,3584]{1,0:T(8,128)(2,1)S(1)}, u32[]{:S(2)}, u32[]{:S(2)}) collective-permute-start(bf16[32,3584]{1,0:T(8,128)(2,1)S(1)} %get-tuple-element.15), channel_id=1, source_target_pairs={{0,14},{2,0},{4,2},{6,4},{8,6},{10,8},{12,10},{14,12},{1,15},{3,1}... | collective-permute-start | bytes 688136 | tf_op jit(solution)/shard_map/ppermute | solution.py:61
  38.5 0.7 collective-permute-start.13
  39.2 2.0 %collective-permute-start.14 = (bf16[32,4608]{1,0:T(8,128)(2,1)S(1)}, bf16[32,4608]{1,0:T(8,128)(2,1)S(1)}, u32[]{:S(2)}, u32[]{:S(2)}) collective-permute-start(bf16[32,4608]{1,0:T(8,128)(2,1)S(1)} %get-tuple-element.17), channel_id=1, source_target_pairs={{0,192},{64,0},{128,64},{192,128},{1,193},{65,1},{129,65},{193,129... | collective-permute-start | bytes 884744 | tf_op jit(solution)/shard_map/ppermute | solution.py:61
  41.2 0.6 collective-permute-done.9.refs_5_
  41.8 0.1 collective-permute-start.10
  41.9 0.0 collective-permute-done.11.refs_6_
  41.9 2.7 %collective-permute-start.12 = (bf16[16,3584]{1,0:T(8,128)(2,1)S(1)}, bf16[16,3584]{1,0:T(8,128)(2,1)S(1)}, u32[]{:S(2)}, u32[]{:S(2)}) collective-permute-start(bf16[16,3584]{1,0:T(8,128)(2,1)S(1)} %slice.9), channel_id=1, source_target_pairs={{0,14},{2,0},{4,2},{6,4},{8,6},{10,8},{12,10},{14,12},{1,15},{3,1}... | collective-permute-start | bytes 344072 | tf_op jit(solution)/shard_map/ppermute | solution.py:61
  44.7 0.0 copy-done
  44.7 2.3 %shard_map.93 = (bf16[224,1024]{1,0:T(8,128)(2,1)S(1)}, f32[8,128]{1,0:T(8,128)S(1)}) custom-call(bf16[32,3584]{1,0:T(8,128)(2,1)S(1)} %shard_map.88._.refs_0_, bf16[32,3584]{1,0:T(8,128)(2,1)S(1)} %collective-permute-done.3._.refs_1_, bf16[32,3584]{1,0:T(8,128)(2,1)S(1)} %collective-permute-done.5.refs_2_, ...), custom_call_target="tpu_custom_call" | custom-call | flops 5000000000 | bytes 1024 | tf_op jit(solution)/shard_map/pallas_call | solution.py:36
  47.0 0.0 collective-permute-done.13.b3
  47.0 0.0 collective-permute-done.14.b4
  47.0 2.3 %shard_map.94 = (bf16[256,1024]{1,0:T(8,128)(2,1)S(1)}, f32[8,128]{1,0:T(8,128)S(1)}) custom-call(bf16[32,4608]{1,0:T(8,128)(2,1)S(1)} %collective-permute-done.13.b3, bf16[32,4608]{1,0:T(8,128)(2,1)S(1)} %collective-permute-done.14.b4, bf16[192,1024]{1,0:T(8,128)(2,1)S(1)} %shard_map.91.refs_0_.near_ref, bf16[2304,1024]{1,0:T(8,128)(2,1)S(1)} %bitcast.3, ...), custom_call_target="tpu_custom_call" | custom-call | flops 5000000000 | bytes 1024 | tf_op jit(solution)/shard_map/pallas_call | solution.py:36
  49.3 0.0 collective-permute-done.10.low.refs_7_
  49.3 0.0 collective-permute-done.12.high.refs_8_
  49.3 1.5 %shard_map.95 = (bf16[32,1024]{1,0:T(8,128)(2,1)S(1)}, f32[16,8,128]{2,1,0:T(8,128)S(1)}) custom-call(bf16[16,3584]{1,0:T(8,128)(2,1)S(1)} %collective-permute-done.10.low.refs_7_, bf16[16,3584]{1,0:T(8,128)(2,1)S(1)} %collective-permute-done.12.high.refs_8_, bf16[1792,1024]{1,0:T(8,128)(2,1)S(1)} %copy-done, ...), custom_call_target="tpu_custom_call" | custom-call | flops 1024 | bytes 1024 | tf_op jit(solution)/shard_map/pallas_call | solution.py:36
  50.9 11.5 %all_to_all.15 = f32[16,8,128]{2,1,0:T(8,128)S(1)} all-to-all(f32[16,8,128]{2,1,0:T(8,128)S(1)} %get-tuple-element.22), channel_id=1, replica_groups=mesh['y'=4,'x'=4,'z'=8,'c'=2] {'y','x'}, dimensions={0} | all-to-all | bytes 131072 | tf_op jit(solution)/shard_map/all_to_all | solution.py:504
  62.4 0.1 shard_map.96.own_ref
  62.4 5.2 %collective-permute-start.15 = (bf16[512,1024]{1,0:T(8,128)(2,1)S(1)}, bf16[512,1024]{1,0:T(8,128)(2,1)S(1)}, u32[]{:S(2)}, u32[]{:S(2)}) collective-permute-start(bf16[512,1024]{1,0:T(8,128)(2,1)S(1)} %shard_map.96.own_ref), channel_id=1, source_target_pairs={{0,1},{1,0},{2,3},{3,2},{4,5},{5,4},{6,7},{7,6},{8,9},{9,8},{10,11... | collective-permute-start | bytes 3145736 | tf_op jit(solution)/shard_map/ppermute | solution.py:57
  67.7 0.8 shard_map.97
  68.5 0.1 collective-permute-start.16
  68.6 13.3 %all_to_all.16.sums_ref = f32[16,8,128]{2,1,0:T(8,128)S(1)} all-to-all(f32[16,8,128]{2,1,0:T(8,128)S(1)} %broadcast_in_dim.2._.refs_9_), channel_id=1, replica_groups=mesh['y'=4,'x'=4,'z'=8,'c'=2] {'z','c'}, dimensions={0} | all-to-all | bytes 131072 | tf_op jit(solution)/shard_map/all_to_all | solution.py:510
  82.0 0.0 collective-permute-done.16.other_rows
  82.0 0.0 collective-permute-done.15.other_ref
  82.0 4.9 %shard_map.98 = (f32[1,2]{1,0:T(1,128)}, bf16[1792,1024]{1,0:T(8,128)(2,1)}) custom-call(f32[16,8,128]{2,1,0:T(8,128)S(1)} %all_to_all.16.sums_ref, bf16[512,1024]{1,0:T(8,128)(2,1)S(1)} %shard_map.96.own_ref, bf16[512,1024]{1,0:T(8,128)(2,1)S(1)} %collective-permute-done.15.other_ref, s32[1,256]{1,0:T(1,128)S(1)} %copy-done.1, ...), custom_call_target="tpu_custom_call" | custom-call | flops 1024 | bytes 1024 | tf_op jit(solution)/shard_map/pallas_call | solution.py:463
  (8 shorter events, 0.1 us)
Async XLA Ops:
  0.6 17.6 %collective-permute-start = (bf16[2304,1024]{1,0:T(8,128)(2,1)}, bf16[2304,1024]{1,0:T(8,128)(2,1)}, u32[]{:S(2)}, u32[]{:S(2)}) collective-permute-start(bf16[2304,1024]{1,0:T(8,128)(2,1)} %own_w_ref.4), channel_id=1, source_target_pairs={{0,1},{1,0},{2,3},{3,2},{4,5},{5,4},{6,7},{7,6},{8,9},{9,8},{10,11... | collective-permute-start | bytes 14155784 | tf_op jit(solution)/shard_map/ppermute | solution.py:57
  4.0 14.3 %collective-permute-start.1 = (bf16[1792,1024]{1,0:T(8,128)(2,1)}, bf16[1792,1024]{1,0:T(8,128)(2,1)}, u32[]{:S(2)}, u32[]{:S(2)}) collective-permute-start(bf16[1792,1024]{1,0:T(8,128)(2,1)} %own_w_ref.5), channel_id=1, source_target_pairs={{0,1},{1,0},{2,3},{3,2},{4,5},{5,4},{6,7},{7,6},{8,9},{9,8},{10,11... | collective-permute-start | bytes 11010056 | tf_op jit(solution)/shard_map/ppermute | solution.py:57
  4.1 0.7 copy-start.5
  4.8 5.7 %copy-start.1 = (s32[1,256]{1,0:T(1,128)S(1)}, s32[1,256]{1,0:T(1,128)}, u32[]{:S(2)}) copy-start(s32[1,256]{1,0:T(1,128)} %targets_ref.3) | copy-start | bytes 3076
  4.8 6.5 %copy-start.2 = (bf16[1,64,4608]{2,1,0:T(8,128)(2,1)S(1)}, bf16[1,64,4608]{2,1,0:T(8,128)(2,1)}, u32[]{:S(2)}) copy-start(bf16[1,64,4608]{2,1,0:T(8,128)(2,1)} %param.8) | copy-start | bytes 1769476
  4.8 6.5 %copy-start.3 = (f32[4608]{0:T(1024)S(1)}, f32[4608]{0:T(1024)}, u32[]{:S(2)}) copy-start(f32[4608]{0:T(1024)} %gain_ref.1) | copy-start | bytes 55300
  5.5 12.7 %all-to-all-start = ((bf16[16,2,3584]{2,1,0:T(2,128)(2,1)}), bf16[16,2,3584]{2,1,0:T(2,128)(2,1)S(1)}, u32[]{:S(2)}, u32[]{:S(2)}) async-start(bf16[16,2,3584]{2,1,0:T(2,128)(2,1)} %shard_map.86._), calls=%async_computation | async-start | bytes 458752 | tf_op jit(solution)/shard_map/all_to_all | solution.py:488
  10.5 6.2 %collective-permute-start.2 = (s32[1,256]{1,0:T(1,128)S(1)}, s32[1,256]{1,0:T(1,128)S(1)}, u32[]{:S(2)}, u32[]{:S(2)}) collective-permute-start(s32[1,256]{1,0:T(1,128)S(1)} %copy-done.1), channel_id=1, source_target_pairs={{0,1},{1,0},{2,3},{3,2},{4,5},{5,4},{6,7},{7,6},{8,9},{9,8},{10,11... | collective-permute-start | bytes 3080 | tf_op jit(solution)/shard_map/ppermute | solution.py:57
  11.3 6.9 %copy-start.4 = (f32[3584]{0:T(1024)S(1)}, f32[3584]{0:T(1024)}, u32[]{:S(2)}) copy-start(f32[3584]{0:T(1024)} %refs_1_.1) | copy-start | bytes 43012
  11.8 21.4 %collective-permute-start.7 = (bf16[64,4608]{1,0:T(8,128)(2,1)S(1)}, bf16[64,4608]{1,0:T(8,128)(2,1)S(1)}, u32[]{:S(2)}, u32[]{:S(2)}) collective-permute-start(bf16[64,4608]{1,0:T(8,128)(2,1)S(1)} %shard_map.87.refs_2_.b0), channel_id=1, source_target_pairs={{0,64},{64,128},{128,192},{192,0},{1,65},{65,129},{129,193},{193,1... | collective-permute-start | bytes 1769480 | tf_op jit(solution)/shard_map/ppermute | solution.py:61
  13.5 19.7 %collective-permute-start.8 = (bf16[64,4608]{1,0:T(8,128)(2,1)S(1)}, bf16[64,4608]{1,0:T(8,128)(2,1)S(1)}, u32[]{:S(2)}, u32[]{:S(2)}) collective-permute-start(bf16[64,4608]{1,0:T(8,128)(2,1)S(1)} %shard_map.87.refs_2_.b0), channel_id=1, source_target_pairs={{0,192},{64,0},{128,64},{192,128},{1,193},{65,1},{129,65},{193,129... | collective-permute-start | bytes 1769480 | tf_op jit(solution)/shard_map/ppermute | solution.py:61
  18.5 10.0 %collective-permute-start.3 = (bf16[32,3584]{1,0:T(8,128)(2,1)S(1)}, bf16[32,3584]{1,0:T(8,128)(2,1)S(1)}, u32[]{:S(2)}, u32[]{:S(2)}) collective-permute-start(bf16[32,3584]{1,0:T(8,128)(2,1)S(1)} %shard_map.88._.refs_0_), channel_id=1, source_target_pairs={{0,2},{2,4},{4,6},{6,8},{8,10},{10,12},{12,14},{14,0},{1,3},{3,5},... | collective-permute-start | bytes 688136 | tf_op jit(solution)/shard_map/ppermute | solution.py:61
  20.2 8.3 %collective-permute-start.5 = (bf16[32,3584]{1,0:T(8,128)(2,1)S(1)}, bf16[32,3584]{1,0:T(8,128)(2,1)S(1)}, u32[]{:S(2)}, u32[]{:S(2)}) collective-permute-start(bf16[32,3584]{1,0:T(8,128)(2,1)S(1)} %shard_map.88._.refs_0_), channel_id=1, source_target_pairs={{0,14},{2,0},{4,2},{6,4},{8,6},{10,8},{12,10},{14,12},{1,15},{3,1}... | collective-permute-start | bytes 688136 | tf_op jit(solution)/shard_map/ppermute | solution.py:61
  24.3 9.0 %slice-start = ((s8[4718592]{0:T(1024)(128)(4,1)}), s8[4194304]{0:T(1024)(128)(4,1)S(1)}, s32[]{:S(2)}) async-start(s8[4718592]{0:T(1024)(128)(4,1)} %bitcast.2), calls=%async_computation.3 | async-start | bytes 8388608
  26.8 6.5 %slice-start.1 = ((s8[4718592]{0:T(1024)(128)(4,1)}), s8[524288]{0:T(1024)(128)(4,1)S(1)}, s32[]{:S(2)}) async-start(s8[4718592]{0:T(1024)(128)(4,1)} %bitcast.2), calls=%async_computation.4 | async-start | bytes 1048576
  28.5 7.0 %collective-permute-start.4 = (bf16[32,3584]{1,0:T(8,128)(2,1)S(1)}, bf16[32,3584]{1,0:T(8,128)(2,1)S(1)}, u32[]{:S(2)}, u32[]{:S(2)}) collective-permute-start(bf16[32,3584]{1,0:T(8,128)(2,1)S(1)} %collective-permute-done.3._.refs_1_), channel_id=1, source_target_pairs={{0,2},{2,4},{4,6},{6,8},{8,10},{10,12},{12,14},{14,0},{1,3},{3,5},... | collective-permute-start | bytes 688136 | tf_op jit(solution)/shard_map/ppermute | solution.py:61
  28.5 7.0 %collective-permute-start.6 = (bf16[32,3584]{1,0:T(8,128)(2,1)S(1)}, bf16[32,3584]{1,0:T(8,128)(2,1)S(1)}, u32[]{:S(2)}, u32[]{:S(2)}) collective-permute-start(bf16[32,3584]{1,0:T(8,128)(2,1)S(1)} %collective-permute-done.5.refs_2_), channel_id=1, source_target_pairs={{0,14},{2,0},{4,2},{6,4},{8,6},{10,8},{12,10},{14,12},{1,15},{3,1}... | collective-permute-start | bytes 688136 | tf_op jit(solution)/shard_map/ppermute | solution.py:61
  35.5 9.2 %copy-start = (bf16[1792,1024]{1,0:T(8,128)(2,1)S(1)}, bf16[1792,1024]{1,0:T(8,128)(2,1)}, u32[]{:S(2)}) copy-start(bf16[1792,1024]{1,0:T(8,128)(2,1)} %own_w_ref.5) | copy-start | bytes 11010052
  35.6 6.2 %collective-permute-start.9 = (bf16[32,3584]{1,0:T(8,128)(2,1)S(1)}, bf16[32,3584]{1,0:T(8,128)(2,1)S(1)}, u32[]{:S(2)}, u32[]{:S(2)}) collective-permute-start(bf16[32,3584]{1,0:T(8,128)(2,1)S(1)} %get-tuple-element.14), channel_id=1, source_target_pairs={{0,2},{2,4},{4,6},{6,8},{8,10},{10,12},{12,14},{14,0},{1,3},{3,5},... | collective-permute-start | bytes 688136 | tf_op jit(solution)/shard_map/ppermute | solution.py:61
  35.7 6.2 %collective-permute-start.11 = (bf16[32,3584]{1,0:T(8,128)(2,1)S(1)}, bf16[32,3584]{1,0:T(8,128)(2,1)S(1)}, u32[]{:S(2)}, u32[]{:S(2)}) collective-permute-start(bf16[32,3584]{1,0:T(8,128)(2,1)S(1)} %get-tuple-element.15), channel_id=1, source_target_pairs={{0,14},{2,0},{4,2},{6,4},{8,6},{10,8},{12,10},{14,12},{1,15},{3,1}... | collective-permute-start | bytes 688136 | tf_op jit(solution)/shard_map/ppermute | solution.py:61
  38.5 8.5 %collective-permute-start.13 = (bf16[32,4608]{1,0:T(8,128)(2,1)S(1)}, bf16[32,4608]{1,0:T(8,128)(2,1)S(1)}, u32[]{:S(2)}, u32[]{:S(2)}) collective-permute-start(bf16[32,4608]{1,0:T(8,128)(2,1)S(1)} %get-tuple-element.16), channel_id=1, source_target_pairs={{0,64},{64,128},{128,192},{192,0},{1,65},{65,129},{129,193},{193,1... | collective-permute-start | bytes 884744 | tf_op jit(solution)/shard_map/ppermute | solution.py:61
  39.2 7.8 %collective-permute-start.14 = (bf16[32,4608]{1,0:T(8,128)(2,1)S(1)}, bf16[32,4608]{1,0:T(8,128)(2,1)S(1)}, u32[]{:S(2)}, u32[]{:S(2)}) collective-permute-start(bf16[32,4608]{1,0:T(8,128)(2,1)S(1)} %get-tuple-element.17), channel_id=1, source_target_pairs={{0,192},{64,0},{128,64},{192,128},{1,193},{65,1},{129,65},{193,129... | collective-permute-start | bytes 884744 | tf_op jit(solution)/shard_map/ppermute | solution.py:61
  41.8 7.5 %collective-permute-start.10 = (bf16[16,3584]{1,0:T(8,128)(2,1)S(1)}, bf16[16,3584]{1,0:T(8,128)(2,1)S(1)}, u32[]{:S(2)}, u32[]{:S(2)}) collective-permute-start(bf16[16,3584]{1,0:T(8,128)(2,1)S(1)} %slice.8), channel_id=1, source_target_pairs={{0,2},{2,4},{4,6},{6,8},{8,10},{10,12},{12,14},{14,0},{1,3},{3,5},... | collective-permute-start | bytes 344072 | tf_op jit(solution)/shard_map/ppermute | solution.py:61
  41.9 7.4 %collective-permute-start.12 = (bf16[16,3584]{1,0:T(8,128)(2,1)S(1)}, bf16[16,3584]{1,0:T(8,128)(2,1)S(1)}, u32[]{:S(2)}, u32[]{:S(2)}) collective-permute-start(bf16[16,3584]{1,0:T(8,128)(2,1)S(1)} %slice.9), channel_id=1, source_target_pairs={{0,14},{2,0},{4,2},{6,4},{8,6},{10,8},{12,10},{14,12},{1,15},{3,1}... | collective-permute-start | bytes 344072 | tf_op jit(solution)/shard_map/ppermute | solution.py:61
  62.4 19.5 %collective-permute-start.15 = (bf16[512,1024]{1,0:T(8,128)(2,1)S(1)}, bf16[512,1024]{1,0:T(8,128)(2,1)S(1)}, u32[]{:S(2)}, u32[]{:S(2)}) collective-permute-start(bf16[512,1024]{1,0:T(8,128)(2,1)S(1)} %shard_map.96.own_ref), channel_id=1, source_target_pairs={{0,1},{1,0},{2,3},{3,2},{4,5},{5,4},{6,7},{7,6},{8,9},{9,8},{10,11... | collective-permute-start | bytes 3145736 | tf_op jit(solution)/shard_map/ppermute | solution.py:57
  68.5 13.5 %collective-permute-start.16 = (bf16[1792,256]{1,0:T(8,128)(2,1)S(1)}, bf16[1792,256]{1,0:T(8,128)(2,1)S(1)}, u32[]{:S(2)}, u32[]{:S(2)}) collective-permute-start(bf16[1792,256]{1,0:T(8,128)(2,1)S(1)} %get-tuple-element.25), channel_id=1, source_target_pairs={{0,1},{1,0},{2,3},{3,2},{4,5},{5,4},{6,7},{7,6},{8,9},{9,8},{10,11... | collective-permute-start | bytes 2752520 | tf_op jit(solution)/shard_map/ppermute | solution.py:57
